TPU v7x, 128 devices: a whole 4x4x4 slice. The times are simulated.
128 devices in a mesh: rep: 8 (over z, y_lo), sp: 16 (over y_hi, x, core).
Axes of the slice: x: 4, y: 4 (y_hi: 2, y_lo: 2; y = y_hi * 2 + y_lo), z: 4, core: 2. Of those that a mesh axis runs over, the one named last changes fastest.
Arguments:
- features: bfloat16 [8, 48, 72, 2048], P('rep', 'sp'), may hold values from -6 to 6
- atrous_weight: bfloat16 [27, 2048, 256], P(None, None, 'sp'), may hold values from -0.046875 to 0.046875
- point_weight: bfloat16 [2048, 256], P(None, 'sp'), may hold values from -0.125 to 0.125
- proj_weight: bfloat16 [1024, 256], replicated, may hold values from -0.1875 to 0.1875
- cotangent: bfloat16 [8, 48, 72, 256], P('rep', 'sp'), may hold values from -6 to 6
Outputs:
- projected: bfloat16 [8, 48, 72, 256], P('rep', 'sp')
- input_grad: bfloat16 [8, 48, 72, 2048], P('rep', 'sp')
- grad_point: float32 [2048, 256], P('sp')
- grad_atrous: float32 [27, 2048, 256], P(None, 'sp')
- grad_proj: float32 [1024, 256], replicated
All inputs are finite; a program needn't handle non-finite values.
Results may differ from a plain program's by a relative error of at most 0.02.
Values may be sent and summed in bfloat16 or wider, within the bound.
No kernel may reach another device: no remote copies, remote signals or barrier semaphores. Data moves between devices by JAX's collectives and lax.ppermute only.
A program may use at most 192 MiB of HBM per device.

v0:
```python
import jax
import jax.numpy as jnp
from jax import lax
from jax.sharding import PartitionSpec as P

FIRST_DILATION = 6
SECOND_DILATION = 12
THIRD_DILATION = 18


def moved(field, off_row, off_col):
    ar = abs(off_row)
    ac = abs(off_col)
    padded = jnp.pad(field, ((0, 0), (ar, ar), (ac, ac), (0, 0)))
    return padded[
        :,
        ar + off_row : ar + off_row + field.shape[1],
        ac + off_col : ac + off_col + field.shape[2],
    ]


def shift_cols(field, off_col):
    ac = abs(off_col)
    padded = jnp.pad(field, ((0, 0), (0, 0), (ac, ac), (0, 0)))
    return padded[:, :, ac + off_col : ac + off_col + field.shape[2]]


def slope_of(value):
    sig = jax.nn.sigmoid(value)
    return sig + value * sig * (1.0 - sig)


def tap_list():
    kernel_taps = [(0, 0, 0)]
    for group_members, dilation_rate in enumerate(
        (FIRST_DILATION, SECOND_DILATION, THIRD_DILATION)
    ):
        for kernel_row in (-1, 0, 1):
            for kernel_column in (-1, 0, 1):
                kernel_taps.append(
                    (group_members + 1, kernel_row * dilation_rate, kernel_column * dilation_rate)
                )
    return kernel_taps


def contract_cells(left, right):
    return lax.dot_general(
        left, right, (((0, 1, 2), (0, 1, 2)), ((), ())), preferred_element_type=jnp.float32
    )


def shards(features, atrous_weight, point_weight, proj_weight, cotangent):
    batch_images, rows, image_width, chans = features.shape
    output_portion = point_weight.shape[1]
    fwide = proj_weight.shape[0] // 4
    complete_rows = rows * lax.axis_size("sp")
    batch_total = batch_images * lax.axis_size("rep")
    kernel_taps = tap_list()
    every_w = jnp.concatenate([point_weight[None], atrous_weight], 0)
    input_channels = lax.all_to_all(features, "sp", split_axis=3, concat_axis=1, tiled=True)
    w_in = lax.all_to_all(every_w, "sp", split_axis=1, concat_axis=2, tiled=True)
    input_padded = jnp.pad(
        input_channels,
        ((0, 0), (THIRD_DILATION, THIRD_DILATION), (THIRD_DILATION, THIRD_DILATION), (0, 0)),
    )
    w_flat = jnp.transpose(every_w, (1, 0, 2)).reshape(chans, 28 * output_portion)
    empty_buffer = jnp.zeros(
        (batch_images, complete_rows + 2 * THIRD_DILATION, image_width, output_portion), jnp.float32
    )
    carry = (empty_buffer, empty_buffer, empty_buffer, empty_buffer)
    piece = lax.all_gather(features, "sp", axis=1, tiled=True)
    start_position = jnp.int32(0)
    prod = jnp.dot(piece, w_flat, preferred_element_type=jnp.float32)
    count = piece.shape[1]
    carry = list(carry)
    groups = {}
    for add_t, (add_g, add_output_row, add_output_column) in enumerate(kernel_taps):
        part = shift_cols(
            prod[..., add_t * output_portion : (add_t + 1) * output_portion], add_output_column
        )
        key_pair = (add_g, add_output_row)
        groups[key_pair] = part if key_pair not in groups else groups[key_pair] + part
    for (add_g, add_output_row), contrib in groups.items():
        begin_offset = start_position + THIRD_DILATION - add_output_row
        block = lax.dynamic_slice_in_dim(carry[add_g], begin_offset, count, 1)
        carry[add_g] = lax.dynamic_update_slice_in_dim(
            carry[add_g], block + contrib, begin_offset, 1
        )
    running_totals = tuple(carry)
    local_preactivation = jnp.stack(
        [
            channel_index[:, THIRD_DILATION : THIRD_DILATION + complete_rows]
            for channel_index in running_totals
        ],
        3,
    )
    own_pre = local_preactivation.astype(jnp.bfloat16)
    regrouped = lax.all_to_all(own_pre, "sp", split_axis=1, concat_axis=4, tiled=True)
    pre_low = regrouped.reshape(batch_images, rows, image_width, 4 * fwide)
    pre_wide = pre_low.astype(jnp.float32)
    acts = jax.nn.silu(pre_wide).astype(jnp.bfloat16)
    out_pre = jnp.dot(acts, proj_weight, preferred_element_type=jnp.float32)
    projected = jax.nn.silu(out_pre).astype(jnp.bfloat16)
    dout = (cotangent.astype(jnp.float32) * slope_of(out_pre)).astype(jnp.bfloat16)
    proj_part = contract_cells(acts, dout)
    proj_sum = lax.psum(proj_part, ("rep", "sp"))
    dacts = jnp.dot(dout, proj_weight.T, preferred_element_type=jnp.float32)
    dacts = (dacts * slope_of(pre_wide)).astype(jnp.bfloat16)
    cot_full = lax.all_gather(dacts, "sp", axis=1, tiled=True)
    dpre = [cot_full[..., j * fwide : (j + 1) * fwide] for j in range(4)]
    point_part = contract_cells(input_channels, dpre[0])
    atrous_parts = []
    for group_members in range(1, 4):
        slabs = [
            input_padded[
                :,
                THIRD_DILATION + output_row : THIRD_DILATION + output_row + complete_rows,
                THIRD_DILATION + output_column : THIRD_DILATION + output_column + image_width,
            ]
            for g, output_row, output_column in kernel_taps
            if g == group_members
        ]
        stacked = jnp.concatenate(slabs, 3)
        atrous_parts.append(
            contract_cells(stacked, dpre[group_members]).reshape(9, input_channels.shape[3], fwide)
        )
    atrous_part = jnp.concatenate(atrous_parts, 0)
    back = jnp.dot(dpre[0], w_in[0].T, preferred_element_type=jnp.float32)
    for t, (g, output_row, output_column) in enumerate(kernel_taps):
        if t > 0:
            back = back + moved(
                jnp.dot(dpre[g], w_in[t].T, preferred_element_type=jnp.float32),
                -output_row,
                -output_column,
            )
    input_grad = lax.all_to_all(
        back.astype(jnp.bfloat16), "sp", split_axis=1, concat_axis=3, tiled=True
    )
    point_sum, atrous_sum = (
        lax.psum(point_part.astype(jnp.bfloat16), "rep").astype(jnp.float32),
        lax.psum(atrous_part.astype(jnp.bfloat16), "rep").astype(jnp.float32),
    )
    return (
        projected,
        input_grad,
        point_sum / batch_total,
        atrous_sum / batch_total,
        proj_sum / batch_total,
    )


def solution(mesh):
    in_specs = (
        P("rep", "sp", None, None),
        P(None, None, "sp"),
        P(None, "sp"),
        P(),
        P("rep", "sp", None, None),
    )
    out_specs = (
        P("rep", "sp", None, None),
        P("rep", "sp", None, None),
        P("sp", None),
        P(None, "sp", None),
        P(),
    )
    return jax.shard_map(shards, mesh=mesh, in_specs=in_specs, out_specs=out_specs, check_vma=False)
```

profile of v0, /device:TPU:1, one launch (start us, length us, event | category | flops | bytes accessed | tf_op | source)
XLA Modules:
  0.0 576.5 jit_solution(17222861409762133090)
XLA Ops:
  9.6 102.6 %all-gather.4.cloned.1.call-done = bf16[1,48,72,2048]{3,2,0,1:T(8,128)(2,1)} async-done(((bf16[1,3,72,2048]{3,2,0,1:T(8,128)(2,1)}), bf16[1,48,72,2048]{3,2,0,1:T(8,128)(2,1)}) %all-gather.4.cloned.1.call-update) | async-done | bytes 14155792 | tf_op jit(solution)/shard_map/all_gather | solution.py:71
  112.2 10.3 %fusion.11 = f32[1,48,72,448]{3,2,1,0:T(8,128)S(1)} fusion(bf16[2048,448,1]{0,1,2:T(8,128)(2,1)S(1)} %bitcast.541, bf16[1,48,72,2048]{3,2,0,1:T(8,128)(2,1)} %all-gather.4.cloned.1.call-done), kind=kOutput, calls=%fused_computation.47 | convolution fusion | flops 6341787648 | bytes 22183936 | tf_op jit(solution)/shard_map/dot_general | solution.py:73
  122.6 6.2 %fusion.319 = (f32[1,48,72,16]{3,2,1,0:T(8,128)}, f32[1,48,72,16]{3,2,1,0:T(8,128)}, f32[1,48,72,16]{3,2,1,0:T(8,128)}, f32[1,48,72,16]{3,2,1,0:T(8,128)}, f32[1...) fusion(f32[1,48,72,448]{3,2,1,0:T(8,128)S(1)} %fusion.11), kind=kLoop, calls=%fused_computation.326 | loop fusion | bytes 2654208 | tf_op jit(solution)/shard_map/slice | solution.py:79
  134.6 16.7 %fusion.23 = (f32[1,84,72,16]{3,2,1,0:T(8,128)S(1)}, f32[1,48,72,16]{3,2,1,0:T(8,128)}, f32[1,48,72,16]{3,2,1,0:T(8,128)}, f32[1,48,72,16]{3,2,1,0:T(8,128)}, f3...) fusion(f32[1,84,72,16]{3,2,1,0:T(8,128)S(1)} %fusion.19, ...), kind=kLoop, calls=%fused_computation.90 | loop fusion | flops 165888 | bytes 9510912 | tf_op jit(solution)/shard_map/dynamic_update_slice | solution.py:86
  151.3 5.2 fusion.51
  160.8 5.0 fusion.55
  165.8 3.5 fusion.59
  176.2 17.0 %all_to_all.60 = bf16[1,48,72,4,16]{2,4,3,0,1:T(8,128)(2,1)S(1)} all-to-all(bf16[1,48,72,4,16]{2,4,3,0,1:T(8,128)(2,1)S(1)} %copy.353), channel_id=1, replica_groups=mesh['rep'=8,'sp'=16] {'sp'}, dimensions={1} | all-to-all | bytes 884736 | tf_op jit(solution)/shard_map/all_to_all | solution.py:98
  199.8 3.7 reshape.329
  203.5 4.2 all-to-all-start.3
  207.7 10.7 %copy.357 = bf16[28,2048,16]{0,2,1:T(8,128)(2,1)} copy(bf16[28,2048,16]{1,2,0:T(8,128)(2,1)} %copy-done.5) | data formatting | bytes 3670016 | tf_op jit(solution)/shard_map/concatenate | solution.py:59
  218.4 19.3 %reshape.327 = bf16[16,2,28672]{2,1,0:T(2,128)(2,1)} reshape(bf16[2048,16,28]{2,1,0:T(8,128)(2,1)} %bitcast.537) | data formatting | bytes 3670016
  237.7 7.3 %all-to-all-start.1 = ((bf16[16,2,28672]{2,1,0:T(2,128)(2,1)}), bf16[16,2,28672]{2,1,0:T(2,128)(2,1)}, u32[]{:S(2)}, u32[]{:S(2)}) async-start(bf16[16,2,28672]{2,1,0:T(2,128)(2,1)} %reshape.327), calls=%async_computation.1 | async-start | bytes 3670016 | tf_op jit(solution)/shard_map/all_to_all | solution.py:61
  245.0 3.7 reshape.330
  267.6 6.7 %all-to-all-done.1 = bf16[16,2,28672]{2,1,0:T(2,128)(2,1)} async-done(((bf16[16,2,28672]{2,1,0:T(2,128)(2,1)}), bf16[16,2,28672]{2,1,0:T(2,128)(2,1)}, u32[]{:S(2)}, u32[]{:S(2)}) %all-to-all-start.1) | async-done | bytes 1835040 | tf_op jit(solution)/shard_map/all_to_all | solution.py:61
  274.3 24.5 %reshape.328 = bf16[2048,16,28]{2,1,0:T(8,128)(2,1)} reshape(bf16[16,2,28672]{2,1,0:T(2,128)(2,1)} %all-to-all-done.1) | data formatting | bytes 3670016
  298.8 9.2 %copy.456 = bf16[28,16,128,16]{2,1,3,0:T(8,128)(2,1)S(1)} copy(bf16[28,16,128,16]{0,3,2,1:T(8,128)(2,1)} %bitcast.538) | data formatting | bytes 3670016 | tf_op jit(solution)/shard_map/all_to_all | solution.py:61
  322.8 3.6 fusion.201
  371.5 5.8 %fusion.224 = bf16[9,128,256]{2,1,0:T(8,128)(2,1)S(1)} fusion(bf16[1,48,72,1024]{3,2,1,0:T(8,128)(2,1)S(1)} %bitcast.534, bf16[1,48,72,1152]{3,2,1,0:T(8,128)(2,1)} %fusion.273), kind=kOutput, calls=%fused_computation.239 | convolution fusion | flops 2038726656 | bytes 10321920 | tf_op jit(solution)/shard_map/dot_general | solution.py:47
  390.3 15.6 %fusion.239 = bf16[1,48,72,128]{3,2,0,1:T(8,128)(2,1)} fusion(f32[1,48,72,128]{3,2,1,0:T(8,128)S(1)} %fusion.204, f32[1,48,72,128]{3,2,1,0:T(8,128)} %fusion.201, f32[1,48,72,128]{3,2,1,0:T(8,128)} %fusion.198, f32[1,48,72,128]{3,2,1,0:T(8,128)} %fusion.195, f32[48,72,128]{2,1,0:T(8,128)} %fusion.82, f32[1,48,72,128]{3,2,1,0:T(8,128)} %fusion.192, ...), kind=kOutput, calls=%fused_computation.242 | convolution fusion | flops 238878720 | bytes 50495488 | tf_op jit(solution)/shard_map/dot_general | solution.py:132
  405.9 4.5 all-to-all-start.2
  411.1 55.8 %all-reduce.50.cloned.1.call-done = f32[1024,256]{1,0:T(8,128)} async-done(((f32[1024,256]{1,0:T(8,128)}), f32[1024,256]{1,0:T(8,128)}) %all-reduce.50.cloned.1.call-update) | async-done | bytes 1048592 | tf_op jit(solution)/shard_map/psum | solution.py:106
  470.3 94.0 %all-reduce.52.cloned.1.call-done = (bf16[128,256]{0,1:T(8,128)(2,1)}, bf16[27,128,256]{2,1,0:T(8,128)(2,1)}) async-done(((bf16[128,256]{0,1:T(8,128)(2,1)}, bf16[27,128,256]{2,1,0:T(8,128)(2,1)}), (bf16[128,256]{0,1:T(8,128)(2,1)}, bf16[27,128,256]{2,1,0:T(8,128)(2,1)})) %all-reduce.52.cloned.1.call-update) | async-done | bytes 1835024 | tf_op jit(solution)/shard_map/psum | solution.py:140
  565.9 3.7 convert_multiply_fusion
  (200 shorter events, 122.6 us)
Async XLA Ops:
  7.2 187.5 %copy-start = (bf16[1024,256]{1,0:T(8,128)(2,1)S(1)}, bf16[1024,256]{1,0:T(8,128)(2,1)}, u32[]{:S(2)}) copy-start(bf16[1024,256]{1,0:T(8,128)(2,1)} %param.8) | copy-start | bytes 1572868
  7.2 105.1 %all-gather.4.cloned.1.call-start = ((), (), s32[]{:S(2)}) async-start(), calls=%async_computation.4 | async-start | bytes 15040512 | tf_op jit(solution)/shard_map/all_gather | solution.py:71
  7.9 312.6 %all-gather.6.cloned.1.call-start = ((), (), s32[]{:S(2)}) async-start(), calls=%async_computation.6 | async-start | bytes 7520256 | tf_op jit(solution)/shard_map/all_gather | solution.py:109
  9.6 113.0 %copy-start.5 = (bf16[28,2048,16]{1,2,0:T(8,128)(2,1)}, bf16[28,2048,16]{1,2,0:T(8,128)(2,1)S(1)}, u32[]{:S(2)}) copy-start(bf16[28,2048,16]{1,2,0:T(8,128)(2,1)S(1)} %pad_maximum_fusion.1) | copy-start | bytes 5505028
  122.6 8.8 %copy-start.3 = (f32[1,48,72,448]{3,2,1,0:T(8,128)}, f32[1,48,72,448]{3,2,1,0:T(8,128)S(1)}, u32[]{:S(2)}) copy-start(f32[1,48,72,448]{3,2,1,0:T(8,128)S(1)} %fusion.11) | copy-start | bytes 18579460
  160.8 5.0 copy-start.6
  160.8 5.0 copy-start.7
  160.8 5.0 copy-start.8
  203.5 34.2 %all-to-all-start.3 = ((bf16[16,2,13824]{2,1,0:T(2,128)(2,1)}), bf16[16,2,13824]{2,1,0:T(2,128)(2,1)S(1)}, u32[]{:S(2)}, u32[]{:S(2)}) async-start(bf16[16,2,13824]{2,1,0:T(2,128)(2,1)} %reshape.329), calls=%async_computation.3 | async-start | bytes 1769472 | tf_op jit(solution)/shard_map/all_to_all | solution.py:60
  237.7 36.6 %all-to-all-start.1 = ((bf16[16,2,28672]{2,1,0:T(2,128)(2,1)}), bf16[16,2,28672]{2,1,0:T(2,128)(2,1)}, u32[]{:S(2)}, u32[]{:S(2)}) async-start(bf16[16,2,28672]{2,1,0:T(2,128)(2,1)} %reshape.327), calls=%async_computation.1 | async-start | bytes 3670016 | tf_op jit(solution)/shard_map/all_to_all | solution.py:61
  245.0 221.9 %all-reduce.50.cloned.1.call-start = ((), (), s32[]{:S(2)}) async-start(), calls=%async_computation.5 | async-start | bytes 2097152 | tf_op jit(solution)/shard_map/psum | solution.py:106
  254.0 3.1 copy-start.33
  258.7 7.8 %copy-start.32 = (bf16[1,48,72,1152]{3,2,1,0:T(8,128)(2,1)}, bf16[1,48,72,1152]{3,2,1,0:T(8,128)(2,1)S(1)}, u32[]{:S(2)}) copy-start(bf16[1,48,72,1152]{3,2,1,0:T(8,128)(2,1)S(1)} %get-tuple-element.98) | copy-start | bytes 23887876
  308.6 9.8 %copy-start.10 = (bf16[1,48,72,4,16]{2,4,3,0,1:T(8,128)(2,1)S(1)}, bf16[1,48,72,4,16]{2,4,3,0,1:T(8,128)(2,1)}, u32[]{:S(2)}) copy-start(bf16[1,48,72,4,16]{2,4,3,0,1:T(8,128)(2,1)} %copy-done.9) | copy-start | bytes 1327108
  313.8 5.1 copy-start.30
  313.8 5.1 copy-start.35
  320.3 244.0 %all-reduce.52.cloned.1.call-start = ((), (), s32[]{:S(2)}) async-start(), calls=%async_computation.7 | async-start | bytes 3670016 | tf_op jit(solution)/shard_map/psum | solution.py:140
  320.5 5.9 %copy-start.2 = (bf16[48,72,1024]{2,1,0:T(8,128)(2,1)S(1)}, bf16[48,72,1024]{2,1,0:T(8,128)(2,1)}, u32[]{:S(2)}) copy-start(bf16[48,72,1024]{2,1,0:T(8,128)(2,1)} %all-gather.6.cloned.1.call-done) | copy-start | bytes 21233668
  370.1 7.1 %slice-start = ((s8[7962624]{0:T(1024)(128)(4,1)}), s8[4194304]{0:T(1024)(128)(4,1)S(1)}, s32[]{:S(2)}) async-start(s8[7962624]{0:T(1024)(128)(4,1)} %bitcast.579), calls=%async_computation.8 | async-start | bytes 8388608
  371.5 5.8 %slice-start.1 = ((s8[7962624]{0:T(1024)(128)(4,1)}), s8[3768320]{0:T(1024)(128)(4,1)S(1)}, s32[]{:S(2)}) async-start(s8[7962624]{0:T(1024)(128)(4,1)} %bitcast.579), calls=%async_computation.9 | async-start | bytes 7536640
  371.5 8.2 %slice-start.2 = ((s8[7962624]{0:T(1024)(128)(4,1)}), s8[4194304]{0:T(1024)(128)(4,1)S(1)}, s32[]{:S(2)}) async-start(s8[7962624]{0:T(1024)(128)(4,1)} %bitcast.581), calls=%async_computation.10 | async-start | bytes 8388608
  405.9 4.5 copy-start.31
  405.9 63.2 %all-to-all-start.2 = ((bf16[1,48,72,128]{3,2,0,1:T(8,128)(2,1)}), bf16[1,48,72,128]{3,2,0,1:T(8,128)(2,1)S(1)}, u32[]{:S(2)}, u32[]{:S(2)}) async-start(bf16[1,48,72,128]{3,2,0,1:T(8,128)(2,1)} %fusion.239), calls=%async_computation.2 | async-start | bytes 1769472 | tf_op jit(solution)/shard_map/all_to_all | solution.py:136
  565.9 3.7 copy-start.1
  (23 other events, 41.6 us)
Sparse Core Ops, SparseCore 0:
  10.4 101.7 all-gather.3
  197.0 91.7 all-gather.5
  320.4 146.4 all-reduce.49
  470.1 94.1 all-reduce.51
where the time goes:
time: 585 us; the launch traced here: 577 us
  waiting for transfers between devices  260 us (44%)
  local copies, waits for them, and re-layouts  124 us (21%)
  matrix products  96.9 us (17%)
  other arithmetic  47.6 us (8%)
  blocking collectives  17 us (3%)
  starting transfers between devices  16.3 us (3%)
  between operations  15.1 us (3%)
    all_gather x1, waiting for transfers between devices, shards(): piece = lax.all_gather(features, 'sp', axis=1, tiled=True)  103 us
    psum x1, waiting for transfers between devices, shards(): lax.psum(point_part.astype(jnp.bfloat16), 'rep').astype(jnp.float32)  94 us
    unnamed x107, local copies, waits for them, and re-layouts  75 us
    dot_general x27, matrix products, shards(): jnp.dot(dpre[g], w_in[t].T, preferred_element_type=jnp.float32)  68.3 us
    psum x1, waiting for transfers between devices, shards(): proj_sum = lax.psum(proj_part, ('rep', 'sp'))  55.8 us
    dynamic_update_slice x4, other arithmetic, shards(): lax.dynamic_update_slice_in_dim(carry[add_g], block + contrib, begin_offs...  26.7 us
    all_to_all x1, blocking collectives, shards(): lax.all_to_all(own_pre, 'sp', split_axis=1, concat_axis=4, tiled=True)  17 us
    dot_general x5, matrix products, contract_cells(): lax.dot_general(left, right, (((0, 1, 2), (0, 1, 2)), ((), ())), preferre...  13.2 us
  transfers between devices with their start and end apart: 7, of which 4 were waited for; matrix products, arithmetic and copies ran while one was open for 34% of the time, Pallas kernels for 0%

commit v1 on v0

v1 whole, which is shorter than its diff:
```python
import functools

import jax
import jax.numpy as jnp
import numpy as np
from jax import lax
from jax.experimental import pallas as pl
from jax.experimental.pallas import tpu as pltpu
from jax.sharding import Mesh
from jax.sharding import PartitionSpec as P

DILATIONS = (6, 12, 18)
SETS = 2
CHIPS = 8
CELLS = 216
PADDED = 224
WIDTH = 72
HALO = 3
K = 512
COLS = 1792
BF16 = jnp.bfloat16
F32 = jnp.float32


def column_order():
    def tap(g, ky, kx):
        return 1 + 9 * g + 3 * (ky + 1) + (kx + 1)

    order = []
    for g in range(3):
        for ky in (-1, 0, 1):
            order += [tap(g, ky, -1), tap(g, ky, 1)]
    order += [tap(0, 0, 0), tap(1, 0, 0), tap(2, 0, 0), 0]
    for g in range(3):
        order += [tap(g, -1, 0), tap(g, 1, 0)]
    return order


ORDER = column_order()


def cell_column():
    row = lax.broadcasted_iota(jnp.int32, (CELLS, 128), 0)
    return jnp.where(row >= 144, row - 144, jnp.where(row >= 72, row - 72, row))


def low_lanes():
    return lax.broadcasted_iota(jnp.int32, (CELLS, 128), 1) < 64


def swap_halves(v):
    return pltpu.roll(v, 64, 1)


def forward_kernel(core, own, other, wt, out, a0, a1, a2, m0, m1, m2, b01, b2p):
    a, m = (a0, a1, a2), (m0, m1, m2)
    column = cell_column()
    low = low_lanes()
    me = core[0]
    zeros = jnp.zeros((HALO, CELLS, 128), F32)
    for which, x in enumerate((own, other)):
        slot = me if which == 0 else 1 - me
        for g in range(3):
            a[g][...] = jnp.zeros((CHIPS + 2 * HALO, CELLS, 128), F32)
            m[g][:HALO] = zeros
            m[g][HALO + CHIPS :] = zeros

        def step(i, _):
            rows = x[pl.ds(pl.multiple_of(i * 2 * CELLS, 2 * CELLS), 2 * CELLS), :]
            y = lax.dot_general(
                rows, wt[...], (((1,), (1,)), ((), ())), preferred_element_type=F32
            )
            for sub in range(2):
                j = 2 * i + sub
                part = y[sub * CELLS : (sub + 1) * CELLS]
                for g in range(3):
                    for n, ky in enumerate((-1, 0, 1)):
                        col = (3 * g + n) * 128
                        a[g][HALO + j - ky * (g + 1)] += part[:, col : col + 128]
                b01[j] = part[:, 9 * 128 : 10 * 128]
                b2p[j] = part[:, 10 * 128 : 11 * 128]
                for g in range(3):
                    m[g][HALO + j] = part[:, (11 + g) * 128 : (12 + g) * 128]
            return 0

        lax.fori_loop(0, CHIPS // 2, step, 0)

        def finish(j, _):
            totals = []
            for g, d in enumerate(DILATIONS):
                v = a[g][HALO + j]
                minus = jnp.where(column >= d, pltpu.roll(v, d, 0), 0.0)
                plus = jnp.where(column < WIDTH - d, pltpu.roll(v, CELLS - d, 0), 0.0)
                s = jnp.where(
                    low,
                    minus + m[g][HALO + j - (g + 1)],
                    plus + m[g][HALO + j + (g + 1)],
                )
                totals.append(s + swap_halves(s))
            c01 = swap_halves(b01[j])
            c2p = swap_halves(b2p[j])
            first = jnp.where(low, c2p, totals[0] + c01)
            second = jnp.where(low, totals[1] + c01, totals[2] + c2p)
            out[j, slot] = jnp.concatenate([first, second], 1).astype(BF16)
            return 0

        lax.fori_loop(0, CHIPS, finish, 0)


def forward(core, own, other, wt):
    vmem = pl.BlockSpec(memory_space=pltpu.VMEM)
    big = pltpu.VMEM((CHIPS + 2 * HALO, CELLS, 128), F32)
    small = pltpu.VMEM((CHIPS, CELLS, 128), F32)
    return pl.pallas_call(
        forward_kernel,
        out_shape=jax.ShapeDtypeStruct((CHIPS, SETS, CELLS, 256), BF16),
        in_specs=[pl.BlockSpec(memory_space=pltpu.SMEM), vmem, vmem, vmem],
        out_specs=vmem,
        scratch_shapes=[big] * 6 + [small] * 2,
        compiler_params=pltpu.CompilerParams(vmem_limit_bytes=56 << 20),
        cost_estimate=pl.CostEstimate(
            flops=2 * 3456 * K * COLS, bytes_accessed=8 << 20, transcendentals=0
        ),
    )(core, own, other, wt)


def sigmoid(v):
    return 1.0 / (1.0 + jnp.exp(-v))


def middle_kernel(got, proj, cot, projected, send, grad):
    parts = []
    for yh in range(2):
        for c in range(2):
            total = got[yh * 8 + c].astype(F32)
            for x in range(1, 4):
                total = total + got[yh * 8 + x * 2 + c].astype(F32)
            parts.append(total)
    pre = jnp.concatenate(parts, 1).astype(BF16).astype(F32)
    sig = sigmoid(pre)
    acts = (pre * sig).astype(BF16)
    slope = sig + pre * sig * (1.0 - sig)
    weight = proj[...]
    out_pre = jnp.dot(acts, weight, preferred_element_type=F32)
    osig = sigmoid(out_pre)
    projected[...] = (out_pre * osig).astype(BF16)
    dout = (cot[...].astype(F32) * (osig + out_pre * osig * (1.0 - osig))).astype(BF16)
    grad[...] = lax.dot_general(
        acts, dout, (((0,), (0,)), ((), ())), preferred_element_type=F32
    )
    dacts = lax.dot_general(
        dout, weight, (((1,), (1,)), ((), ())), preferred_element_type=F32
    )
    dpre = (dacts * slope).astype(BF16)
    for yh in range(2):
        for c in range(2):
            q = 2 * yh + c
            for x in range(4):
                send[yh * 8 + x * 2 + c] = dpre[:, q * 256 : (q + 1) * 256]


def middle(got, proj, cot):
    vmem = pl.BlockSpec(memory_space=pltpu.VMEM)
    return pl.pallas_call(
        middle_kernel,
        out_shape=(
            jax.ShapeDtypeStruct((CELLS, 256), BF16),
            jax.ShapeDtypeStruct((16, CELLS, 256), BF16),
            jax.ShapeDtypeStruct((1024, 256), F32),
        ),
        in_specs=[vmem] * 3,
        out_specs=(vmem,) * 3,
        compiler_params=pltpu.CompilerParams(vmem_limit_bytes=48 << 20),
    )(got, proj, cot)


def spread(got, slot, c, e, f01, f2p, dup):
    column = cell_column()
    low = low_lanes()
    halo = jnp.zeros((HALO, PADDED, 128), BF16)
    tail = jnp.zeros((PADDED - CELLS, 128), BF16)
    for g in range(3):
        for ref in (c[g], dup[g]):
            ref[:HALO] = halo
            ref[HALO + CHIPS :] = halo

    def put(ref, j, v):
        ref[j, :CELLS] = v.astype(BF16)
        ref[j, CELLS:] = tail

    def step(j, _):
        block = got[2 * j + slot]
        lo = block[:, :128].astype(F32)
        hi = block[:, 128:].astype(F32)
        rlo, rhi = swap_halves(lo), swap_halves(hi)
        twice = (jnp.where(low, rlo, lo), jnp.where(low, hi, rhi), jnp.where(low, rhi, hi))
        for g, d in enumerate(DILATIONS):
            v = twice[g]
            minus = jnp.where(column < WIDTH - d, pltpu.roll(v, CELLS - d, 0), 0.0)
            plus = jnp.where(column >= d, pltpu.roll(v, d, 0), 0.0)
            put(c[g], HALO + j, jnp.where(low, minus, plus))
            put(dup[g], HALO + j, v)
        put(f01, j, jnp.where(low, rlo, rhi))
        put(f2p, j, jnp.where(low, rhi, rlo))
        return 0

    lax.fori_loop(0, CHIPS, step, 0)
    lanes = lax.broadcasted_iota(jnp.int32, (PADDED, 128), 1) < 64

    def mix(j, _):
        for g in range(3):
            up = dup[g][HALO + j + g + 1].astype(F32)
            down = dup[g][HALO + j - g - 1].astype(F32)
            e[g][j] = jnp.where(lanes, up, down).astype(BF16)
        return 0

    lax.fori_loop(0, CHIPS, mix, 0)


def spread_scratch():
    halo = pltpu.VMEM((CHIPS + 2 * HALO, PADDED, 128), BF16)
    plain = pltpu.VMEM((CHIPS, PADDED, 128), BF16)
    return [halo] * 6 + [plain] * 5


def spread_columns(scratch, first, count):
    c, e, f01, f2p = scratch[0:3], scratch[6:9], scratch[9], scratch[10]

    def flat(v):
        return v.reshape(count * PADDED, 128)

    blocks = []
    for g in range(3):
        for ky in (-1, 0, 1):
            begin = HALO + first - ky * (g + 1)
            blocks.append(flat(c[g][pl.ds(begin, count)]))
    for ref in (f01, f2p, e[0], e[1], e[2]):
        blocks.append(flat(ref[pl.ds(first, count)]))
    return blocks


def kernel_grad_kernel(core, got, xt, out, total, *scratch):
    me = core[0]
    for which in range(2):
        slot = me if which == 0 else 1 - me
        spread(got, slot, scratch[0:3], scratch[6:9], scratch[9], scratch[10], scratch[3:6])
        left = xt[which]
        blocks = spread_columns(scratch, 0, CHIPS)
        for n in range(7):
            right = jnp.concatenate([blocks[2 * n], blocks[2 * n + 1]], 1)
            part = jnp.dot(left, right, preferred_element_type=F32)
            cols = slice(n * 256, (n + 1) * 256)
            if which == 0:
                total[:, cols] = part
            else:
                part = (part + total[:, cols]).astype(BF16)
                for q in range(4):
                    out[:, q, :, cols] = part[q * 128 : (q + 1) * 128].reshape(8, 16, 256)


def kernel_grad(core, got, xt):
    vmem = pl.BlockSpec(memory_space=pltpu.VMEM)
    return pl.pallas_call(
        kernel_grad_kernel,
        out_shape=jax.ShapeDtypeStruct((8, 4, 16, COLS), BF16),
        in_specs=[pl.BlockSpec(memory_space=pltpu.SMEM), vmem, vmem],
        out_specs=vmem,
        scratch_shapes=[pltpu.VMEM((K, COLS), F32)] + spread_scratch(),
        compiler_params=pltpu.CompilerParams(vmem_limit_bytes=56 << 20),
        cost_estimate=pl.CostEstimate(
            flops=2 * 3456 * K * COLS, bytes_accessed=8 << 20, transcendentals=0
        ),
    )(core, got, xt)


def feature_grad_kernel(core, got, wt, own, other, *scratch):
    me = core[0]
    for which, out in ((1, other), (0, own)):
        slot = me if which == 0 else 1 - me
        spread(got, slot, scratch[0:3], scratch[6:9], scratch[9], scratch[10], scratch[3:6])

        def step(i, _):
            left = jnp.concatenate(spread_columns(scratch, 2 * i, 2), 1)
            part = jnp.dot(left, wt[...], preferred_element_type=F32)
            for sub in range(2):
                out[2 * i + sub] = part[sub * PADDED : sub * PADDED + CELLS].astype(BF16)
            return 0

        lax.fori_loop(0, CHIPS // 2, step, 0)


def feature_grad(core, got, wt):
    vmem = pl.BlockSpec(memory_space=pltpu.VMEM)
    return pl.pallas_call(
        feature_grad_kernel,
        out_shape=(jax.ShapeDtypeStruct((CHIPS, CELLS, K), BF16),) * 2,
        in_specs=[pl.BlockSpec(memory_space=pltpu.SMEM), vmem, vmem],
        out_specs=(vmem,) * 2,
        scratch_shapes=spread_scratch(),
        compiler_params=pltpu.CompilerParams(vmem_limit_bytes=56 << 20),
        cost_estimate=pl.CostEstimate(
            flops=2 * 3456 * K * COLS, bytes_accessed=8 << 20, transcendentals=0
        ),
    )(core, got, wt)


def place_matrix():
    place = np.zeros((4, 128, 512), np.float32)
    for yh in range(2):
        for c in range(2):
            for tap in range(2):
                for x in range(4):
                    for i in range(16):
                        place[2 * yh + c, tap * 64 + x * 16 + i, tap * 256 + yh * 128 + x * 32 + c * 16 + i] = 0.125
    return place.reshape(512, 512)


def place_kernel(got, place, point, atrous):
    for v in range(14):
        lanes = slice(v * 128, (v + 1) * 128)
        left = jnp.concatenate([got[:, q, :, lanes].reshape(128, 128) for q in range(4)], 1)
        wide = jnp.dot(left, place[...], preferred_element_type=F32)
        for half in range(2):
            tap = ORDER[2 * v + half]
            part = wide[:, half * 256 : (half + 1) * 256]
            if tap == 0:
                point[...] = part
            else:
                atrous[tap - 1] = part


def place_grads(got):
    vmem = pl.BlockSpec(memory_space=pltpu.VMEM)
    return pl.pallas_call(
        place_kernel,
        out_shape=(
            jax.ShapeDtypeStruct((128, 256), F32),
            jax.ShapeDtypeStruct((27, 128, 256), F32),
        ),
        in_specs=[vmem] * 2,
        out_specs=(vmem,) * 2,
        compiler_params=pltpu.CompilerParams(vmem_limit_bytes=40 << 20),
    )(got, jnp.asarray(place_matrix(), BF16))


def shards(features, atrous_weight, point_weight, proj_weight, cotangent):
    core = lax.axis_index("c").astype(jnp.int32).reshape(1)

    atrous_t = jnp.transpose(atrous_weight, (0, 2, 1))
    point_t = jnp.transpose(point_weight, (1, 0))[None]
    every_t = [point_t] + [atrous_t[t : t + 1] for t in range(27)]
    stacked = jnp.concatenate([every_t[t] for t in ORDER], 0)
    w_send = jnp.transpose(stacked.reshape(28, 16, 2, 4, 2, 128), (3, 0, 1, 2, 4, 5))
    w_got = lax.all_to_all(w_send.reshape(4, 28, 16, K), "x", 0, 0, tiled=True)
    wt = jnp.transpose(w_got, (1, 0, 2, 3)).reshape(COLS, K)

    by_column = jnp.transpose(features.reshape(CELLS, 2, 4, 2, 128), (2, 0, 1, 3, 4)).reshape(4, CELLS, K)
    x_send = jnp.broadcast_to(by_column[None], (2, 4, CELLS, K)).reshape(CHIPS, CELLS, K)
    own = lax.all_to_all(x_send, ("yh", "x"), 0, 0, tiled=True)
    other = lax.ppermute(own, "c", [(0, 1), (1, 0)])

    partial = forward(core, own.reshape(CHIPS * CELLS, K), other.reshape(CHIPS * CELLS, K), wt)
    got = lax.all_to_all(partial.reshape(16, CELLS, 256), ("yh", "x", "c"), 0, 0, tiled=True)

    proj = proj_weight.reshape(4, 2, 4, 2, 16, 256).transpose(1, 3, 0, 2, 4, 5).reshape(1024, 256)
    projected, d_send, proj_part = middle(got, proj, cotangent.reshape(CELLS, 256))
    proj_sum = lax.psum(proj_part, ("z", "yl", "yh", "x", "c"))
    grad_proj = (
        proj_sum.reshape(2, 2, 4, 4, 16, 256).transpose(2, 0, 3, 1, 4, 5).reshape(1024, 256) * 0.125
    )
    dpre = lax.all_to_all(d_send, ("yh", "x", "c"), 0, 0, tiled=True)

    def turned(v):
        padded = jnp.pad(v, ((0, 0), (0, PADDED - CELLS), (0, 0)))
        return jnp.transpose(padded.reshape(CHIPS * PADDED, K))

    xt = jnp.stack([turned(own), turned(other)])
    g_part = kernel_grad(core, dpre, xt)
    g_got = lax.all_to_all(g_part.reshape(32, 16, COLS), ("z", "yl", "yh", "c"), 0, 0, tiled=True)
    g_sum = jnp.sum(g_got.reshape(8, 4, 16, COLS).astype(F32), 0).astype(BF16)
    g_all = lax.all_to_all(
        jnp.broadcast_to(g_sum[None], (8, 4, 16, COLS)), ("z", "yl"), 0, 0, tiled=True
    )
    grad_point, grad_atrous = place_grads(g_all)

    back_own, back_other = feature_grad(core, dpre, wt)
    back_got = lax.ppermute(back_other, "c", [(0, 1), (1, 0)])
    back = (back_own.astype(F32) + back_got.astype(F32)).astype(BF16)
    b_got = lax.all_to_all(back, ("yh", "x"), 0, 0, tiled=True).reshape(2, 4, CELLS, 2, 256)
    b_sum = (b_got[0].astype(F32) + b_got[1].astype(F32)).astype(BF16)
    input_grad = jnp.transpose(b_sum, (1, 2, 0, 3)).reshape(1, 3, WIDTH, 2048)

    return (
        projected.reshape(1, 3, WIDTH, 256),
        input_grad,
        grad_point,
        grad_atrous,
        grad_proj,
    )


def solution(mesh):
    fine = Mesh(mesh.devices.reshape(4, 2, 2, 4, 2), ("z", "yl", "yh", "x", "c"))
    rep, sp = ("z", "yl"), ("yh", "x", "c")
    in_specs = (
        P(rep, sp, None, None),
        P(None, None, sp),
        P(None, sp),
        P(),
        P(rep, sp, None, None),
    )
    out_specs = (
        P(rep, sp, None, None),
        P(rep, sp, None, None),
        P(sp, None),
        P(None, sp, None),
        P(),
    )
    return jax.shard_map(shards, mesh=fine, in_specs=in_specs, out_specs=out_specs, check_vma=False)
```

time: 585 us -> 439 us (0.75); the launches traced: 577 us -> 438 us
  matrix products: 96.9 us -> 0 us
  local copies, waits for them, and re-layouts: 124 us -> 50.6 us
  Pallas kernels: 0 us -> 51.5 us
  other arithmetic: 47.6 us -> 11.6 us
  starting transfers between devices: 16.3 us -> 36 us
  blocking collectives: 17 us -> 0 us
  waiting for transfers between devices: 260 us -> 274 us
    all_to_all x3 -> x7, waiting for transfers between devices: 6.7 us -> 116 us  [the longest x1 25.1 us: shards(): lax.all_to_all(partial.reshape(16, CELLS, 256), ('yh', 'x', 'c'), 0, 0, t...]
    all_gather x2 -> x0, waiting for transfers between devices: 103 us -> none  [the longest x1 103 us: shards(): piece = lax.all_gather(features, 'sp', axis=1, tiled=True)]
    dot_general x36 -> x0, matrix products: 96.9 us -> none  [the longest x27 68.3 us: shards(): jnp.dot(dpre[g], w_in[t].T, preferred_element_type=jnp.float32)]
    unnamed x107 -> x29, local copies, waits for them, and re-layouts: 75 us -> 14.6 us
    pallas_call x0 -> x5, Pallas kernels: none -> 51.5 us  [the longest x1 16.3 us: forward(): pl.pallas_call(forward_kernel, out_shape=jax.ShapeDtypeStruct((CHIPS, SET...]
    dynamic_update_slice x4 -> x0, other arithmetic: 26.7 us -> none  [shards(): lax.dynamic_update_slice_in_dim(carry[add_g], block + contrib, begin_offs...]
    all_to_all x3 -> x7, starting transfers between devices: 16 us -> 34.4 us  [the longest x1 7.61 us: shards(): own = lax.all_to_all(x_send, ('yh', 'x'), 0, 0, tiled=True)]
    all_to_all x1 -> x0, blocking collectives: 17 us -> none  [shards(): lax.all_to_all(own_pre, 'sp', split_axis=1, concat_axis=4, tiled=True)]
  transfers between devices with their start and end apart: 7 -> 10, of which waited for: 4 -> 7; matrix products, arithmetic and copies ran while one was open for 34% -> 12% of each run, Pallas kernels for 0% -> 3%
where the time goes in v1:
time: 439 us; the launch traced here: 438 us
  waiting for transfers between devices  274 us (62%)
  Pallas kernels  51.5 us (12%)
  local copies, waits for them, and re-layouts  50.6 us (12%)
  starting transfers between devices  36 us (8%)
  between operations  14.3 us (3%)
  other arithmetic  11.6 us (3%)
    psum x1, waiting for transfers between devices, shards(): proj_sum = lax.psum(proj_part, ('z', 'yl', 'yh', 'x', 'c'))  157 us
    all_to_all x1, waiting for transfers between devices, shards(): lax.all_to_all(partial.reshape(16, CELLS, 256), ('yh', 'x', 'c'), 0, 0, t...  25.1 us
    all_to_all x1, waiting for transfers between devices, shards(): lax.all_to_all(back, ('yh', 'x'), 0, 0, tiled=True)  24.6 us
    all_to_all x1, waiting for transfers between devices, shards(): w_got = lax.all_to_all(w_send.reshape(4, 28, 16, K), 'x', 0, 0, tiled=True)  23.7 us
    all_to_all x1, waiting for transfers between devices, shards(): lax.all_to_all(g_part.reshape(32, 16, COLS), ('z', 'yl', 'yh', 'c'), 0, 0...  21.8 us
    pallas_call x1, Pallas kernels, forward(): pl.pallas_call(forward_kernel, out_shape=jax.ShapeDtypeStruct((CHIPS, SET...  16.3 us
    pallas_call x1, Pallas kernels, kernel_grad(): pl.pallas_call(kernel_grad_kernel, out_shape=jax.ShapeDtypeStruct((8, 4,...  15.2 us
    pallas_call x1, Pallas kernels, feature_grad(): pl.pallas_call(feature_grad_kernel, out_shape=(jax.ShapeDtypeStruct((CHIP...  15.1 us
  transfers between devices with their start and end apart: 10, of which 7 were waited for; matrix products, arithmetic and copies ran while one was open for 12% of the time, Pallas kernels for 3%

profile of v1, /device:TPU:1, one launch (start us, length us, event | category | flops | bytes accessed | tf_op | source)
XLA Modules:
  0.0 437.9 jit_solution(9415813222242937633)
XLA Ops:
  12.2 7.6 %all-to-all-start = ((bf16[8,216,512]{2,1,0:T(8,128)(2,1)}), bf16[8,216,512]{2,1,0:T(8,128)(2,1)}, u32[]{:S(2)}, u32[]{:S(2)}) async-start(bf16[8,216,512]{2,1,0:T(8,128)(2,1)} %bitcast.2), calls=%async_computation | async-start | bytes 3538944 | tf_op jit(solution)/shard_map/all_to_all | solution.py:359
  33.3 11.7 %all-to-all-done = bf16[8,216,512]{2,1,0:T(8,128)(2,1)} async-done(((bf16[8,216,512]{2,1,0:T(8,128)(2,1)}), bf16[8,216,512]{2,1,0:T(8,128)(2,1)}, u32[]{:S(2)}, u32[]{:S(2)}) %all-to-all-start) | async-done | bytes 1769504 | tf_op jit(solution)/shard_map/all_to_all | solution.py:359
  48.7 3.6 copy.54
  53.9 3.6 all-to-all-start.1
  57.5 23.7 %all-to-all-done.1 = bf16[4,28,16,512]{3,2,1,0:T(8,128)(2,1)S(1)} async-done(((bf16[4,28,16,512]{3,2,1,0:T(8,128)(2,1)}), bf16[4,28,16,512]{3,2,1,0:T(8,128)(2,1)S(1)}, u32[]{:S(2)}, u32[]{:S(2)}) %all-to-all-start.1) | async-done | bytes 1835040 | tf_op jit(solution)/shard_map/all_to_all | solution.py:354
  82.6 16.3 %shard_map.101 = bf16[8,2,216,256]{3,2,1,0:T(8,128)(2,1)} custom-call(s32[1]{0:T(128)} %bitcast.core, bf16[1728,512]{1,0:T(8,128)(2,1)} %bitcast.3.own, bf16[1728,512]{1,0:T(8,128)(2,1)} %bitcast.4.other, bf16[1792,512]{1,0:T(8,128)(2,1)} %bitcast.50), custom_call_target="tpu_custom_call" | custom-call | flops 6341787648 | bytes 8388608 | tf_op jit(solution)/shard_map/pallas_call | solution.py:114
  98.8 4.4 %all-to-all-start.2 = ((bf16[16,216,256]{2,1,0:T(8,128)(2,1)}), bf16[16,216,256]{2,1,0:T(8,128)(2,1)S(1)}, u32[]{:S(2)}, u32[]{:S(2)}) async-start(bf16[16,216,256]{2,1,0:T(8,128)(2,1)} %bitcast.53), calls=%async_computation.2 | async-start | bytes 3538944 | tf_op jit(solution)/shard_map/all_to_all | solution.py:363
  103.3 25.1 %all-to-all-done.2.got = bf16[16,216,256]{2,1,0:T(8,128)(2,1)S(1)} async-done(((bf16[16,216,256]{2,1,0:T(8,128)(2,1)}), bf16[16,216,256]{2,1,0:T(8,128)(2,1)S(1)}, u32[]{:S(2)}, u32[]{:S(2)}) %all-to-all-start.2) | async-done | bytes 1769504 | tf_op jit(solution)/shard_map/all_to_all | solution.py:363
  131.7 4.8 %all-to-all-start.3 = ((bf16[16,216,256]{2,1,0:T(8,128)(2,1)}), bf16[16,216,256]{2,1,0:T(8,128)(2,1)}, u32[]{:S(2)}, u32[]{:S(2)}) async-start(bf16[16,216,256]{2,1,0:T(8,128)(2,1)} %copy-done), calls=%async_computation.3 | async-start | bytes 3538944 | tf_op jit(solution)/shard_map/all_to_all | solution.py:371
  136.5 3.0 pad.7
  142.3 2.9 pad.8
  145.2 3.9 copy.49
  149.0 3.7 pad_maximum_fusion.xt
  152.7 9.1 %all-to-all-done.3.got = bf16[16,216,256]{2,1,0:T(8,128)(2,1)} async-done(((bf16[16,216,256]{2,1,0:T(8,128)(2,1)}), bf16[16,216,256]{2,1,0:T(8,128)(2,1)}, u32[]{:S(2)}, u32[]{:S(2)}) %all-to-all-start.3) | async-done | bytes 1769504 | tf_op jit(solution)/shard_map/all_to_all | solution.py:371
  161.8 15.1 %shard_map.103 = (bf16[8,216,512]{2,1,0:T(8,128)(2,1)}, bf16[8,216,512]{2,1,0:T(8,128)(2,1)}) custom-call(s32[1]{0:T(128)} %bitcast.core, bf16[16,216,256]{2,1,0:T(8,128)(2,1)} %all-to-all-done.3.got, bf16[1792,512]{1,0:T(8,128)(2,1)} %bitcast.51), custom_call_target="tpu_custom_call" | custom-call | flops 6341787648 | bytes 8388608 | tf_op jit(solution)/shard_map/pallas_call | solution.py:294
  177.6 15.2 %shard_map.104 = bf16[8,4,16,1792]{3,2,1,0:T(8,128)(2,1)} custom-call(s32[1]{0:T(128)} %bitcast.core, bf16[16,216,256]{2,1,0:T(8,128)(2,1)} %all-to-all-done.3.got, bf16[2,512,1792]{2,1,0:T(8,128)(2,1)} %pad_maximum_fusion.xt), custom_call_target="tpu_custom_call" | custom-call | flops 6341787648 | bytes 8388608 | tf_op jit(solution)/shard_map/pallas_call | solution.py:263
  192.8 5.8 %all-to-all-start.5 = ((bf16[32,16,1792]{2,1,0:T(8,128)(2,1)}), bf16[32,16,1792]{2,1,0:T(8,128)(2,1)S(1)}, u32[]{:S(2)}, u32[]{:S(2)}) async-start(bf16[32,16,1792]{2,1,0:T(8,128)(2,1)} %bitcast.52), calls=%async_computation.5 | async-start | bytes 3670016 | tf_op jit(solution)/shard_map/all_to_all | solution.py:379
  198.7 3.8 add_convert_fusion
  202.4 21.8 %all-to-all-done.5 = bf16[32,16,1792]{2,1,0:T(8,128)(2,1)S(1)} async-done(((bf16[32,16,1792]{2,1,0:T(8,128)(2,1)}), bf16[32,16,1792]{2,1,0:T(8,128)(2,1)S(1)}, u32[]{:S(2)}, u32[]{:S(2)}) %all-to-all-start.5) | async-done | bytes 1835040 | tf_op jit(solution)/shard_map/all_to_all | solution.py:379
  224.2 4.5 %all-to-all-start.4 = ((bf16[8,216,512]{2,1,0:T(8,128)(2,1)}), bf16[8,216,512]{2,1,0:T(8,128)(2,1)}, u32[]{:S(2)}, u32[]{:S(2)}) async-start(bf16[8,216,512]{2,1,0:T(8,128)(2,1)} %add_convert_fusion), calls=%async_computation.4 | async-start | bytes 3538944 | tf_op jit(solution)/shard_map/all_to_all | solution.py:389
  229.0 24.6 %all-to-all-done.4 = bf16[8,216,512]{2,1,0:T(8,128)(2,1)} async-done(((bf16[8,216,512]{2,1,0:T(8,128)(2,1)}), bf16[8,216,512]{2,1,0:T(8,128)(2,1)}, u32[]{:S(2)}, u32[]{:S(2)}) %all-to-all-start.4) | async-done | bytes 1769504 | tf_op jit(solution)/shard_map/all_to_all | solution.py:389
  255.1 3.6 all-to-all-start.6
  259.4 157.2 %all-reduce.4.cloned.1.call-done = f32[1024,256]{1,0:T(8,128)} async-done(((f32[1024,256]{1,0:T(8,128)}), f32[1024,256]{1,0:T(8,128)}) %all-reduce.4.cloned.1.call-update) | async-done | bytes 1048592 | tf_op jit(solution)/shard_map/psum | solution.py:367
  428.1 2.9 shard_map.105
  (76 shorter events, 45.8 us)
Async XLA Ops:
  12.2 7.6 %copy-start.3 = (bf16[27,2048,16]{1,2,0:T(8,128)(2,1)S(1)}, bf16[27,2048,16]{1,2,0:T(8,128)(2,1)}, u32[]{:S(2)}) copy-start(bf16[27,2048,16]{1,2,0:T(8,128)(2,1)} %param.7) | copy-start | bytes 5308420
  12.2 32.8 %all-to-all-start = ((bf16[8,216,512]{2,1,0:T(8,128)(2,1)}), bf16[8,216,512]{2,1,0:T(8,128)(2,1)}, u32[]{:S(2)}, u32[]{:S(2)}) async-start(bf16[8,216,512]{2,1,0:T(8,128)(2,1)} %bitcast.2), calls=%async_computation | async-start | bytes 3538944 | tf_op jit(solution)/shard_map/all_to_all | solution.py:359
  45.0 37.6 %collective-permute-start = (bf16[8,216,512]{2,1,0:T(8,128)(2,1)}, bf16[8,216,512]{2,1,0:T(8,128)(2,1)}, u32[]{:S(2)}, u32[]{:S(2)}) collective-permute-start(bf16[8,216,512]{2,1,0:T(8,128)(2,1)} %all-to-all-done), channel_id=1, source_target_pairs={{0,1},{1,0},{2,3},{3,2},{4,5},{5,4},{6,7},{7,6},{8,9},{9,8},{10,11... | collective-permute-start | bytes 5308424 | tf_op jit(solution)/shard_map/ppermute | solution.py:360
  53.9 27.2 %all-to-all-start.1 = ((bf16[4,28,16,512]{3,2,1,0:T(8,128)(2,1)}), bf16[4,28,16,512]{3,2,1,0:T(8,128)(2,1)S(1)}, u32[]{:S(2)}, u32[]{:S(2)}) async-start(bf16[4,28,16,512]{3,2,1,0:T(8,128)(2,1)} %reshape.105), calls=%async_computation.1 | async-start | bytes 3670016 | tf_op jit(solution)/shard_map/all_to_all | solution.py:354
  98.8 4.4 %copy-start.4 = (bf16[1024,256]{1,0:T(8,128)(2,1)S(1)}, bf16[1024,256]{1,0:T(8,128)(2,1)}, u32[]{:S(2)}) copy-start(bf16[1024,256]{1,0:T(8,128)(2,1)} %param.9) | copy-start | bytes 1572868
  98.8 29.6 %copy-start.2 = (bf16[1,3,72,256]{3,2,1,0:T(8,128)(2,1)S(1)}, bf16[1,3,72,256]{3,2,1,0:T(8,128)(2,1)}, u32[]{:S(2)}) copy-start(bf16[1,3,72,256]{3,2,1,0:T(8,128)(2,1)} %param.10) | copy-start | bytes 331780
  98.8 29.6 %all-to-all-start.2 = ((bf16[16,216,256]{2,1,0:T(8,128)(2,1)}), bf16[16,216,256]{2,1,0:T(8,128)(2,1)S(1)}, u32[]{:S(2)}, u32[]{:S(2)}) async-start(bf16[16,216,256]{2,1,0:T(8,128)(2,1)} %bitcast.53), calls=%async_computation.2 | async-start | bytes 3538944 | tf_op jit(solution)/shard_map/all_to_all | solution.py:363
  130.4 1.2 copy-start
  131.7 30.1 %all-to-all-start.3 = ((bf16[16,216,256]{2,1,0:T(8,128)(2,1)}), bf16[16,216,256]{2,1,0:T(8,128)(2,1)}, u32[]{:S(2)}, u32[]{:S(2)}) async-start(bf16[16,216,256]{2,1,0:T(8,128)(2,1)} %copy-done), calls=%async_computation.3 | async-start | bytes 3538944 | tf_op jit(solution)/shard_map/all_to_all | solution.py:371
  176.9 21.7 %collective-permute-start.1 = (bf16[8,216,512]{2,1,0:T(8,128)(2,1)}, bf16[8,216,512]{2,1,0:T(8,128)(2,1)}, u32[]{:S(2)}, u32[]{:S(2)}) collective-permute-start(bf16[8,216,512]{2,1,0:T(8,128)(2,1)} %get-tuple-element.15), channel_id=1, source_target_pairs={{0,1},{1,0},{2,3},{3,2},{4,5},{5,4},{6,7},{7,6},{8,9},{9,8},{10,11... | collective-permute-start | bytes 5308424 | tf_op jit(solution)/shard_map/ppermute | solution.py:387
  192.8 31.4 %all-to-all-start.5 = ((bf16[32,16,1792]{2,1,0:T(8,128)(2,1)}), bf16[32,16,1792]{2,1,0:T(8,128)(2,1)S(1)}, u32[]{:S(2)}, u32[]{:S(2)}) async-start(bf16[32,16,1792]{2,1,0:T(8,128)(2,1)} %bitcast.52), calls=%async_computation.5 | async-start | bytes 3670016 | tf_op jit(solution)/shard_map/all_to_all | solution.py:379
  224.2 29.5 %all-to-all-start.4 = ((bf16[8,216,512]{2,1,0:T(8,128)(2,1)}), bf16[8,216,512]{2,1,0:T(8,128)(2,1)}, u32[]{:S(2)}, u32[]{:S(2)}) async-start(bf16[8,216,512]{2,1,0:T(8,128)(2,1)} %add_convert_fusion), calls=%async_computation.4 | async-start | bytes 3538944 | tf_op jit(solution)/shard_map/all_to_all | solution.py:389
  255.1 173.1 %all-to-all-start.6 = ((bf16[8,4,16,1792]{3,2,1,0:T(8,128)(2,1)}), bf16[8,4,16,1792]{3,2,1,0:T(8,128)(2,1)S(1)}, u32[]{:S(2)}, u32[]{:S(2)}) async-start(bf16[8,4,16,1792]{3,2,1,0:T(8,128)(2,1)} %broadcast_in_dim.16), calls=%async_computation.6 | async-start | bytes 3670016 | tf_op jit(solution)/shard_map/all_to_all | solution.py:381
  258.7 157.9 %all-reduce.4.cloned.1.call-start = ((), (), s32[]{:S(2)}) async-start(), calls=%async_computation.7 | async-start | bytes 2097152 | tf_op jit(solution)/shard_map/psum | solution.py:367
  423.9 4.3 copy-start.1
Sparse Core Ops, SparseCore 0:
  264.9 151.6 all-reduce.3

commit v2 on v0

v2 whole, which is shorter than its diff:
```python
import jax
import jax.numpy as jnp
from jax import lax
from jax.experimental import pallas as pl
from jax.experimental.pallas import tpu as pltpu
from jax.sharding import Mesh
from jax.sharding import PartitionSpec as P

DILATIONS = (6, 12, 18)
CHIPS = 8
CELLS = 216
PADDED = 224
WIDTH = 72
HALO = 3
K = 512
TAPS = 28
COLS = TAPS * 128
QUARTER = TAPS // 4
BF16 = jnp.bfloat16
F32 = jnp.float32
VMEM = pl.BlockSpec(memory_space=pltpu.VMEM)
SMEM = pl.BlockSpec(memory_space=pltpu.SMEM)


def tap_of(g, ky, kx):
    return 1 + 9 * g + 3 * (ky + 1) + (kx + 1)


def tap_pairs():
    def tap(g, ky, kx):
        return (tap_of(g, ky, kx), g, ky, kx)

    pairs = [((0, -1, 0, 0), tap(0, 0, 0)), (tap(1, 0, 0), tap(2, 0, 0))]
    for ky in (0, -1, 1):
        for g in range(3):
            pairs.append((tap(g, ky, -1), tap(g, ky, 1)))
    for ky in (-1, 1):
        pairs.append((tap(0, ky, 0), tap(1, ky, 0)))
    pairs.append((tap(2, -1, 0), tap(2, 1, 0)))
    return pairs


PAIRS = tap_pairs()


def params(mib):
    return pltpu.CompilerParams(vmem_limit_bytes=mib << 20)


def cost(flops, nbytes):
    return pl.CostEstimate(flops=flops, bytes_accessed=nbytes, transcendentals=0)


CONV_COST = cost(2 * 1728 * K * COLS, 8 << 20)


def cell_column(rows):
    row = lax.broadcasted_iota(jnp.int32, (rows, 128), 0)
    return jnp.where(row >= 144, row - 144, jnp.where(row >= 72, row - 72, row))


def split_features_kernel(x, out):
    for col in range(4):
        for yh in range(2):
            part = x[:, (yh * 4 + col) * 256 : (yh * 4 + col + 1) * 256]
            for dest in range(2):
                out[dest * 4 + col, :, yh * 256 : (yh + 1) * 256] = part


def split_features(x):
    return pl.pallas_call(
        split_features_kernel,
        out_shape=jax.ShapeDtypeStruct((CHIPS, CELLS, K), BF16),
        in_specs=[VMEM],
        out_specs=VMEM,
        compiler_params=params(16),
        cost_estimate=cost(0, 3 << 20),
    )(x)


def split_weights_kernel(place, point, atrous, out0, out1, out2, out3, taps, sem):
    z, x = place[0], place[1]
    begin = jnp.where(z == 0, 0, QUARTER * z - 1)
    copy = pltpu.make_async_copy(atrous.at[pl.ds(begin, QUARTER)], taps.at[pl.ds(1, QUARTER)], sem)
    copy.start()
    taps[0] = point[...]
    copy.wait()
    first = jnp.where(z == 0, 0, 1)
    for d, out in enumerate((out0, out1, out2, out3)):
        col = lax.rem(x + d, 4)
        for yh in range(2):
            lanes = pl.ds(pl.multiple_of((yh * 4 + col) * 256, 256), 256)
            for t in range(QUARTER):
                out[t, :, yh * 256 : (yh + 1) * 256] = taps[first + t, :, lanes]


def split_weights(place, point, atrous):
    return pl.pallas_call(
        split_weights_kernel,
        out_shape=(jax.ShapeDtypeStruct((QUARTER, 16, K), BF16),) * 4,
        in_specs=[SMEM, VMEM, pl.BlockSpec(memory_space=pl.ANY)],
        out_specs=(VMEM,) * 4,
        scratch_shapes=[pltpu.VMEM((QUARTER + 1, 16, 2048), BF16), pltpu.SemaphoreType.DMA],
        compiler_params=params(16),
        cost_estimate=cost(0, 1 << 20),
    )(place, point, atrous)


def join_weights_kernel(place, *refs):
    out = refs[8]
    z, me = place[0], place[2]
    for which in range(2):
        c = me if which == 0 else 1 - me
        for d in range(4):
            quarter = lax.rem(z + 4 - d, 4)
            block = refs[which * 4 + d]
            for x in range(4):
                for t in range(QUARTER):
                    out[quarter * QUARTER + t, x, c] = block[x, t]


def join_weights(place, blocks):
    return pl.pallas_call(
        join_weights_kernel,
        out_shape=jax.ShapeDtypeStruct((TAPS, 4, 2, 16, K), BF16),
        in_specs=[SMEM] + [VMEM] * 8,
        out_specs=VMEM,
        compiler_params=params(24),
        cost_estimate=cost(0, 8 << 20),
    )(place, *blocks)


def stack_columns_kernel(place, b0, b1, b2, b3, out):
    for d, block in enumerate((b0, b1, b2, b3)):
        out[lax.rem(place[1] + 4 - d, 4)] = block[...]


def stack_columns(place, blocks):
    return pl.pallas_call(
        stack_columns_kernel,
        out_shape=jax.ShapeDtypeStruct((4, QUARTER, 16, K), BF16),
        in_specs=[SMEM] + [VMEM] * 4,
        out_specs=VMEM,
        compiler_params=params(16),
        cost_estimate=cost(0, 1 << 20),
    )(place, *blocks)


def forward_kernel(x, wt, out, xs, acc):
    for j in range(CHIPS):
        xs[j, :CELLS] = x[j]
        xs[j, CELLS:] = jnp.zeros((PADDED - CELLS, K), BF16)

    def span(g, ky):
        return max(0, ky * (g + 1)), CHIPS + min(0, ky * (g + 1))

    for pair in PAIRS:
        begin = min(span(g, ky)[0] for _, g, ky, _ in pair)
        end = max(span(g, ky)[1] for _, g, ky, _ in pair)
        rows = xs[begin:end].reshape((end - begin) * PADDED, K)
        right = jnp.concatenate([wt[t] for t, _, _, _ in pair], 0)
        y = lax.dot_general(rows, right, (((1,), (1,)), ((), ())), preferred_element_type=F32)
        y = y.reshape(end - begin, PADDED, 256)
        for half, (_, g, ky, kx) in enumerate(pair):
            which = 3 if g < 0 else (g if kx == 0 else 4 + 2 * g + (kx + 1) // 2)
            lo, hi = span(g, ky)
            part = y[lo - begin : hi - begin, :, half * 128 : (half + 1) * 128]
            to = slice(lo - ky * (g + 1), hi - ky * (g + 1))
            if ky == 0:
                acc[which, to] = part
            else:
                acc[which, to] += part

    column = cell_column(PADDED)

    def finish(j, _):
        parts = [acc[3, j]]
        for g, d in enumerate(DILATIONS):
            minus = pltpu.roll(acc[4 + 2 * g, j], d, 0)
            plus = pltpu.roll(acc[5 + 2 * g, j], PADDED - d, 0)
            parts.append(
                acc[g, j]
                + jnp.where(column >= d, minus, 0.0)
                + jnp.where(column < WIDTH - d, plus, 0.0)
            )
        out[j] = jnp.concatenate(parts, 1).astype(BF16)[:CELLS]
        return 0

    lax.fori_loop(0, CHIPS, finish, 0)


def forward(x, wt):
    return pl.pallas_call(
        forward_kernel,
        out_shape=jax.ShapeDtypeStruct((CHIPS, CELLS, 512), BF16),
        in_specs=[VMEM] * 2,
        out_specs=VMEM,
        scratch_shapes=[
            pltpu.VMEM((CHIPS, PADDED, K), BF16),
            pltpu.VMEM((10, CHIPS, PADDED, 128), F32),
        ],
        compiler_params=params(56),
        cost_estimate=CONV_COST,
    )(x, wt)


def sigmoid(v):
    return 1.0 / (1.0 + jnp.exp(-v))


def middle_kernel(got, proj, cot, projected, send, grad):
    parts = []
    for yh in range(2):
        total = got[yh * 4].astype(F32)
        for x in range(1, 4):
            total = total + got[yh * 4 + x].astype(F32)
        parts.append(total)
    pre = jnp.concatenate(parts, 1).astype(BF16).astype(F32)
    sig = sigmoid(pre)
    acts = (pre * sig).astype(BF16)
    slope = sig + pre * sig * (1.0 - sig)
    weight = proj[...]
    out_pre = jnp.dot(acts, weight, preferred_element_type=F32)
    osig = sigmoid(out_pre)
    projected[...] = (out_pre * osig).astype(BF16)
    dout = (cot[...].astype(F32) * (osig + out_pre * osig * (1.0 - osig))).astype(BF16)
    dacts = lax.dot_general(
        dout, weight, (((1,), (1,)), ((), ())), preferred_element_type=F32
    )
    dpre = (dacts * slope).astype(BF16)
    for yh in range(2):
        for x in range(4):
            send[yh * 4 + x] = dpre[:, yh * 512 : (yh + 1) * 512]
    grad[...] = lax.dot_general(
        acts, dout, (((0,), (0,)), ((), ())), preferred_element_type=F32
    )


def middle(got, proj, cot):
    return pl.pallas_call(
        middle_kernel,
        out_shape=(
            jax.ShapeDtypeStruct((CELLS, 256), BF16),
            jax.ShapeDtypeStruct((CHIPS, CELLS, 512), BF16),
            jax.ShapeDtypeStruct((1024, 256), F32),
        ),
        in_specs=[VMEM] * 3,
        out_specs=(VMEM,) * 3,
        compiler_params=params(48),
    )(got, proj, cot)


SPREAD = [pltpu.VMEM((9, CHIPS + 2 * HALO, PADDED, 128), BF16), pltpu.VMEM((CHIPS, PADDED, 128), BF16)]


def spread(got, moved, point):
    column = cell_column(CELLS)
    for n in range(9):
        moved[n, :HALO] = jnp.zeros((HALO, PADDED, 128), BF16)
        moved[n, HALO + CHIPS :] = jnp.zeros((HALO, PADDED, 128), BF16)
    tail = jnp.zeros((PADDED - CELLS, 128), BF16)

    def step(j, _):
        point[j, :CELLS] = got[j, :, :128]
        point[j, CELLS:] = tail
        for g, d in enumerate(DILATIONS):
            v = got[j, :, (g + 1) * 128 : (g + 2) * 128]
            wide = v.astype(F32)
            minus = jnp.where(column < WIDTH - d, pltpu.roll(wide, CELLS - d, 0), 0.0)
            plus = jnp.where(column >= d, pltpu.roll(wide, d, 0), 0.0)
            for kx, part in enumerate((minus.astype(BF16), v, plus.astype(BF16))):
                moved[3 * g + kx, HALO + j, :CELLS] = part
                moved[3 * g + kx, HALO + j, CELLS:] = tail
        return 0

    lax.fori_loop(0, CHIPS, step, 0)


def spread_columns(moved, point, tap, first, count):
    _, g, ky, kx = tap
    if g < 0:
        v = point[pl.ds(first, count)]
    else:
        v = moved[3 * g + kx + 1, pl.ds(HALO + first - ky * (g + 1), count)]
    return v.reshape(count * PADDED, 128)


def kernel_grad_kernel(place, got, xt, keep, send, moved, point):
    spread(got, moved, point)
    c = place[2]
    for pair in PAIRS:
        right = jnp.concatenate([spread_columns(moved, point, tap, 0, CHIPS) for tap in pair], 1)
        part = jnp.dot(xt[...], right, preferred_element_type=F32).astype(BF16)
        for half, tap in enumerate(pair):
            cols = slice(tap[0] * 128, (tap[0] + 1) * 128)
            for yh in range(2):
                for core in range(2):
                    row = (yh * 2 + core) * 128
                    block = part[row : row + 128, half * 128 : (half + 1) * 128].reshape(8, 16, 128)

                    @pl.when(c == core)
                    def _():
                        keep[:, yh, :, cols] = block

                    @pl.when(c != core)
                    def _():
                        send[:, yh, :, cols] = block


def kernel_grad(place, got, xt):
    return pl.pallas_call(
        kernel_grad_kernel,
        out_shape=(jax.ShapeDtypeStruct((8, 2, 16, COLS), BF16),) * 2,
        in_specs=[SMEM, VMEM, VMEM],
        out_specs=(VMEM,) * 2,
        scratch_shapes=SPREAD,
        compiler_params=params(56),
        cost_estimate=CONV_COST,
    )(place, got, xt)


def feature_grad_kernel(got, wt, out, moved, point):
    spread(got, moved, point)

    def step(i, _):
        cols, rows = [], []
        for pair in PAIRS:
            for tap in pair:
                cols.append(spread_columns(moved, point, tap, 2 * i, 2))
                rows.append(wt[tap[0]])
        part = jnp.dot(
            jnp.concatenate(cols, 1), jnp.concatenate(rows, 0), preferred_element_type=F32
        )
        for sub in range(2):
            out[2 * i + sub] = part[sub * PADDED : sub * PADDED + CELLS].astype(BF16)
        return 0

    lax.fori_loop(0, CHIPS // 2, step, 0)


def feature_grad(got, wt):
    return pl.pallas_call(
        feature_grad_kernel,
        out_shape=jax.ShapeDtypeStruct((CHIPS, CELLS, K), BF16),
        in_specs=[VMEM, VMEM],
        out_specs=VMEM,
        scratch_shapes=SPREAD,
        compiler_params=params(56),
        cost_estimate=CONV_COST,
    )(got, wt)


def place_grads_kernel(place, *refs):
    blocks, point, atrous = refs[:8], refs[8], refs[9]
    z, yl = place[0], place[3]
    for d in range(4):
        for l in range(2):
            rep = 2 * lax.rem(z + 4 - d, 4) + lax.rem(yl + 2 - l, 2)
            rows = pl.ds(pl.multiple_of(rep * 16, 16), 16)
            block = blocks[2 * d + l]
            for yh in range(2):
                cols = slice(yh * 128, (yh + 1) * 128)
                for t in range(TAPS):
                    part = block[yh, :, t * 128 : (t + 1) * 128].astype(F32) * 0.125
                    if t == 0:
                        point[rows, cols] = part
                    else:
                        atrous[t - 1, rows, cols] = part


def place_grads(place, blocks):
    return pl.pallas_call(
        place_grads_kernel,
        out_shape=(
            jax.ShapeDtypeStruct((128, 256), F32),
            jax.ShapeDtypeStruct((27, 128, 256), F32),
        ),
        in_specs=[SMEM] + [VMEM] * 8,
        out_specs=(VMEM,) * 2,
        compiler_params=params(40),
    )(place, *blocks)


def join_features_kernel(got, out):
    for x in range(4):
        total = (got[x].astype(F32) + got[4 + x].astype(F32)).astype(BF16)
        for yh in range(2):
            out[:, (yh * 4 + x) * 256 : (yh * 4 + x + 1) * 256] = total[:, yh * 256 : (yh + 1) * 256]


def join_features(got):
    return pl.pallas_call(
        join_features_kernel,
        out_shape=jax.ShapeDtypeStruct((CELLS, 2048), BF16),
        in_specs=[VMEM],
        out_specs=VMEM,
        compiler_params=params(16),
    )(got)


def turn(n, d):
    return [(i, (i + d) % n) for i in range(n)]


def swap(v, axis):
    return lax.ppermute(v, axis, turn(2, 1))


def sum_everywhere(v):
    c, x, yh = (lax.axis_index(a) for a in ("c", "x", "yh"))
    beside = [(i, i ^ 1) for i in range(4)]
    across = [(i, 3 - i) for i in range(4)]
    halvings = (
        ("c", turn(2, 1), c),
        ("x", beside, (x ^ (x >> 1)) & 1),
        ("x", across, x >> 1),
        ("yh", turn(2, 1), yh),
    )
    for axis, pairs, bit in halvings:
        half = v.shape[0] // 2
        mine = lax.dynamic_slice_in_dim(v, bit * half, half, 0)
        theirs = lax.dynamic_slice_in_dim(v, (1 - bit) * half, half, 0)
        v = mine + lax.ppermute(theirs.astype(BF16), axis, pairs).astype(F32)
    for axis, pairs in (("yl", turn(2, 1)), ("z", beside), ("z", across)):
        v = v + lax.ppermute(v, axis, pairs)
    v = v.astype(BF16)
    for axis, pairs, bit in reversed(halvings):
        got = lax.ppermute(v, axis, pairs)
        v = jnp.where(bit == 0, jnp.concatenate([v, got], 0), jnp.concatenate([got, v], 0))
    return v.astype(F32)


def shards(features, atrous_weight, point_weight, proj_weight, cotangent):
    place = jnp.stack([lax.axis_index(a) for a in ("z", "x", "c", "yl")]).astype(jnp.int32)

    atrous_t = jnp.transpose(atrous_weight, (0, 2, 1))
    parts = split_weights(place, jnp.transpose(point_weight, (1, 0)), atrous_t)
    from_x = [parts[0]] + [lax.ppermute(parts[d], "x", turn(4, d)) for d in (1, 2, 3)]
    quarter = stack_columns(place, from_x)
    quarters = [quarter] + [lax.ppermute(quarter, "z", turn(4, d)) for d in (1, 2, 3)]
    blocks = quarters + [swap(v, "c") for v in quarters]
    wt = join_weights(place, blocks).reshape(TAPS, 128, K)

    x_send = split_features(features.reshape(CELLS, 2048))
    x = lax.all_to_all(x_send, ("yh", "x"), 0, 0, tiled=True)

    partial = forward(x, wt)
    got = lax.all_to_all(partial, ("yh", "x"), 0, 0, tiled=True)
    proj = proj_weight.reshape(4, 2, 128, 256).transpose(1, 0, 2, 3).reshape(1024, 256)
    projected, d_send, proj_part = middle(got, proj, cotangent.reshape(CELLS, 256))
    grad_proj = sum_everywhere(proj_part)
    grad_proj = grad_proj.reshape(2, 4, 128, 256).transpose(1, 0, 2, 3).reshape(1024, 256) * 0.125
    dpre = lax.all_to_all(d_send, ("yh", "x"), 0, 0, tiled=True)

    xt = jnp.transpose(
        jnp.pad(x, ((0, 0), (0, PADDED - CELLS), (0, 0))).reshape(CHIPS * PADDED, K)
    )
    keep, send = kernel_grad(place, dpre, xt)
    g_part = (keep.astype(F32) + swap(send, "c").astype(F32)).astype(BF16)
    g_got = lax.all_to_all(g_part.reshape(16, 16, COLS), ("z", "yl", "yh"), 0, 0, tiled=True)
    g_sum = jnp.sum(g_got.reshape(8, 2, 16, COLS).astype(F32), 0).astype(BF16)
    g_all = [g_sum]
    for d in range(4):
        for l in range(2):
            if d or l:
                pairs = [
                    (z * 2 + y, (z + d) % 4 * 2 + (y + l) % 2) for z in range(4) for y in range(2)
                ]
                g_all.append(lax.ppermute(g_sum, ("z", "yl"), pairs))
    grad_point, grad_atrous = place_grads(place, g_all)

    back = feature_grad(dpre, wt)
    back, _ = lax.optimization_barrier((back, g_sum))
    input_grad = join_features(lax.all_to_all(back, ("yh", "x"), 0, 0, tiled=True))

    return (
        projected.reshape(1, 3, WIDTH, 256),
        input_grad.reshape(1, 3, WIDTH, 2048),
        grad_point,
        grad_atrous,
        grad_proj,
    )


def solution(mesh):
    fine = Mesh(mesh.devices.reshape(4, 2, 2, 4, 2), ("z", "yl", "yh", "x", "c"))
    rep, sp = ("z", "yl"), ("yh", "x", "c")
    in_specs = (
        P(rep, sp, None, None),
        P(None, None, sp),
        P(None, sp),
        P(),
        P(rep, sp, None, None),
    )
    out_specs = (
        P(rep, sp, None, None),
        P(rep, sp, None, None),
        P(sp, None),
        P(None, sp, None),
        P(),
    )
    return jax.shard_map(shards, mesh=fine, in_specs=in_specs, out_specs=out_specs, check_vma=False)
```

time: 585 us -> 284 us (0.49)
  waiting for transfers between devices: 260 us -> 115 us
  local copies, waits for them, and re-layouts: 124 us -> 9.4 us
  matrix products: 96.9 us -> 0 us
  starting transfers between devices: 16.3 us -> 96.6 us
  Pallas kernels: 0 us -> 52.7 us
  other arithmetic: 47.6 us -> 6.38 us
  blocking collectives: 17 us -> 0 us
  between operations: 15.1 us -> 0.88 us
    psum x2 -> x0, waiting for transfers between devices: 150 us -> none  [the longest x1 94 us: shards(): lax.psum(point_part.astype(jnp.bfloat16), 'rep').astype(jnp.float32)]
    all_gather x2 -> x0, waiting for transfers between devices: 103 us -> none  [the longest x1 103 us: shards(): piece = lax.all_gather(features, 'sp', axis=1, tiled=True)]
    dot_general x36 -> x0, matrix products: 96.9 us -> none  [the longest x27 68.3 us: shards(): jnp.dot(dpre[g], w_in[t].T, preferred_element_type=jnp.float32)]
    ppermute x0 -> x29, starting transfers between devices: none -> 72.3 us  [the longest x4 27 us: sum_everywhere(): got = lax.ppermute(v, axis, pairs)]
    unnamed x107 -> x22, local copies, waits for them, and re-layouts: 75 us -> 4.2 us
    ppermute x0 -> x29, waiting for transfers between devices: none -> 69.2 us  [the longest x3 21.2 us: shards(): lax.ppermute(parts[d], 'x', turn(4, d))]
    pallas_call x0 -> x10, Pallas kernels: none -> 52.7 us  [the longest x1 21.1 us: kernel_grad(): pl.pallas_call(kernel_grad_kernel, out_shape=(jax.ShapeDtypeStruct((8, 2,...]
    all_to_all x3 -> x5, waiting for transfers between devices: 6.7 us -> 45.9 us  [the longest x1 25 us: shards(): got = lax.all_to_all(partial, ('yh', 'x'), 0, 0, tiled=True)]
  transfers between devices with their start and end apart: 7 -> 34, of which waited for: 4 -> 20; matrix products, arithmetic and copies ran while one was open for 34% -> 4% of each run, Pallas kernels for 0% -> 6%
where the time goes in v2:
time: 284 us; the launch traced here: 281 us
  waiting for transfers between devices  115 us (40%)
  starting transfers between devices  96.6 us (34%)
  Pallas kernels  52.7 us (19%)
  local copies, waits for them, and re-layouts  9.4 us (3%)
  other arithmetic  6.38 us (2%)
    ppermute x4, starting transfers between devices, sum_everywhere(): got = lax.ppermute(v, axis, pairs)  27 us
    all_to_all x1, waiting for transfers between devices, shards(): got = lax.all_to_all(partial, ('yh', 'x'), 0, 0, tiled=True)  25 us
    ppermute x3, waiting for transfers between devices, shards(): lax.ppermute(parts[d], 'x', turn(4, d))  21.2 us
    pallas_call x1, Pallas kernels, kernel_grad(): pl.pallas_call(kernel_grad_kernel, out_shape=(jax.ShapeDtypeStruct((8, 2,...  21.1 us
    all_to_all x1, waiting for transfers between devices, shards(): dpre = lax.all_to_all(d_send, ('yh', 'x'), 0, 0, tiled=True)  20.8 us
    ppermute x7, starting transfers between devices, shards(): g_all.append(lax.ppermute(g_sum, ('z', 'yl'), pairs))  16.5 us
    pallas_call x1, Pallas kernels, feature_grad(): pl.pallas_call(feature_grad_kernel, out_shape=jax.ShapeDtypeStruct((CHIPS...  12.2 us
    ppermute x5, starting transfers between devices, swap(): return lax.ppermute(v, axis, turn(2, 1))  11 us
  transfers between devices with their start and end apart: 34, of which 20 were waited for; matrix products, arithmetic and copies ran while one was open for 4% of the time, Pallas kernels for 6%

profile of v2, /device:TPU:1, one launch (start us, length us, event | category | flops | bytes accessed | tf_op | source)
XLA Modules:
  0.0 281.1 jit_solution(3551152864129255004)
XLA Ops:
  3.1 7.6 %all-to-all-start = ((bf16[8,216,512]{2,1,0:T(8,128)(2,1)}), bf16[8,216,512]{2,1,0:T(8,128)(2,1)}, u32[]{:S(2)}, u32[]{:S(2)}) async-start(bf16[8,216,512]{2,1,0:T(8,128)(2,1)} %shard_map.92), calls=%async_computation | async-start | bytes 3538944 | tf_op jit(solution)/shard_map/all_to_all | solution.py:445
  16.9 19.1 %collective-permute-done.b1 = bf16[7,16,512]{2,1,0:T(8,128)(2,1)S(1)} collective-permute-done((bf16[7,16,512]{2,1,0:T(8,128)(2,1)S(1)}, bf16[7,16,512]{2,1,0:T(8,128)(2,1)S(1)}, u32[]{:S(2)}, u32[]{:S(2)}) %collective-permute-start) | collective-permute-done | bytes 114720 | tf_op jit(solution)/shard_map/ppermute | solution.py:438
  47.3 3.8 %collective-permute-done.3.refs_1_ = bf16[4,7,16,512]{3,2,1,0:T(8,128)(2,1)S(1)} collective-permute-done((bf16[4,7,16,512]{3,2,1,0:T(8,128)(2,1)S(1)}, bf16[4,7,16,512]{3,2,1,0:T(8,128)(2,1)S(1)}, u32[]{:S(2)}, u32[]{:S(2)}) %collective-permute-start.3) | collective-permute-done | bytes 458784 | tf_op jit(solution)/shard_map/ppermute | solution.py:440
  51.2 4.2 %collective-permute-start.7 = (bf16[4,7,16,512]{3,2,1,0:T(8,128)(2,1)S(1)}, bf16[4,7,16,512]{3,2,1,0:T(8,128)(2,1)S(1)}, u32[]{:S(2)}, u32[]{:S(2)}) collective-permute-start(bf16[4,7,16,512]{3,2,1,0:T(8,128)(2,1)S(1)} %collective-permute-done.3.refs_1_), channel_id=1, source_target_pairs={{0,1},{1,0},{2,3},{3,2},{4,5},{5,4},{6,7},{7,6},{8,9},{9,8},{10,11... | collective-permute-start | bytes 1376264 | tf_op jit(solution)/shard_map/ppermute | solution.py:406
  55.4 6.5 %collective-permute-done.4.refs_2_ = bf16[4,7,16,512]{3,2,1,0:T(8,128)(2,1)S(1)} collective-permute-done((bf16[4,7,16,512]{3,2,1,0:T(8,128)(2,1)S(1)}, bf16[4,7,16,512]{3,2,1,0:T(8,128)(2,1)S(1)}, u32[]{:S(2)}, u32[]{:S(2)}) %collective-permute-start.4) | collective-permute-done | bytes 458784 | tf_op jit(solution)/shard_map/ppermute | solution.py:440
  69.7 10.4 %shard_map.96 = bf16[8,216,512]{2,1,0:T(8,128)(2,1)} custom-call(bf16[8,216,512]{2,1,0:T(8,128)(2,1)} %all-to-all-done.x, bf16[28,128,512]{2,1,0:T(8,128)(2,1)} %bitcast.23), custom_call_target="tpu_custom_call" | custom-call | flops 6341787648 | bytes 8388608 | tf_op jit(solution)/shard_map/pallas_call | solution.py:193
  80.1 4.3 %all-to-all-start.1 = ((bf16[8,216,512]{2,1,0:T(8,128)(2,1)}), bf16[8,216,512]{2,1,0:T(8,128)(2,1)S(1)}, u32[]{:S(2)}, u32[]{:S(2)}) async-start(bf16[8,216,512]{2,1,0:T(8,128)(2,1)} %shard_map.96), calls=%async_computation.1 | async-start | bytes 3538944 | tf_op jit(solution)/shard_map/all_to_all | solution.py:448
  84.4 25.0 %all-to-all-done.1.got = bf16[8,216,512]{2,1,0:T(8,128)(2,1)S(1)} async-done(((bf16[8,216,512]{2,1,0:T(8,128)(2,1)}), bf16[8,216,512]{2,1,0:T(8,128)(2,1)S(1)}, u32[]{:S(2)}, u32[]{:S(2)}) %all-to-all-start.1) | async-done | bytes 1769504 | tf_op jit(solution)/shard_map/all_to_all | solution.py:448
  111.9 4.5 %all-to-all-start.2 = ((bf16[8,216,512]{2,1,0:T(8,128)(2,1)}), bf16[8,216,512]{2,1,0:T(8,128)(2,1)}, u32[]{:S(2)}, u32[]{:S(2)}) async-start(bf16[8,216,512]{2,1,0:T(8,128)(2,1)} %copy-done.1), calls=%async_computation.2 | async-start | bytes 3538944 | tf_op jit(solution)/shard_map/all_to_all | solution.py:453
  120.5 20.8 %all-to-all-done.2.got = bf16[8,216,512]{2,1,0:T(8,128)(2,1)} async-done(((bf16[8,216,512]{2,1,0:T(8,128)(2,1)}), bf16[8,216,512]{2,1,0:T(8,128)(2,1)}, u32[]{:S(2)}, u32[]{:S(2)}) %all-to-all-start.2) | async-done | bytes 1769504 | tf_op jit(solution)/shard_map/all_to_all | solution.py:453
  141.3 21.1 %shard_map.99 = (bf16[8,2,16,3584]{3,2,1,0:T(8,128)(2,1)}, bf16[8,2,16,3584]{3,2,1,0:T(8,128)(2,1)}) custom-call(s32[4]{0:T(128)} %copy-done.6, bf16[8,216,512]{2,1,0:T(8,128)(2,1)} %all-to-all-done.2.got, bf16[512,1792]{1,0:T(8,128)(2,1)} %bitcast.34), custom_call_target="tpu_custom_call" | custom-call | flops 6341787648 | bytes 8388608 | tf_op jit(solution)/shard_map/pallas_call | solution.py:311
  163.3 3.9 %collective-permute-done.10 = bf16[8,2,16,3584]{3,2,1,0:T(8,128)(2,1)S(1)} collective-permute-done((bf16[8,2,16,3584]{3,2,1,0:T(8,128)(2,1)}, bf16[8,2,16,3584]{3,2,1,0:T(8,128)(2,1)S(1)}, u32[]{:S(2)}, u32[]{:S(2)}) %collective-permute-start.10) | collective-permute-done | bytes 1835040 | tf_op jit(solution)/shard_map/ppermute | solution.py:406
  170.5 3.7 %all-to-all-start.3 = ((bf16[16,16,3584]{2,1,0:T(8,128)(2,1)}), bf16[16,16,3584]{2,1,0:T(8,128)(2,1)S(1)}, u32[]{:S(2)}, u32[]{:S(2)}) async-start(bf16[16,16,3584]{2,1,0:T(8,128)(2,1)} %bitcast.32), calls=%async_computation.3 | async-start | bytes 3670016 | tf_op jit(solution)/shard_map/all_to_all | solution.py:460
  176.0 4.1 %collective-permute-done.19 = bf16[256,256]{1,0:T(8,128)(2,1)S(1)} collective-permute-done((bf16[256,256]{1,0:T(8,128)(2,1)S(1)}, bf16[256,256]{1,0:T(8,128)(2,1)S(1)}, u32[]{:S(2)}, u32[]{:S(2)}) %collective-permute-start.19) | collective-permute-done | bytes 131104 | tf_op jit(solution)/shard_map/ppermute | solution.py:423
  180.3 4.5 %collective-permute-done.20 = bf16[128,256]{1,0:T(8,128)(2,1)S(1)} collective-permute-done((bf16[128,256]{1,0:T(8,128)(2,1)S(1)}, bf16[128,256]{1,0:T(8,128)(2,1)S(1)}, u32[]{:S(2)}, u32[]{:S(2)}) %collective-permute-start.20) | collective-permute-done | bytes 65568 | tf_op jit(solution)/shard_map/ppermute | solution.py:423
  187.6 12.2 %shard_map.98 = bf16[8,216,512]{2,1,0:T(8,128)(2,1)} custom-call(bf16[8,216,512]{2,1,0:T(8,128)(2,1)} %all-to-all-done.2.got, bf16[28,128,512]{2,1,0:T(8,128)(2,1)} %bitcast.24), custom_call_target="tpu_custom_call" | custom-call | flops 6341787648 | bytes 8388608 | tf_op jit(solution)/shard_map/pallas_call | solution.py:342
  200.1 4.2 %all-to-all-start.4 = ((bf16[8,216,512]{2,1,0:T(8,128)(2,1)}), bf16[8,216,512]{2,1,0:T(8,128)(2,1)S(1)}, u32[]{:S(2)}, u32[]{:S(2)}) async-start(bf16[8,216,512]{2,1,0:T(8,128)(2,1)} %shard_map.98), calls=%async_computation.4 | async-start | bytes 3538944 | tf_op jit(solution)/shard_map/all_to_all | solution.py:474
  204.4 4.4 %collective-permute-done.22 = f32[64,256]{1,0:T(8,128)S(1)} collective-permute-done((f32[64,256]{1,0:T(8,128)S(1)}, f32[64,256]{1,0:T(8,128)S(1)}, u32[]{:S(2)}, u32[]{:S(2)}) %collective-permute-start.22) | collective-permute-done | bytes 65568 | tf_op jit(solution)/shard_map/ppermute | solution.py:425
  217.0 3.4 %collective-permute-start.25 = (bf16[64,256]{1,0:T(8,128)(2,1)S(1)}, bf16[64,256]{1,0:T(8,128)(2,1)S(1)}, u32[]{:S(2)}, u32[]{:S(2)}) collective-permute-start(bf16[64,256]{1,0:T(8,128)(2,1)S(1)} %add_convert_fusion.1), channel_id=1, source_target_pairs={{0,8},{8,0},{1,9},{9,1},{2,10},{10,2},{3,11},{11,3},{4,12},{12,4},... | collective-permute-start | bytes 98312 | tf_op jit(solution)/shard_map/ppermute | solution.py:428
  223.2 16.8 %collective-permute-start.26 = (bf16[128,256]{1,0:T(8,128)(2,1)S(1)}, bf16[128,256]{1,0:T(8,128)(2,1)S(1)}, u32[]{:S(2)}, u32[]{:S(2)}) collective-permute-start(bf16[128,256]{1,0:T(8,128)(2,1)S(1)} %maximum_select_fusion.3), channel_id=1, source_target_pairs={{0,6},{2,4},{4,2},{6,0},{1,7},{3,5},{5,3},{7,1},{8,14},{10,12},{12... | collective-permute-start | bytes 196616 | tf_op jit(solution)/shard_map/ppermute | solution.py:428
  242.4 3.6 %collective-permute-done.27 = bf16[256,256]{1,0:T(8,128)(2,1)S(1)} collective-permute-done((bf16[256,256]{1,0:T(8,128)(2,1)S(1)}, bf16[256,256]{1,0:T(8,128)(2,1)S(1)}, u32[]{:S(2)}, u32[]{:S(2)}) %collective-permute-start.27) | collective-permute-done | bytes 131104 | tf_op jit(solution)/shard_map/ppermute | solution.py:428
  246.0 6.2 %collective-permute-start.28 = (bf16[512,256]{1,0:T(8,128)(2,1)S(1)}, bf16[512,256]{1,0:T(8,128)(2,1)S(1)}, u32[]{:S(2)}, u32[]{:S(2)}) collective-permute-start(bf16[512,256]{1,0:T(8,128)(2,1)S(1)} %maximum_select_fusion.1), channel_id=1, source_target_pairs={{0,1},{1,0},{2,3},{3,2},{4,5},{5,4},{6,7},{7,6},{8,9},{9,8},{10,11... | collective-permute-start | bytes 786440 | tf_op jit(solution)/shard_map/ppermute | solution.py:428
  261.9 7.7 %collective-permute-start.17 = (bf16[2,16,3584]{2,1,0:T(8,128)(2,1)S(1)}, bf16[2,16,3584]{2,1,0:T(8,128)(2,1)}, u32[]{:S(2)}, u32[]{:S(2)}) collective-permute-start(bf16[2,16,3584]{2,1,0:T(8,128)(2,1)S(1)} %reduce_sum.12.refs_0_), channel_id=1, source_target_pairs={{0,112},{16,96},{32,16},{48,0},{64,48},{80,32},{96,80},{112,64},{1... | collective-permute-start | bytes 688136 | tf_op jit(solution)/shard_map/ppermute | solution.py:469
  272.2 4.7 %collective-permute-done.14.refs_4_ = bf16[2,16,3584]{2,1,0:T(8,128)(2,1)S(1)} collective-permute-done((bf16[2,16,3584]{2,1,0:T(8,128)(2,1)S(1)}, bf16[2,16,3584]{2,1,0:T(8,128)(2,1)S(1)}, u32[]{:S(2)}, u32[]{:S(2)}) %collective-permute-start.14) | collective-permute-done | bytes 229408 | tf_op jit(solution)/shard_map/ppermute | solution.py:469
  (98 shorter events, 73.4 us)
Async XLA Ops:
  3.1 66.5 %all-to-all-start = ((bf16[8,216,512]{2,1,0:T(8,128)(2,1)}), bf16[8,216,512]{2,1,0:T(8,128)(2,1)}, u32[]{:S(2)}, u32[]{:S(2)}) async-start(bf16[8,216,512]{2,1,0:T(8,128)(2,1)} %shard_map.92), calls=%async_computation | async-start | bytes 3538944 | tf_op jit(solution)/shard_map/all_to_all | solution.py:445
  11.8 24.2 %collective-permute-start = (bf16[7,16,512]{2,1,0:T(8,128)(2,1)S(1)}, bf16[7,16,512]{2,1,0:T(8,128)(2,1)S(1)}, u32[]{:S(2)}, u32[]{:S(2)}) collective-permute-start(bf16[7,16,512]{2,1,0:T(8,128)(2,1)S(1)} %get-tuple-element.18), channel_id=1, source_target_pairs={{0,2},{2,4},{4,6},{6,0},{1,3},{3,5},{5,7},{7,1},{8,10},{10,12},{12... | collective-permute-start | bytes 344072 | tf_op jit(solution)/shard_map/ppermute | solution.py:438
  13.3 24.8 %collective-permute-start.1 = (bf16[7,16,512]{2,1,0:T(8,128)(2,1)S(1)}, bf16[7,16,512]{2,1,0:T(8,128)(2,1)S(1)}, u32[]{:S(2)}, u32[]{:S(2)}) collective-permute-start(bf16[7,16,512]{2,1,0:T(8,128)(2,1)S(1)} %get-tuple-element.19), channel_id=1, source_target_pairs={{0,4},{2,6},{4,0},{6,2},{1,5},{3,7},{5,1},{7,3},{8,12},{10,14},{12... | collective-permute-start | bytes 344072 | tf_op jit(solution)/shard_map/ppermute | solution.py:438
  15.7 22.4 %collective-permute-start.2 = (bf16[7,16,512]{2,1,0:T(8,128)(2,1)S(1)}, bf16[7,16,512]{2,1,0:T(8,128)(2,1)S(1)}, u32[]{:S(2)}, u32[]{:S(2)}) collective-permute-start(bf16[7,16,512]{2,1,0:T(8,128)(2,1)S(1)} %get-tuple-element.20), channel_id=1, source_target_pairs={{0,6},{2,0},{4,2},{6,4},{1,7},{3,1},{5,3},{7,5},{8,14},{10,8},{12,... | collective-permute-start | bytes 344072 | tf_op jit(solution)/shard_map/ppermute | solution.py:438
  38.7 12.5 %collective-permute-start.3 = (bf16[4,7,16,512]{3,2,1,0:T(8,128)(2,1)S(1)}, bf16[4,7,16,512]{3,2,1,0:T(8,128)(2,1)S(1)}, u32[]{:S(2)}, u32[]{:S(2)}) collective-permute-start(bf16[4,7,16,512]{3,2,1,0:T(8,128)(2,1)S(1)} %shard_map.94.refs_0_), channel_id=1, source_target_pairs={{0,32},{32,64},{64,96},{96,0},{1,33},{33,65},{65,97},{97,1},{2,34}... | collective-permute-start | bytes 1376264 | tf_op jit(solution)/shard_map/ppermute | solution.py:440
  40.4 21.6 %collective-permute-start.4 = (bf16[4,7,16,512]{3,2,1,0:T(8,128)(2,1)S(1)}, bf16[4,7,16,512]{3,2,1,0:T(8,128)(2,1)S(1)}, u32[]{:S(2)}, u32[]{:S(2)}) collective-permute-start(bf16[4,7,16,512]{3,2,1,0:T(8,128)(2,1)S(1)} %shard_map.94.refs_0_), channel_id=1, source_target_pairs={{0,64},{32,96},{64,0},{96,32},{1,65},{33,97},{65,1},{97,33},{2,66}... | collective-permute-start | bytes 1376264 | tf_op jit(solution)/shard_map/ppermute | solution.py:440
  43.7 21.3 %collective-permute-start.5 = (bf16[4,7,16,512]{3,2,1,0:T(8,128)(2,1)S(1)}, bf16[4,7,16,512]{3,2,1,0:T(8,128)(2,1)S(1)}, u32[]{:S(2)}, u32[]{:S(2)}) collective-permute-start(bf16[4,7,16,512]{3,2,1,0:T(8,128)(2,1)S(1)} %shard_map.94.refs_0_), channel_id=1, source_target_pairs={{0,96},{32,0},{64,32},{96,64},{1,97},{33,1},{65,33},{97,65},{2,98}... | collective-permute-start | bytes 1376264 | tf_op jit(solution)/shard_map/ppermute | solution.py:440
  44.4 20.6 %collective-permute-start.6 = (bf16[4,7,16,512]{3,2,1,0:T(8,128)(2,1)S(1)}, bf16[4,7,16,512]{3,2,1,0:T(8,128)(2,1)S(1)}, u32[]{:S(2)}, u32[]{:S(2)}) collective-permute-start(bf16[4,7,16,512]{3,2,1,0:T(8,128)(2,1)S(1)} %shard_map.94.refs_0_), channel_id=1, source_target_pairs={{0,1},{1,0},{2,3},{3,2},{4,5},{5,4},{6,7},{7,6},{8,9},{9,8},{10,11... | collective-permute-start | bytes 1376264 | tf_op jit(solution)/shard_map/ppermute | solution.py:406
  51.2 13.8 %collective-permute-start.7 = (bf16[4,7,16,512]{3,2,1,0:T(8,128)(2,1)S(1)}, bf16[4,7,16,512]{3,2,1,0:T(8,128)(2,1)S(1)}, u32[]{:S(2)}, u32[]{:S(2)}) collective-permute-start(bf16[4,7,16,512]{3,2,1,0:T(8,128)(2,1)S(1)} %collective-permute-done.3.refs_1_), channel_id=1, source_target_pairs={{0,1},{1,0},{2,3},{3,2},{4,5},{5,4},{6,7},{7,6},{8,9},{9,8},{10,11... | collective-permute-start | bytes 1376264 | tf_op jit(solution)/shard_map/ppermute | solution.py:406
  80.1 29.3 %all-to-all-start.1 = ((bf16[8,216,512]{2,1,0:T(8,128)(2,1)}), bf16[8,216,512]{2,1,0:T(8,128)(2,1)S(1)}, u32[]{:S(2)}, u32[]{:S(2)}) async-start(bf16[8,216,512]{2,1,0:T(8,128)(2,1)} %shard_map.96), calls=%async_computation.1 | async-start | bytes 3538944 | tf_op jit(solution)/shard_map/all_to_all | solution.py:448
  111.9 29.4 %all-to-all-start.2 = ((bf16[8,216,512]{2,1,0:T(8,128)(2,1)}), bf16[8,216,512]{2,1,0:T(8,128)(2,1)}, u32[]{:S(2)}, u32[]{:S(2)}) async-start(bf16[8,216,512]{2,1,0:T(8,128)(2,1)} %copy-done.1), calls=%async_computation.2 | async-start | bytes 3538944 | tf_op jit(solution)/shard_map/all_to_all | solution.py:453
  163.3 11.0 %collective-permute-start.18 = (bf16[512,256]{1,0:T(8,128)(2,1)S(1)}, bf16[512,256]{1,0:T(8,128)(2,1)}, u32[]{:S(2)}, u32[]{:S(2)}) collective-permute-start(bf16[512,256]{1,0:T(8,128)(2,1)S(1)} %dynamic-slice_convert_fusion), channel_id=1, source_target_pairs={{0,1},{1,0},{2,3},{3,2},{4,5},{5,4},{6,7},{7,6},{8,9},{9,8},{10,11... | collective-permute-start | bytes 786440 | tf_op jit(solution)/shard_map/ppermute | solution.py:423
  170.5 29.3 %all-to-all-start.3 = ((bf16[16,16,3584]{2,1,0:T(8,128)(2,1)}), bf16[16,16,3584]{2,1,0:T(8,128)(2,1)S(1)}, u32[]{:S(2)}, u32[]{:S(2)}) async-start(bf16[16,16,3584]{2,1,0:T(8,128)(2,1)} %bitcast.32), calls=%async_computation.3 | async-start | bytes 3670016 | tf_op jit(solution)/shard_map/all_to_all | solution.py:460
  184.9 19.4 %collective-permute-start.21 = (bf16[64,256]{1,0:T(8,128)(2,1)S(1)}, bf16[64,256]{1,0:T(8,128)(2,1)S(1)}, u32[]{:S(2)}, u32[]{:S(2)}) collective-permute-start(bf16[64,256]{1,0:T(8,128)(2,1)S(1)} %dynamic-slice_convert_fusion.3), channel_id=1, source_target_pairs={{0,8},{8,0},{1,9},{9,1},{2,10},{10,2},{3,11},{11,3},{4,12},{12,4},... | collective-permute-start | bytes 98312 | tf_op jit(solution)/shard_map/ppermute | solution.py:423
  200.1 79.8 %all-to-all-start.4 = ((bf16[8,216,512]{2,1,0:T(8,128)(2,1)}), bf16[8,216,512]{2,1,0:T(8,128)(2,1)S(1)}, u32[]{:S(2)}, u32[]{:S(2)}) async-start(bf16[8,216,512]{2,1,0:T(8,128)(2,1)} %shard_map.98), calls=%async_computation.4 | async-start | bytes 3538944 | tf_op jit(solution)/shard_map/all_to_all | solution.py:474
  223.2 18.5 %collective-permute-start.26 = (bf16[128,256]{1,0:T(8,128)(2,1)S(1)}, bf16[128,256]{1,0:T(8,128)(2,1)S(1)}, u32[]{:S(2)}, u32[]{:S(2)}) collective-permute-start(bf16[128,256]{1,0:T(8,128)(2,1)S(1)} %maximum_select_fusion.3), channel_id=1, source_target_pairs={{0,6},{2,4},{4,2},{6,0},{1,7},{3,5},{5,3},{7,1},{8,14},{10,12},{12... | collective-permute-start | bytes 196616 | tf_op jit(solution)/shard_map/ppermute | solution.py:428
  246.0 11.3 %collective-permute-start.28 = (bf16[512,256]{1,0:T(8,128)(2,1)S(1)}, bf16[512,256]{1,0:T(8,128)(2,1)S(1)}, u32[]{:S(2)}, u32[]{:S(2)}) collective-permute-start(bf16[512,256]{1,0:T(8,128)(2,1)S(1)} %maximum_select_fusion.1), channel_id=1, source_target_pairs={{0,1},{1,0},{2,3},{3,2},{4,5},{5,4},{6,7},{7,6},{8,9},{9,8},{10,11... | collective-permute-start | bytes 786440 | tf_op jit(solution)/shard_map/ppermute | solution.py:428
  252.2 7.2 %collective-permute-start.11 = (bf16[2,16,3584]{2,1,0:T(8,128)(2,1)S(1)}, bf16[2,16,3584]{2,1,0:T(8,128)(2,1)S(1)}, u32[]{:S(2)}, u32[]{:S(2)}) collective-permute-start(bf16[2,16,3584]{2,1,0:T(8,128)(2,1)S(1)} %reduce_sum.12.refs_0_), channel_id=1, source_target_pairs={{0,16},{16,0},{32,48},{48,32},{64,80},{80,64},{96,112},{112,96},{1... | collective-permute-start | bytes 688136 | tf_op jit(solution)/shard_map/ppermute | solution.py:469
  253.7 8.2 %collective-permute-start.12 = (bf16[2,16,3584]{2,1,0:T(8,128)(2,1)S(1)}, bf16[2,16,3584]{2,1,0:T(8,128)(2,1)S(1)}, u32[]{:S(2)}, u32[]{:S(2)}) collective-permute-start(bf16[2,16,3584]{2,1,0:T(8,128)(2,1)S(1)} %reduce_sum.12.refs_0_), channel_id=1, source_target_pairs={{0,32},{16,48},{32,64},{48,80},{64,96},{80,112},{96,0},{112,16},{1... | collective-permute-start | bytes 688136 | tf_op jit(solution)/shard_map/ppermute | solution.py:469
  253.7 18.4 %collective-permute-start.13 = (bf16[2,16,3584]{2,1,0:T(8,128)(2,1)S(1)}, bf16[2,16,3584]{2,1,0:T(8,128)(2,1)S(1)}, u32[]{:S(2)}, u32[]{:S(2)}) collective-permute-start(bf16[2,16,3584]{2,1,0:T(8,128)(2,1)S(1)} %reduce_sum.12.refs_0_), channel_id=1, source_target_pairs={{0,48},{16,32},{32,80},{48,64},{64,112},{80,96},{96,16},{112,0},{1... | collective-permute-start | bytes 688136 | tf_op jit(solution)/shard_map/ppermute | solution.py:469
  254.7 22.2 %collective-permute-start.14 = (bf16[2,16,3584]{2,1,0:T(8,128)(2,1)S(1)}, bf16[2,16,3584]{2,1,0:T(8,128)(2,1)S(1)}, u32[]{:S(2)}, u32[]{:S(2)}) collective-permute-start(bf16[2,16,3584]{2,1,0:T(8,128)(2,1)S(1)} %reduce_sum.12.refs_0_), channel_id=1, source_target_pairs={{0,64},{16,80},{32,96},{48,112},{64,0},{80,16},{96,32},{112,48},{1... | collective-permute-start | bytes 688136 | tf_op jit(solution)/shard_map/ppermute | solution.py:469
  257.3 19.6 %collective-permute-start.15 = (bf16[2,16,3584]{2,1,0:T(8,128)(2,1)S(1)}, bf16[2,16,3584]{2,1,0:T(8,128)(2,1)S(1)}, u32[]{:S(2)}, u32[]{:S(2)}) collective-permute-start(bf16[2,16,3584]{2,1,0:T(8,128)(2,1)S(1)} %reduce_sum.12.refs_0_), channel_id=1, source_target_pairs={{0,80},{16,64},{32,112},{48,96},{64,16},{80,0},{96,48},{112,32},{1... | collective-permute-start | bytes 688136 | tf_op jit(solution)/shard_map/ppermute | solution.py:469
  259.4 17.5 %collective-permute-start.16 = (bf16[2,16,3584]{2,1,0:T(8,128)(2,1)S(1)}, bf16[2,16,3584]{2,1,0:T(8,128)(2,1)S(1)}, u32[]{:S(2)}, u32[]{:S(2)}) collective-permute-start(bf16[2,16,3584]{2,1,0:T(8,128)(2,1)S(1)} %reduce_sum.12.refs_0_), channel_id=1, source_target_pairs={{0,96},{16,112},{32,0},{48,16},{64,32},{80,48},{96,64},{112,80},{1... | collective-permute-start | bytes 688136 | tf_op jit(solution)/shard_map/ppermute | solution.py:469
  261.9 15.0 %collective-permute-start.17 = (bf16[2,16,3584]{2,1,0:T(8,128)(2,1)S(1)}, bf16[2,16,3584]{2,1,0:T(8,128)(2,1)}, u32[]{:S(2)}, u32[]{:S(2)}) collective-permute-start(bf16[2,16,3584]{2,1,0:T(8,128)(2,1)S(1)} %reduce_sum.12.refs_0_), channel_id=1, source_target_pairs={{0,112},{16,96},{32,16},{48,0},{64,48},{80,32},{96,80},{112,64},{1... | collective-permute-start | bytes 688136 | tf_op jit(solution)/shard_map/ppermute | solution.py:469
  (21 other events, 181.9 us)

commit v3 on v2

--- a/solution.py
+++ b/solution.py
@@ -12,6 +12,7 @@
 PADDED = 224
 WIDTH = 72
 HALO = 3
+RIDER = 32
 K = 512
 TAPS = 28
 COLS = TAPS * 128
@@ -285,42 +286,79 @@
     return v.reshape(count * PADDED, 128)
 
 
-def kernel_grad_kernel(place, got, xt, keep, send, moved, point):
+def turn_features_kernel(place, x, out, xs):
+    for j in range(CHIPS):
+        xs[j, :CELLS] = x[j]
+        xs[j, CELLS:] = jnp.zeros((PADDED - CELLS, K), BF16)
+    flat = xs[...].reshape(CHIPS * PADDED, K)
+    for yh in range(2):
+        for core in range(2):
+            lanes = slice((yh * 2 + core) * 128, (yh * 2 + core + 1) * 128)
+            away = jnp.where(place[2] == core, 0, 1)
+            for n in range(7):
+                block = flat[n * 256 : (n + 1) * 256, lanes]
+                out[2 * away + yh, :, n * 256 : (n + 1) * 256] = block.T
+
+
+def turn_features(place, x):
+    return pl.pallas_call(
+        turn_features_kernel,
+        out_shape=jax.ShapeDtypeStruct((4, 128, CHIPS * PADDED), BF16),
+        in_specs=[SMEM, VMEM],
+        out_specs=VMEM,
+        scratch_shapes=[pltpu.VMEM((CHIPS, PADDED, K), BF16)],
+        compiler_params=params(32),
+        cost_estimate=cost(0, 8 << 20),
+    )(place, x)
+
+
+def kernel_grad_kernel(got, xt, keep, send, moved, point):
     spread(got, moved, point)
-    c = place[2]
+    left = xt[...].reshape(K, CHIPS * PADDED)
     for pair in PAIRS:
         right = jnp.concatenate([spread_columns(moved, point, tap, 0, CHIPS) for tap in pair], 1)
-        part = jnp.dot(xt[...], right, preferred_element_type=F32).astype(BF16)
+        part = jnp.dot(left, right, preferred_element_type=F32).astype(BF16)
         for half, tap in enumerate(pair):
             cols = slice(tap[0] * 128, (tap[0] + 1) * 128)
+            block = part[:, half * 128 : (half + 1) * 128].reshape(2, 2, 8, 16, 128)
             for yh in range(2):
-                for core in range(2):
-                    row = (yh * 2 + core) * 128
-                    block = part[row : row + 128, half * 128 : (half + 1) * 128].reshape(8, 16, 128)
-
-                    @pl.when(c == core)
-                    def _():
-                        keep[:, yh, :, cols] = block
-
-                    @pl.when(c != core)
-                    def _():
-                        send[:, yh, :, cols] = block
-
-
-def kernel_grad(place, got, xt):
+                keep[:, yh, :, cols] = block[0, yh]
+                send[:, yh, :, cols] = block[1, yh]
+
+
+def kernel_grad(got, xt):
     return pl.pallas_call(
         kernel_grad_kernel,
         out_shape=(jax.ShapeDtypeStruct((8, 2, 16, COLS), BF16),) * 2,
-        in_specs=[SMEM, VMEM, VMEM],
+        in_specs=[VMEM, VMEM],
         out_specs=(VMEM,) * 2,
         scratch_shapes=SPREAD,
         compiler_params=params(56),
         cost_estimate=CONV_COST,
-    )(place, got, xt)
-
-
-def feature_grad_kernel(got, wt, out, moved, point):
+    )(got, xt)
+
+
+def sum_samples_kernel(got, first, second):
+    for yh, out in enumerate((first, second)):
+        total = got[yh].astype(F32)
+        for rep in range(1, 8):
+            total = total + got[2 * rep + yh].astype(F32)
+        out[...] = total.astype(BF16)
+
+
+def sum_samples(got):
+    return pl.pallas_call(
+        sum_samples_kernel,
+        out_shape=(jax.ShapeDtypeStruct((16, COLS), BF16),) * 2,
+        in_specs=[VMEM],
+        out_specs=(VMEM,) * 2,
+        compiler_params=params(24),
+    )(got)
+
+
+def feature_grad_kernel(got, wt, proj, out, moved, point):
     spread(got, moved, point)
+    rider = jnp.concatenate([proj[:RIDER], proj[RIDER:]], 1).astype(BF16)
 
     def step(i, _):
         cols, rows = [], []
@@ -331,37 +369,38 @@
         part = jnp.dot(
             jnp.concatenate(cols, 1), jnp.concatenate(rows, 0), preferred_element_type=F32
         )
+        part = part.astype(BF16)
         for sub in range(2):
-            out[2 * i + sub] = part[sub * PADDED : sub * PADDED + CELLS].astype(BF16)
+            out[2 * i + sub, :PADDED] = part[sub * PADDED : (sub + 1) * PADDED]
+            out[2 * i + sub, PADDED:] = rider
         return 0
 
     lax.fori_loop(0, CHIPS // 2, step, 0)
 
 
-def feature_grad(got, wt):
+def feature_grad(got, wt, proj):
     return pl.pallas_call(
         feature_grad_kernel,
-        out_shape=jax.ShapeDtypeStruct((CHIPS, CELLS, K), BF16),
-        in_specs=[VMEM, VMEM],
+        out_shape=jax.ShapeDtypeStruct((CHIPS, PADDED + RIDER, K), BF16),
+        in_specs=[VMEM] * 3,
         out_specs=VMEM,
         scratch_shapes=SPREAD,
         compiler_params=params(56),
         cost_estimate=CONV_COST,
-    )(got, wt)
+    )(got, wt, proj)
 
 
 def place_grads_kernel(place, *refs):
-    blocks, point, atrous = refs[:8], refs[8], refs[9]
+    point, atrous = refs[6], refs[7]
     z, yl = place[0], place[3]
     for d in range(4):
         for l in range(2):
-            rep = 2 * lax.rem(z + 4 - d, 4) + lax.rem(yl + 2 - l, 2)
+            rep = 2 * lax.rem(z + 4 - d, 4) + lax.rem(yl + l, 2)
             rows = pl.ds(pl.multiple_of(rep * 16, 16), 16)
-            block = blocks[2 * d + l]
-            for yh in range(2):
+            for yh, block in enumerate((refs[d][l], refs[4 + l][d])):
                 cols = slice(yh * 128, (yh + 1) * 128)
                 for t in range(TAPS):
-                    part = block[yh, :, t * 128 : (t + 1) * 128].astype(F32) * 0.125
+                    part = block[:, t * 128 : (t + 1) * 128].astype(F32) * 0.125
                     if t == 0:
                         point[rows, cols] = part
                     else:
@@ -375,25 +414,36 @@
             jax.ShapeDtypeStruct((128, 256), F32),
             jax.ShapeDtypeStruct((27, 128, 256), F32),
         ),
-        in_specs=[SMEM] + [VMEM] * 8,
+        in_specs=[SMEM] + [VMEM] * 6,
         out_specs=(VMEM,) * 2,
         compiler_params=params(40),
     )(place, *blocks)
 
 
-def join_features_kernel(got, out):
+def gray(x):
+    return (x ^ (x >> 1)) & 1
+
+
+def join_features_kernel(got, out, proj):
     for x in range(4):
-        total = (got[x].astype(F32) + got[4 + x].astype(F32)).astype(BF16)
+        total = (got[x, :CELLS].astype(F32) + got[4 + x, :CELLS].astype(F32)).astype(BF16)
         for yh in range(2):
             out[:, (yh * 4 + x) * 256 : (yh * 4 + x + 1) * 256] = total[:, yh * 256 : (yh + 1) * 256]
+            rider = got[yh * 4 + x, PADDED:]
+            row = gray(x) * 256 + (x >> 1) * 128 + yh * 64
+            proj[row : row + RIDER] = rider[:, :256]
+            proj[row + RIDER : row + 2 * RIDER] = rider[:, 256:]
 
 
 def join_features(got):
     return pl.pallas_call(
         join_features_kernel,
-        out_shape=jax.ShapeDtypeStruct((CELLS, 2048), BF16),
+        out_shape=(
+            jax.ShapeDtypeStruct((CELLS, 2048), BF16),
+            jax.ShapeDtypeStruct((512, 256), BF16),
+        ),
         in_specs=[VMEM],
-        out_specs=VMEM,
+        out_specs=(VMEM,) * 2,
         compiler_params=params(16),
     )(got)
 
@@ -406,28 +456,15 @@
     return lax.ppermute(v, axis, turn(2, 1))
 
 
-def sum_everywhere(v):
-    c, x, yh = (lax.axis_index(a) for a in ("c", "x", "yh"))
-    beside = [(i, i ^ 1) for i in range(4)]
-    across = [(i, 3 - i) for i in range(4)]
-    halvings = (
-        ("c", turn(2, 1), c),
-        ("x", beside, (x ^ (x >> 1)) & 1),
-        ("x", across, x >> 1),
-        ("yh", turn(2, 1), yh),
-    )
-    for axis, pairs, bit in halvings:
-        half = v.shape[0] // 2
-        mine = lax.dynamic_slice_in_dim(v, bit * half, half, 0)
-        theirs = lax.dynamic_slice_in_dim(v, (1 - bit) * half, half, 0)
-        v = mine + lax.ppermute(theirs.astype(BF16), axis, pairs).astype(F32)
-    for axis, pairs in (("yl", turn(2, 1)), ("z", beside), ("z", across)):
-        v = v + lax.ppermute(v, axis, pairs)
-    v = v.astype(BF16)
-    for axis, pairs, bit in reversed(halvings):
-        got = lax.ppermute(v, axis, pairs)
-        v = jnp.where(bit == 0, jnp.concatenate([v, got], 0), jnp.concatenate([got, v], 0))
-    return v.astype(F32)
+BESIDE = [(i, i ^ 1) for i in range(4)]
+ACROSS = [(i, 3 - i) for i in range(4)]
+
+
+def halved(v, axis, pairs, bit):
+    half = v.shape[0] // 2
+    mine = lax.dynamic_slice_in_dim(v, bit * half, half, 0)
+    theirs = lax.dynamic_slice_in_dim(v, (1 - bit) * half, half, 0)
+    return mine + lax.ppermute(theirs.astype(BF16), axis, pairs).astype(F32)
 
 
 def shards(features, atrous_weight, point_weight, proj_weight, cotangent):
@@ -442,36 +479,45 @@
     wt = join_weights(place, blocks).reshape(TAPS, 128, K)
 
     x_send = split_features(features.reshape(CELLS, 2048))
+    x_send, quarter = lax.optimization_barrier((x_send, quarter))
     x = lax.all_to_all(x_send, ("yh", "x"), 0, 0, tiled=True)
 
     partial = forward(x, wt)
     got = lax.all_to_all(partial, ("yh", "x"), 0, 0, tiled=True)
     proj = proj_weight.reshape(4, 2, 128, 256).transpose(1, 0, 2, 3).reshape(1024, 256)
     projected, d_send, proj_part = middle(got, proj, cotangent.reshape(CELLS, 256))
-    grad_proj = sum_everywhere(proj_part)
-    grad_proj = grad_proj.reshape(2, 4, 128, 256).transpose(1, 0, 2, 3).reshape(1024, 256) * 0.125
     dpre = lax.all_to_all(d_send, ("yh", "x"), 0, 0, tiled=True)
-
-    xt = jnp.transpose(
-        jnp.pad(x, ((0, 0), (0, PADDED - CELLS), (0, 0))).reshape(CHIPS * PADDED, K)
-    )
-    keep, send = kernel_grad(place, dpre, xt)
+    xt = turn_features(place, x)
+
+    core, column, side = (lax.axis_index(a) for a in ("c", "x", "yh"))
+    share = halved(proj_part, "c", turn(2, 1), core)
+    share = halved(share, "x", BESIDE, gray(column))
+    share = halved(share, "x", ACROSS, column >> 1)
+    dpre, share = lax.optimization_barrier((dpre, share))
+
+    keep, send = kernel_grad(dpre, xt)
     g_part = (keep.astype(F32) + swap(send, "c").astype(F32)).astype(BF16)
     g_got = lax.all_to_all(g_part.reshape(16, 16, COLS), ("z", "yl", "yh"), 0, 0, tiled=True)
-    g_sum = jnp.sum(g_got.reshape(8, 2, 16, COLS).astype(F32), 0).astype(BF16)
-    g_all = [g_sum]
-    for d in range(4):
-        for l in range(2):
-            if d or l:
-                pairs = [
-                    (z * 2 + y, (z + d) % 4 * 2 + (y + l) % 2) for z in range(4) for y in range(2)
-                ]
-                g_all.append(lax.ppermute(g_sum, ("z", "yl"), pairs))
-    grad_point, grad_atrous = place_grads(place, g_all)
-
-    back = feature_grad(dpre, wt)
-    back, _ = lax.optimization_barrier((back, g_sum))
-    input_grad = join_features(lax.all_to_all(back, ("yh", "x"), 0, 0, tiled=True))
+
+    share = halved(share, "yh", turn(2, 1), side)
+    share = share + swap(share, "yl")
+    share = share + lax.ppermute(share, "z", BESIDE)
+    share = share + lax.ppermute(share, "z", ACROSS)
+    back = feature_grad(dpre, wt, share)
+
+    first, second = sum_samples(g_got)
+    back, first, second = lax.optimization_barrier((back, first, second))
+    pair = jnp.stack([first, swap(first, "yl")])
+    four = jnp.stack([second] + [lax.ppermute(second, "z", turn(4, d)) for d in (1, 2, 3)])
+    pairs = [pair] + [lax.ppermute(pair, "z", turn(4, d)) for d in (1, 2, 3)]
+    grad_point, grad_atrous = place_grads(place, pairs + [four, swap(four, "yl")])
+
+    b_got = lax.all_to_all(back, ("yh", "x"), 0, 0, tiled=True)
+    input_grad, half = join_features(b_got)
+    other = swap(half, "c")
+    grad_proj = jnp.where(core == 0, jnp.stack([half, other]), jnp.stack([other, half]))
+    grad_proj = grad_proj.astype(F32).reshape(2, 4, 128, 256).transpose(1, 0, 2, 3)
+    grad_proj = grad_proj.reshape(1024, 256) * 0.125
 
     return (
         projected.reshape(1, 3, WIDTH, 256),

time: 284 us -> 261 us (0.919)
  starting transfers between devices: 96.6 us -> 72.3 us
  waiting for transfers between devices: 115 us -> 128 us
  Pallas kernels: 52.7 us -> 44.2 us
    ppermute x18 -> x12, starting transfers between devices: 50.4 us -> 19 us  [the longest x4 8.56 us: halved(): return mine + lax.ppermute(theirs.astype(BF16), axis, pairs).astype(F32)]
    ppermute x18 -> x12, waiting for transfers between devices: 31.7 us -> 60.1 us  [the longest x4 40.3 us: halved(): return mine + lax.ppermute(theirs.astype(BF16), axis, pairs).astype(F32)]
    all_to_all x1, waiting for transfers between devices: 20.8 us -> 0.01 us  [shards(): dpre = lax.all_to_all(d_send, ('yh', 'x'), 0, 0, tiled=True)]
    all_to_all x1, waiting for transfers between devices: 0.01 us -> 19.7 us  [shards(): b_got = lax.all_to_all(back, ('yh', 'x'), 0, 0, tiled=True)]
    ppermute x3, waiting for transfers between devices: 21.2 us -> 2.51 us  [shards(): lax.ppermute(parts[d], 'x', turn(4, d))]
    pallas_call x1, Pallas kernels: 21.1 us -> 11.6 us  [kernel_grad(): pl.pallas_call(kernel_grad_kernel, out_shape=(jax.ShapeDtypeStruct((8, 2,...]
    ppermute x5 -> x9, starting transfers between devices: 11 us -> 15.9 us  [swap(): return lax.ppermute(v, axis, turn(2, 1))]
    unnamed x22 -> x20, local copies, waits for them, and re-layouts: 4.2 us -> 7.78 us
  transfers between devices with their start and end apart: 34 -> 32, of which waited for: 20 -> 20; matrix products, arithmetic and copies ran while one was open for 4% -> 1% of each run, Pallas kernels for 6% -> 7%
where the time goes in v3:
time: 261 us; the launch traced here: 260 us
  waiting for transfers between devices  128 us (49%)
  starting transfers between devices  72.3 us (28%)
  Pallas kernels  44.2 us (17%)
  local copies, waits for them, and re-layouts  8.94 us (3%)
  other arithmetic  6.23 us (2%)
    ppermute x4, waiting for transfers between devices, halved(): return mine + lax.ppermute(theirs.astype(BF16), axis, pairs).astype(F32)  40.3 us
    all_to_all x1, waiting for transfers between devices, shards(): got = lax.all_to_all(partial, ('yh', 'x'), 0, 0, tiled=True)  25 us
    all_to_all x1, waiting for transfers between devices, shards(): b_got = lax.all_to_all(back, ('yh', 'x'), 0, 0, tiled=True)  19.7 us
    ppermute x9, starting transfers between devices, swap(): return lax.ppermute(v, axis, turn(2, 1))  15.9 us
    pallas_call x1, Pallas kernels, feature_grad(): pl.pallas_call(feature_grad_kernel, out_shape=jax.ShapeDtypeStruct((CHIPS...  12.3 us
    pallas_call x1, Pallas kernels, kernel_grad(): pl.pallas_call(kernel_grad_kernel, out_shape=(jax.ShapeDtypeStruct((8, 2,...  11.6 us
    ppermute x3, waiting for transfers between devices, shards(): lax.ppermute(quarter, 'z', turn(4, d))  11.4 us
    pallas_call x1, Pallas kernels, forward(): pl.pallas_call(forward_kernel, out_shape=jax.ShapeDtypeStruct((CHIPS, CEL...  10.4 us
  transfers between devices with their start and end apart: 32, of which 20 were waited for; matrix products, arithmetic and copies ran while one was open for 1% of the time, Pallas kernels for 7%

profile of v3, /device:TPU:1, one launch (start us, length us, event | category | flops | bytes accessed | tf_op | source)
XLA Modules:
  0.0 260.2 jit_solution(11740991424295737394)
XLA Ops:
  14.1 6.3 %all-to-all-start = ((bf16[8,216,512]{2,1,0:T(8,128)(2,1)}), bf16[8,216,512]{2,1,0:T(8,128)(2,1)S(1)}, u32[]{:S(2)}, u32[]{:S(2)}) async-start(bf16[8,216,512]{2,1,0:T(8,128)(2,1)} %shard_map.92), calls=%async_computation | async-start | bytes 3538944 | tf_op jit(solution)/shard_map/all_to_all | solution.py:483
  22.0 3.3 %collective-permute-start.4 = (bf16[4,7,16,512]{3,2,1,0:T(8,128)(2,1)S(1)}, bf16[4,7,16,512]{3,2,1,0:T(8,128)(2,1)S(1)}, u32[]{:S(2)}, u32[]{:S(2)}) collective-permute-start(bf16[4,7,16,512]{3,2,1,0:T(8,128)(2,1)S(1)} %shard_map.94.refs_0_), channel_id=1, source_target_pairs={{0,64},{32,96},{64,0},{96,32},{1,65},{33,97},{65,1},{97,33},{2,66}... | collective-permute-start | bytes 1376264 | tf_op jit(solution)/shard_map/ppermute | solution.py:477
  28.7 4.4 %collective-permute-done.3.refs_1_ = bf16[4,7,16,512]{3,2,1,0:T(8,128)(2,1)S(1)} collective-permute-done((bf16[4,7,16,512]{3,2,1,0:T(8,128)(2,1)S(1)}, bf16[4,7,16,512]{3,2,1,0:T(8,128)(2,1)S(1)}, u32[]{:S(2)}, u32[]{:S(2)}) %collective-permute-start.3) | collective-permute-done | bytes 458784 | tf_op jit(solution)/shard_map/ppermute | solution.py:477
  33.1 3.7 %collective-permute-start.7 = (bf16[4,7,16,512]{3,2,1,0:T(8,128)(2,1)S(1)}, bf16[4,7,16,512]{3,2,1,0:T(8,128)(2,1)S(1)}, u32[]{:S(2)}, u32[]{:S(2)}) collective-permute-start(bf16[4,7,16,512]{3,2,1,0:T(8,128)(2,1)S(1)} %collective-permute-done.3.refs_1_), channel_id=1, source_target_pairs={{0,1},{1,0},{2,3},{3,2},{4,5},{5,4},{6,7},{7,6},{8,9},{9,8},{10,11... | collective-permute-start | bytes 1376264 | tf_op jit(solution)/shard_map/ppermute | solution.py:456
  36.8 7.0 %collective-permute-done.4.refs_2_ = bf16[4,7,16,512]{3,2,1,0:T(8,128)(2,1)S(1)} collective-permute-done((bf16[4,7,16,512]{3,2,1,0:T(8,128)(2,1)S(1)}, bf16[4,7,16,512]{3,2,1,0:T(8,128)(2,1)S(1)}, u32[]{:S(2)}, u32[]{:S(2)}) %collective-permute-start.4) | collective-permute-done | bytes 458784 | tf_op jit(solution)/shard_map/ppermute | solution.py:477
  52.5 10.4 %shard_map.96 = bf16[8,216,512]{2,1,0:T(8,128)(2,1)} custom-call(bf16[8,216,512]{2,1,0:T(8,128)(2,1)} %copy-done, bf16[28,128,512]{2,1,0:T(8,128)(2,1)} %bitcast.27), custom_call_target="tpu_custom_call" | custom-call | flops 6341787648 | bytes 8388608 | tf_op jit(solution)/shard_map/pallas_call | solution.py:194
  63.0 6.8 %all-to-all-start.1 = ((bf16[8,216,512]{2,1,0:T(8,128)(2,1)}), bf16[8,216,512]{2,1,0:T(8,128)(2,1)S(1)}, u32[]{:S(2)}, u32[]{:S(2)}) async-start(bf16[8,216,512]{2,1,0:T(8,128)(2,1)} %shard_map.96), calls=%async_computation.1 | async-start | bytes 3538944 | tf_op jit(solution)/shard_map/all_to_all | solution.py:486
  69.8 25.0 %all-to-all-done.1.got = bf16[8,216,512]{2,1,0:T(8,128)(2,1)S(1)} async-done(((bf16[8,216,512]{2,1,0:T(8,128)(2,1)}), bf16[8,216,512]{2,1,0:T(8,128)(2,1)S(1)}, u32[]{:S(2)}, u32[]{:S(2)}) %all-to-all-start.1) | async-done | bytes 1769504 | tf_op jit(solution)/shard_map/all_to_all | solution.py:486
  97.3 4.3 %all-to-all-start.2 = ((bf16[8,216,512]{2,1,0:T(8,128)(2,1)}), bf16[8,216,512]{2,1,0:T(8,128)(2,1)}, u32[]{:S(2)}, u32[]{:S(2)}) async-start(bf16[8,216,512]{2,1,0:T(8,128)(2,1)} %copy-done.4), calls=%async_computation.2 | async-start | bytes 3538944 | tf_op jit(solution)/shard_map/all_to_all | solution.py:489
  107.7 16.4 %collective-permute-done.11 = bf16[256,256]{1,0:T(8,128)(2,1)S(1)} collective-permute-done((bf16[256,256]{1,0:T(8,128)(2,1)S(1)}, bf16[256,256]{1,0:T(8,128)(2,1)S(1)}, u32[]{:S(2)}, u32[]{:S(2)}) %collective-permute-start.11) | collective-permute-done | bytes 131104 | tf_op jit(solution)/shard_map/ppermute | solution.py:467
  128.6 11.6 %shard_map.100 = (bf16[8,2,16,3584]{3,2,1,0:T(8,128)(2,1)}, bf16[8,2,16,3584]{3,2,1,0:T(8,128)(2,1)}) custom-call(bf16[8,216,512]{2,1,0:T(8,128)(2,1)} %all-to-all-done.2.got, bf16[4,128,1792]{2,1,0:T(8,128)(2,1)} %copy-done.3), custom_call_target="tpu_custom_call" | custom-call | flops 6341787648 | bytes 8388608 | tf_op jit(solution)/shard_map/pallas_call | solution.py:330
  140.1 3.7 %collective-permute-start.17 = (bf16[8,2,16,3584]{3,2,1,0:T(8,128)(2,1)}, bf16[8,2,16,3584]{3,2,1,0:T(8,128)(2,1)S(1)}, u32[]{:S(2)}, u32[]{:S(2)}) collective-permute-start(bf16[8,2,16,3584]{3,2,1,0:T(8,128)(2,1)} %get-tuple-element.37), channel_id=1, source_target_pairs={{0,1},{1,0},{2,3},{3,2},{4,5},{5,4},{6,7},{7,6},{8,9},{9,8},{10,11... | collective-permute-start | bytes 5505032 | tf_op jit(solution)/shard_map/ppermute | solution.py:456
  143.8 3.6 %collective-permute-done.17 = bf16[8,2,16,3584]{3,2,1,0:T(8,128)(2,1)S(1)} collective-permute-done((bf16[8,2,16,3584]{3,2,1,0:T(8,128)(2,1)}, bf16[8,2,16,3584]{3,2,1,0:T(8,128)(2,1)S(1)}, u32[]{:S(2)}, u32[]{:S(2)}) %collective-permute-start.17) | collective-permute-done | bytes 1835040 | tf_op jit(solution)/shard_map/ppermute | solution.py:456
  147.4 3.3 %add_convert_fusion = bf16[8,2,16,3584]{3,2,1,0:T(8,128)(2,1)} fusion(bf16[8,2,16,3584]{3,2,1,0:T(8,128)(2,1)S(1)} %collective-permute-done.17, bf16[8,2,16,3584]{3,2,1,0:T(8,128)(2,1)} %get-tuple-element.36), kind=kLoop, calls=%fused_computation | loop fusion | flops 3670016 | bytes 5505024 | tf_op jit(solution)/shard_map/convert_element_type | solution.py:499
  150.8 5.1 %all-to-all-start.3 = ((bf16[16,16,3584]{2,1,0:T(8,128)(2,1)}), bf16[16,16,3584]{2,1,0:T(8,128)(2,1)S(1)}, u32[]{:S(2)}, u32[]{:S(2)}) async-start(bf16[16,16,3584]{2,1,0:T(8,128)(2,1)} %bitcast.37), calls=%async_computation.3 | async-start | bytes 3670016 | tf_op jit(solution)/shard_map/all_to_all | solution.py:500
  155.9 2.9 %collective-permute-start.13 = (bf16[64,256]{1,0:T(8,128)(2,1)S(1)}, bf16[64,256]{1,0:T(8,128)(2,1)S(1)}, u32[]{:S(2)}, u32[]{:S(2)}) collective-permute-start(bf16[64,256]{1,0:T(8,128)(2,1)S(1)} %dynamic-slice_convert_fusion.3), channel_id=1, source_target_pairs={{0,8},{8,0},{1,9},{9,1},{2,10},{10,2},{3,11},{11,3},{4,12},{12,4},... | collective-permute-start | bytes 98312 | tf_op jit(solution)/shard_map/ppermute | solution.py:467
  158.9 22.5 %collective-permute-done.13 = bf16[64,256]{1,0:T(8,128)(2,1)S(1)} collective-permute-done((bf16[64,256]{1,0:T(8,128)(2,1)S(1)}, bf16[64,256]{1,0:T(8,128)(2,1)S(1)}, u32[]{:S(2)}, u32[]{:S(2)}) %collective-permute-start.13) | collective-permute-done | bytes 32800 | tf_op jit(solution)/shard_map/ppermute | solution.py:467
  181.4 3.1 %collective-permute-done.14 = f32[64,256]{1,0:T(8,128)S(1)} collective-permute-done((f32[64,256]{1,0:T(8,128)S(1)}, f32[64,256]{1,0:T(8,128)S(1)}, u32[]{:S(2)}, u32[]{:S(2)}) %collective-permute-start.14) | collective-permute-done | bytes 65568 | tf_op jit(solution)/shard_map/ppermute | solution.py:456
  192.8 12.3 %shard_map.98 = bf16[8,256,512]{2,1,0:T(8,128)(2,1)} custom-call(bf16[8,216,512]{2,1,0:T(8,128)(2,1)} %all-to-all-done.2.got, bf16[28,128,512]{2,1,0:T(8,128)(2,1)} %bitcast.28, f32[64,256]{1,0:T(8,128)} %add.62.proj), custom_call_target="tpu_custom_call" | custom-call | flops 6341787648 | bytes 8388608 | tf_op jit(solution)/shard_map/pallas_call | solution.py:382
  205.4 3.6 %all-to-all-start.4 = ((bf16[8,256,512]{2,1,0:T(8,128)(2,1)}), bf16[8,256,512]{2,1,0:T(8,128)(2,1)S(1)}, u32[]{:S(2)}, u32[]{:S(2)}) async-start(bf16[8,256,512]{2,1,0:T(8,128)(2,1)} %shard_map.98), calls=%async_computation.4 | async-start | bytes 4194304 | tf_op jit(solution)/shard_map/all_to_all | solution.py:515
  217.7 19.7 %all-to-all-done.4.got = bf16[8,256,512]{2,1,0:T(8,128)(2,1)S(1)} async-done(((bf16[8,256,512]{2,1,0:T(8,128)(2,1)}), bf16[8,256,512]{2,1,0:T(8,128)(2,1)S(1)}, u32[]{:S(2)}, u32[]{:S(2)}) %all-to-all-start.4) | async-done | bytes 2097184 | tf_op jit(solution)/shard_map/all_to_all | solution.py:515
  242.2 3.5 %collective-permute-start.20 = (bf16[2,16,3584]{2,1,0:T(8,128)(2,1)S(1)}, bf16[2,16,3584]{2,1,0:T(8,128)(2,1)S(1)}, u32[]{:S(2)}, u32[]{:S(2)}) collective-permute-start(bf16[2,16,3584]{2,1,0:T(8,128)(2,1)S(1)} %pad_maximum_fusion.1.refs_0_), channel_id=1, source_target_pairs={{0,64},{32,96},{64,0},{96,32},{1,65},{33,97},{65,1},{97,33},{2,66}... | collective-permute-start | bytes 688136 | tf_op jit(solution)/shard_map/ppermute | solution.py:512
  245.9 4.7 %collective-permute-done.19.refs_1_ = bf16[2,16,3584]{2,1,0:T(8,128)(2,1)S(1)} collective-permute-done((bf16[2,16,3584]{2,1,0:T(8,128)(2,1)S(1)}, bf16[2,16,3584]{2,1,0:T(8,128)(2,1)S(1)}, u32[]{:S(2)}, u32[]{:S(2)}) %collective-permute-start.19) | collective-permute-done | bytes 229408 | tf_op jit(solution)/shard_map/ppermute | solution.py:512
  250.6 5.7 %collective-permute-done.20.refs_2_ = bf16[2,16,3584]{2,1,0:T(8,128)(2,1)S(1)} collective-permute-done((bf16[2,16,3584]{2,1,0:T(8,128)(2,1)S(1)}, bf16[2,16,3584]{2,1,0:T(8,128)(2,1)S(1)}, u32[]{:S(2)}, u32[]{:S(2)}) %collective-permute-start.20) | collective-permute-done | bytes 229408 | tf_op jit(solution)/shard_map/ppermute | solution.py:512
  (90 shorter events, 66.3 us)
Async XLA Ops:
  3.9 7.1 %collective-permute-start = (bf16[7,16,512]{2,1,0:T(8,128)(2,1)S(1)}, bf16[7,16,512]{2,1,0:T(8,128)(2,1)S(1)}, u32[]{:S(2)}, u32[]{:S(2)}) collective-permute-start(bf16[7,16,512]{2,1,0:T(8,128)(2,1)S(1)} %get-tuple-element.27), channel_id=1, source_target_pairs={{0,2},{2,4},{4,6},{6,0},{1,3},{3,5},{5,7},{7,1},{8,10},{10,12},{12... | collective-permute-start | bytes 344072 | tf_op jit(solution)/shard_map/ppermute | solution.py:475
  6.1 7.5 %collective-permute-start.1 = (bf16[7,16,512]{2,1,0:T(8,128)(2,1)S(1)}, bf16[7,16,512]{2,1,0:T(8,128)(2,1)S(1)}, u32[]{:S(2)}, u32[]{:S(2)}) collective-permute-start(bf16[7,16,512]{2,1,0:T(8,128)(2,1)S(1)} %get-tuple-element.28), channel_id=1, source_target_pairs={{0,4},{2,6},{4,0},{6,2},{1,5},{3,7},{5,1},{7,3},{8,12},{10,14},{12... | collective-permute-start | bytes 344072 | tf_op jit(solution)/shard_map/ppermute | solution.py:475
  14.1 37.2 %all-to-all-start = ((bf16[8,216,512]{2,1,0:T(8,128)(2,1)}), bf16[8,216,512]{2,1,0:T(8,128)(2,1)S(1)}, u32[]{:S(2)}, u32[]{:S(2)}) async-start(bf16[8,216,512]{2,1,0:T(8,128)(2,1)} %shard_map.92), calls=%async_computation | async-start | bytes 3538944 | tf_op jit(solution)/shard_map/all_to_all | solution.py:483
  20.4 12.7 %collective-permute-start.3 = (bf16[4,7,16,512]{3,2,1,0:T(8,128)(2,1)S(1)}, bf16[4,7,16,512]{3,2,1,0:T(8,128)(2,1)S(1)}, u32[]{:S(2)}, u32[]{:S(2)}) collective-permute-start(bf16[4,7,16,512]{3,2,1,0:T(8,128)(2,1)S(1)} %shard_map.94.refs_0_), channel_id=1, source_target_pairs={{0,32},{32,64},{64,96},{96,0},{1,33},{33,65},{65,97},{97,1},{2,34}... | collective-permute-start | bytes 1376264 | tf_op jit(solution)/shard_map/ppermute | solution.py:477
  22.0 21.8 %collective-permute-start.4 = (bf16[4,7,16,512]{3,2,1,0:T(8,128)(2,1)S(1)}, bf16[4,7,16,512]{3,2,1,0:T(8,128)(2,1)S(1)}, u32[]{:S(2)}, u32[]{:S(2)}) collective-permute-start(bf16[4,7,16,512]{3,2,1,0:T(8,128)(2,1)S(1)} %shard_map.94.refs_0_), channel_id=1, source_target_pairs={{0,64},{32,96},{64,0},{96,32},{1,65},{33,97},{65,1},{97,33},{2,66}... | collective-permute-start | bytes 1376264 | tf_op jit(solution)/shard_map/ppermute | solution.py:477
  25.3 21.3 %collective-permute-start.5 = (bf16[4,7,16,512]{3,2,1,0:T(8,128)(2,1)S(1)}, bf16[4,7,16,512]{3,2,1,0:T(8,128)(2,1)S(1)}, u32[]{:S(2)}, u32[]{:S(2)}) collective-permute-start(bf16[4,7,16,512]{3,2,1,0:T(8,128)(2,1)S(1)} %shard_map.94.refs_0_), channel_id=1, source_target_pairs={{0,96},{32,0},{64,32},{96,64},{1,97},{33,1},{65,33},{97,65},{2,98}... | collective-permute-start | bytes 1376264 | tf_op jit(solution)/shard_map/ppermute | solution.py:477
  26.0 20.6 %collective-permute-start.6 = (bf16[4,7,16,512]{3,2,1,0:T(8,128)(2,1)S(1)}, bf16[4,7,16,512]{3,2,1,0:T(8,128)(2,1)S(1)}, u32[]{:S(2)}, u32[]{:S(2)}) collective-permute-start(bf16[4,7,16,512]{3,2,1,0:T(8,128)(2,1)S(1)} %shard_map.94.refs_0_), channel_id=1, source_target_pairs={{0,1},{1,0},{2,3},{3,2},{4,5},{5,4},{6,7},{7,6},{8,9},{9,8},{10,11... | collective-permute-start | bytes 1376264 | tf_op jit(solution)/shard_map/ppermute | solution.py:456
  33.1 13.5 %collective-permute-start.7 = (bf16[4,7,16,512]{3,2,1,0:T(8,128)(2,1)S(1)}, bf16[4,7,16,512]{3,2,1,0:T(8,128)(2,1)S(1)}, u32[]{:S(2)}, u32[]{:S(2)}) collective-permute-start(bf16[4,7,16,512]{3,2,1,0:T(8,128)(2,1)S(1)} %collective-permute-done.3.refs_1_), channel_id=1, source_target_pairs={{0,1},{1,0},{2,3},{3,2},{4,5},{5,4},{6,7},{7,6},{8,9},{9,8},{10,11... | collective-permute-start | bytes 1376264 | tf_op jit(solution)/shard_map/ppermute | solution.py:456
  63.0 31.9 %all-to-all-start.1 = ((bf16[8,216,512]{2,1,0:T(8,128)(2,1)}), bf16[8,216,512]{2,1,0:T(8,128)(2,1)S(1)}, u32[]{:S(2)}, u32[]{:S(2)}) async-start(bf16[8,216,512]{2,1,0:T(8,128)(2,1)} %shard_map.96), calls=%async_computation.1 | async-start | bytes 3538944 | tf_op jit(solution)/shard_map/all_to_all | solution.py:486
  97.3 31.2 %all-to-all-start.2 = ((bf16[8,216,512]{2,1,0:T(8,128)(2,1)}), bf16[8,216,512]{2,1,0:T(8,128)(2,1)}, u32[]{:S(2)}, u32[]{:S(2)}) async-start(bf16[8,216,512]{2,1,0:T(8,128)(2,1)} %copy-done.4), calls=%async_computation.2 | async-start | bytes 3538944 | tf_op jit(solution)/shard_map/all_to_all | solution.py:489
  105.7 18.4 %collective-permute-start.11 = (bf16[256,256]{1,0:T(8,128)(2,1)S(1)}, bf16[256,256]{1,0:T(8,128)(2,1)S(1)}, u32[]{:S(2)}, u32[]{:S(2)}) collective-permute-start(bf16[256,256]{1,0:T(8,128)(2,1)S(1)} %dynamic-slice_convert_fusion.1), channel_id=1, source_target_pairs={{0,2},{2,0},{4,6},{6,4},{1,3},{3,1},{5,7},{7,5},{8,10},{10,8},{12,... | collective-permute-start | bytes 393224 | tf_op jit(solution)/shard_map/ppermute | solution.py:467
  140.1 7.3 %collective-permute-start.17 = (bf16[8,2,16,3584]{3,2,1,0:T(8,128)(2,1)}, bf16[8,2,16,3584]{3,2,1,0:T(8,128)(2,1)S(1)}, u32[]{:S(2)}, u32[]{:S(2)}) collective-permute-start(bf16[8,2,16,3584]{3,2,1,0:T(8,128)(2,1)} %get-tuple-element.37), channel_id=1, source_target_pairs={{0,1},{1,0},{2,3},{3,2},{4,5},{5,4},{6,7},{7,6},{8,9},{9,8},{10,11... | collective-permute-start | bytes 5505032 | tf_op jit(solution)/shard_map/ppermute | solution.py:456
  150.8 54.4 %all-to-all-start.3 = ((bf16[16,16,3584]{2,1,0:T(8,128)(2,1)}), bf16[16,16,3584]{2,1,0:T(8,128)(2,1)S(1)}, u32[]{:S(2)}, u32[]{:S(2)}) async-start(bf16[16,16,3584]{2,1,0:T(8,128)(2,1)} %bitcast.37), calls=%async_computation.3 | async-start | bytes 3670016 | tf_op jit(solution)/shard_map/all_to_all | solution.py:500
  155.9 25.4 %collective-permute-start.13 = (bf16[64,256]{1,0:T(8,128)(2,1)S(1)}, bf16[64,256]{1,0:T(8,128)(2,1)S(1)}, u32[]{:S(2)}, u32[]{:S(2)}) collective-permute-start(bf16[64,256]{1,0:T(8,128)(2,1)S(1)} %dynamic-slice_convert_fusion.3), channel_id=1, source_target_pairs={{0,8},{8,0},{1,9},{9,1},{2,10},{10,2},{3,11},{11,3},{4,12},{12,4},... | collective-permute-start | bytes 98312 | tf_op jit(solution)/shard_map/ppermute | solution.py:467
  205.4 32.0 %all-to-all-start.4 = ((bf16[8,256,512]{2,1,0:T(8,128)(2,1)}), bf16[8,256,512]{2,1,0:T(8,128)(2,1)S(1)}, u32[]{:S(2)}, u32[]{:S(2)}) async-start(bf16[8,256,512]{2,1,0:T(8,128)(2,1)} %shard_map.98), calls=%async_computation.4 | async-start | bytes 4194304 | tf_op jit(solution)/shard_map/all_to_all | solution.py:515
  209.0 5.3 %collective-permute-start.24 = (bf16[16,3584]{1,0:T(8,128)(2,1)S(1)}, bf16[16,3584]{1,0:T(8,128)(2,1)S(1)}, u32[]{:S(2)}, u32[]{:S(2)}) collective-permute-start(bf16[16,3584]{1,0:T(8,128)(2,1)S(1)} %get-tuple-element.43), channel_id=1, source_target_pairs={{0,96},{32,0},{64,32},{96,64},{1,97},{33,1},{65,33},{97,65},{2,98}... | collective-permute-start | bytes 344072 | tf_op jit(solution)/shard_map/ppermute | solution.py:511
  211.4 5.3 %collective-permute-start.23 = (bf16[16,3584]{1,0:T(8,128)(2,1)S(1)}, bf16[16,3584]{1,0:T(8,128)(2,1)S(1)}, u32[]{:S(2)}, u32[]{:S(2)}) collective-permute-start(bf16[16,3584]{1,0:T(8,128)(2,1)S(1)} %get-tuple-element.43), channel_id=1, source_target_pairs={{0,64},{32,96},{64,0},{96,32},{1,65},{33,97},{65,1},{97,33},{2,66}... | collective-permute-start | bytes 344072 | tf_op jit(solution)/shard_map/ppermute | solution.py:511
  211.4 6.1 %collective-permute-start.22 = (bf16[16,3584]{1,0:T(8,128)(2,1)S(1)}, bf16[16,3584]{1,0:T(8,128)(2,1)S(1)}, u32[]{:S(2)}, u32[]{:S(2)}) collective-permute-start(bf16[16,3584]{1,0:T(8,128)(2,1)S(1)} %get-tuple-element.43), channel_id=1, source_target_pairs={{0,32},{32,64},{64,96},{96,0},{1,33},{33,65},{65,97},{97,1},{2,34}... | collective-permute-start | bytes 344072 | tf_op jit(solution)/shard_map/ppermute | solution.py:511
  212.0 29.2 %collective-permute-start.18 = (bf16[16,3584]{1,0:T(8,128)(2,1)S(1)}, bf16[16,3584]{1,0:T(8,128)(2,1)}, u32[]{:S(2)}, u32[]{:S(2)}) collective-permute-start(bf16[16,3584]{1,0:T(8,128)(2,1)S(1)} %get-tuple-element.42), channel_id=1, source_target_pairs={{0,16},{16,0},{1,17},{17,1},{2,18},{18,2},{3,19},{19,3},{4,20},{20... | collective-permute-start | bytes 344072 | tf_op jit(solution)/shard_map/ppermute | solution.py:456
  217.5 38.8 %collective-permute-start.25 = (bf16[4,16,3584]{2,1,0:T(8,128)(2,1)S(1)}, bf16[4,16,3584]{2,1,0:T(8,128)(2,1)S(1)}, u32[]{:S(2)}, u32[]{:S(2)}) collective-permute-start(bf16[4,16,3584]{2,1,0:T(8,128)(2,1)S(1)} %pad_maximum_fusion.refs_4_), channel_id=1, source_target_pairs={{0,16},{16,0},{1,17},{17,1},{2,18},{18,2},{3,19},{19,3},{4,20},{20... | collective-permute-start | bytes 1376264 | tf_op jit(solution)/shard_map/ppermute | solution.py:456
  238.5 20.5 %collective-permute-start.26 = (bf16[512,256]{1,0:T(8,128)(2,1)S(1)}, bf16[512,256]{1,0:T(8,128)(2,1)S(1)}, u32[]{:S(2)}, u32[]{:S(2)}) collective-permute-start(bf16[512,256]{1,0:T(8,128)(2,1)S(1)} %get-tuple-element.46), channel_id=1, source_target_pairs={{0,1},{1,0},{2,3},{3,2},{4,5},{5,4},{6,7},{7,6},{8,9},{9,8},{10,11... | collective-permute-start | bytes 786440 | tf_op jit(solution)/shard_map/ppermute | solution.py:456
  242.1 8.5 %collective-permute-start.19 = (bf16[2,16,3584]{2,1,0:T(8,128)(2,1)S(1)}, bf16[2,16,3584]{2,1,0:T(8,128)(2,1)S(1)}, u32[]{:S(2)}, u32[]{:S(2)}) collective-permute-start(bf16[2,16,3584]{2,1,0:T(8,128)(2,1)S(1)} %pad_maximum_fusion.1.refs_0_), channel_id=1, source_target_pairs={{0,32},{32,64},{64,96},{96,0},{1,33},{33,65},{65,97},{97,1},{2,34}... | collective-permute-start | bytes 688136 | tf_op jit(solution)/shard_map/ppermute | solution.py:512
  242.2 14.1 %collective-permute-start.20 = (bf16[2,16,3584]{2,1,0:T(8,128)(2,1)S(1)}, bf16[2,16,3584]{2,1,0:T(8,128)(2,1)S(1)}, u32[]{:S(2)}, u32[]{:S(2)}) collective-permute-start(bf16[2,16,3584]{2,1,0:T(8,128)(2,1)S(1)} %pad_maximum_fusion.1.refs_0_), channel_id=1, source_target_pairs={{0,64},{32,96},{64,0},{96,32},{1,65},{33,97},{65,1},{97,33},{2,66}... | collective-permute-start | bytes 688136 | tf_op jit(solution)/shard_map/ppermute | solution.py:512
  245.7 10.7 %collective-permute-start.21 = (bf16[2,16,3584]{2,1,0:T(8,128)(2,1)S(1)}, bf16[2,16,3584]{2,1,0:T(8,128)(2,1)S(1)}, u32[]{:S(2)}, u32[]{:S(2)}) collective-permute-start(bf16[2,16,3584]{2,1,0:T(8,128)(2,1)S(1)} %pad_maximum_fusion.1.refs_0_), channel_id=1, source_target_pairs={{0,96},{32,0},{64,32},{96,64},{1,97},{33,1},{65,33},{97,65},{2,98}... | collective-permute-start | bytes 688136 | tf_op jit(solution)/shard_map/ppermute | solution.py:512
  (18 other events, 107.0 us)

commit v4 on v3

--- a/solution.py
+++ b/solution.py
@@ -12,7 +12,6 @@
 PADDED = 224
 WIDTH = 72
 HALO = 3
-RIDER = 32
 K = 512
 TAPS = 28
 COLS = TAPS * 128
@@ -338,69 +337,82 @@
     )(got, xt)
 
 
-def sum_samples_kernel(got, first, second):
-    for yh, out in enumerate((first, second)):
+def sum_samples_kernel(got, out):
+    for yh in range(2):
         total = got[yh].astype(F32)
         for rep in range(1, 8):
             total = total + got[2 * rep + yh].astype(F32)
-        out[...] = total.astype(BF16)
+        out[yh] = total.astype(BF16)
 
 
 def sum_samples(got):
     return pl.pallas_call(
         sum_samples_kernel,
-        out_shape=(jax.ShapeDtypeStruct((16, COLS), BF16),) * 2,
+        out_shape=jax.ShapeDtypeStruct((2, 16, COLS), BF16),
         in_specs=[VMEM],
-        out_specs=(VMEM,) * 2,
+        out_specs=VMEM,
         compiler_params=params(24),
     )(got)
 
 
-def feature_grad_kernel(got, wt, proj, out, moved, point):
+def feature_grad_kernel(got, wt, out, moved, point):
     spread(got, moved, point)
-    rider = jnp.concatenate([proj[:RIDER], proj[RIDER:]], 1).astype(BF16)
+    taps = [tap for pair in PAIRS for tap in pair]
 
     def step(i, _):
-        cols, rows = [], []
-        for pair in PAIRS:
-            for tap in pair:
-                cols.append(spread_columns(moved, point, tap, 2 * i, 2))
-                rows.append(wt[tap[0]])
-        part = jnp.dot(
-            jnp.concatenate(cols, 1), jnp.concatenate(rows, 0), preferred_element_type=F32
-        )
-        part = part.astype(BF16)
+        left = jnp.concatenate([spread_columns(moved, point, tap, 2 * i, 2) for tap in taps], 1)
+        right = jnp.concatenate([wt[tap[0]] for tap in taps], 0)
+        part = jnp.dot(left, right, preferred_element_type=F32).astype(BF16)
         for sub in range(2):
-            out[2 * i + sub, :PADDED] = part[sub * PADDED : (sub + 1) * PADDED]
-            out[2 * i + sub, PADDED:] = rider
+            out[2 * i + sub] = part[sub * PADDED : sub * PADDED + CELLS]
         return 0
 
     lax.fori_loop(0, CHIPS // 2, step, 0)
 
 
-def feature_grad(got, wt, proj):
+def feature_grad(got, wt):
     return pl.pallas_call(
         feature_grad_kernel,
-        out_shape=jax.ShapeDtypeStruct((CHIPS, PADDED + RIDER, K), BF16),
-        in_specs=[VMEM] * 3,
+        out_shape=jax.ShapeDtypeStruct((CHIPS, CELLS, K), BF16),
+        in_specs=[VMEM] * 2,
         out_specs=VMEM,
         scratch_shapes=SPREAD,
         compiler_params=params(56),
         cost_estimate=CONV_COST,
-    )(got, wt, proj)
+    )(got, wt)
+
+
+def pack_sums_kernel(mine, other, proj, out):
+    for n, block in enumerate((mine, other)):
+        for yh in range(2):
+            out[n, yh, :, :COLS] = block[yh]
+            for half in range(2):
+                row = half * 64 + n * 32 + yh * 16
+                lane = COLS + half * 256
+                out[n, yh, :, lane : lane + 256] = proj[row : row + 16, :].astype(BF16)
+
+
+def pack_sums(mine, other, proj):
+    return pl.pallas_call(
+        pack_sums_kernel,
+        out_shape=jax.ShapeDtypeStruct((2, 2, 16, COLS + 512), BF16),
+        in_specs=[VMEM] * 3,
+        out_specs=VMEM,
+        compiler_params=params(16),
+    )(mine, other, proj)
 
 
 def place_grads_kernel(place, *refs):
-    point, atrous = refs[6], refs[7]
+    point, atrous = refs[4], refs[5]
     z, yl = place[0], place[3]
     for d in range(4):
         for l in range(2):
             rep = 2 * lax.rem(z + 4 - d, 4) + lax.rem(yl + l, 2)
             rows = pl.ds(pl.multiple_of(rep * 16, 16), 16)
-            for yh, block in enumerate((refs[d][l], refs[4 + l][d])):
+            for yh in range(2):
                 cols = slice(yh * 128, (yh + 1) * 128)
                 for t in range(TAPS):
-                    part = block[:, t * 128 : (t + 1) * 128].astype(F32) * 0.125
+                    part = refs[d][l, yh, :, t * 128 : (t + 1) * 128].astype(F32) * 0.125
                     if t == 0:
                         point[rows, cols] = part
                     else:
@@ -414,36 +426,67 @@
             jax.ShapeDtypeStruct((128, 256), F32),
             jax.ShapeDtypeStruct((27, 128, 256), F32),
         ),
-        in_specs=[SMEM] + [VMEM] * 6,
+        in_specs=[SMEM] + [VMEM] * 4,
         out_specs=(VMEM,) * 2,
         compiler_params=params(40),
     )(place, *blocks)
 
 
-def gray(x):
-    return (x ^ (x >> 1)) & 1
-
-
-def join_features_kernel(got, out, proj):
+def proj_half_kernel(place, b0, b1, b2, b3, out):
+    for d, block in enumerate((b0, b1, b2, b3)):
+        z = lax.rem(place[0] + 4 - d, 4)
+        row = gray(z) * 256 + (z >> 1) * 128
+        for n in range(2):
+            for yh in range(2):
+                for half in range(2):
+                    at = pl.multiple_of(row + half * 64 + n * 32 + yh * 16, 16)
+                    lane = COLS + half * 256
+                    out[pl.ds(at, 16), :] = block[n, yh, :, lane : lane + 256]
+
+
+def proj_half(place, blocks):
+    return pl.pallas_call(
+        proj_half_kernel,
+        out_shape=jax.ShapeDtypeStruct((512, 256), BF16),
+        in_specs=[SMEM] + [VMEM] * 4,
+        out_specs=VMEM,
+        compiler_params=params(24),
+    )(place, *blocks)
+
+
+def join_proj_kernel(place, mine, other, out):
+    c = place[2]
+    for half, block in enumerate((mine, other)):
+        yh = c if half == 0 else 1 - c
+        for branch in range(4):
+            part = block[branch * 128 : (branch + 1) * 128, :].astype(F32) * 0.125
+            rows = pl.multiple_of(branch * 256 + yh * 128, 128)
+            out[pl.ds(rows, 128), :] = part
+
+
+def join_proj(place, mine, other):
+    return pl.pallas_call(
+        join_proj_kernel,
+        out_shape=jax.ShapeDtypeStruct((1024, 256), F32),
+        in_specs=[SMEM, VMEM, VMEM],
+        out_specs=VMEM,
+        compiler_params=params(16),
+    )(place, mine, other)
+
+
+def join_features_kernel(got, out):
     for x in range(4):
-        total = (got[x, :CELLS].astype(F32) + got[4 + x, :CELLS].astype(F32)).astype(BF16)
+        total = (got[x].astype(F32) + got[4 + x].astype(F32)).astype(BF16)
         for yh in range(2):
             out[:, (yh * 4 + x) * 256 : (yh * 4 + x + 1) * 256] = total[:, yh * 256 : (yh + 1) * 256]
-            rider = got[yh * 4 + x, PADDED:]
-            row = gray(x) * 256 + (x >> 1) * 128 + yh * 64
-            proj[row : row + RIDER] = rider[:, :256]
-            proj[row + RIDER : row + 2 * RIDER] = rider[:, 256:]
 
 
 def join_features(got):
     return pl.pallas_call(
         join_features_kernel,
-        out_shape=(
-            jax.ShapeDtypeStruct((CELLS, 2048), BF16),
-            jax.ShapeDtypeStruct((512, 256), BF16),
-        ),
+        out_shape=jax.ShapeDtypeStruct((CELLS, 2048), BF16),
         in_specs=[VMEM],
-        out_specs=(VMEM,) * 2,
+        out_specs=VMEM,
         compiler_params=params(16),
     )(got)
 
@@ -458,6 +501,10 @@
 
 BESIDE = [(i, i ^ 1) for i in range(4)]
 ACROSS = [(i, 3 - i) for i in range(4)]
+
+
+def gray(i):
+    return (i ^ (i >> 1)) & 1
 
 
 def halved(v, axis, pairs, bit):
@@ -467,8 +514,20 @@
     return mine + lax.ppermute(theirs.astype(BF16), axis, pairs).astype(F32)
 
 
+def added(v, axis, pairs):
+    return v + lax.ppermute(v.astype(BF16), axis, pairs).astype(F32)
+
+
+def added_over_y(v):
+    total, sent = v, v.astype(BF16)
+    for l, h in ((0, 1), (1, 0), (1, 1)):
+        pairs = [(2 * i + j, 2 * ((i + l) % 2) + (j + h) % 2) for i in range(2) for j in range(2)]
+        total = total + lax.ppermute(sent, ("yl", "yh"), pairs).astype(F32)
+    return total
+
+
 def shards(features, atrous_weight, point_weight, proj_weight, cotangent):
-    place = jnp.stack([lax.axis_index(a) for a in ("z", "x", "c", "yl")]).astype(jnp.int32)
+    place = jnp.stack([lax.axis_index(a) for a in ("z", "x", "c", "yl", "yh")]).astype(jnp.int32)
 
     atrous_t = jnp.transpose(atrous_weight, (0, 2, 1))
     parts = split_weights(place, jnp.transpose(point_weight, (1, 0)), atrous_t)
@@ -489,35 +548,33 @@
     dpre = lax.all_to_all(d_send, ("yh", "x"), 0, 0, tiled=True)
     xt = turn_features(place, x)
 
-    core, column, side = (lax.axis_index(a) for a in ("c", "x", "yh"))
+    core, layer = lax.axis_index("c"), lax.axis_index("z")
     share = halved(proj_part, "c", turn(2, 1), core)
-    share = halved(share, "x", BESIDE, gray(column))
-    share = halved(share, "x", ACROSS, column >> 1)
+    share = halved(share, "z", BESIDE, gray(layer))
+    share = halved(share, "z", ACROSS, layer >> 1)
+    share = added_over_y(share)
     dpre, share = lax.optimization_barrier((dpre, share))
 
     keep, send = kernel_grad(dpre, xt)
     g_part = (keep.astype(F32) + swap(send, "c").astype(F32)).astype(BF16)
     g_got = lax.all_to_all(g_part.reshape(16, 16, COLS), ("z", "yl", "yh"), 0, 0, tiled=True)
 
-    share = halved(share, "yh", turn(2, 1), side)
-    share = share + swap(share, "yl")
-    share = share + lax.ppermute(share, "z", BESIDE)
-    share = share + lax.ppermute(share, "z", ACROSS)
-    back = feature_grad(dpre, wt, share)
-
-    first, second = sum_samples(g_got)
-    back, first, second = lax.optimization_barrier((back, first, second))
-    pair = jnp.stack([first, swap(first, "yl")])
-    four = jnp.stack([second] + [lax.ppermute(second, "z", turn(4, d)) for d in (1, 2, 3)])
+    dpre, _ = lax.optimization_barrier((dpre, g_part))
+    back = feature_grad(dpre, wt)
+    share, _ = lax.optimization_barrier((share, back))
+    share = added(share, "x", BESIDE)
+    share = added(share, "x", ACROSS)
+
+    g_got, back, share = lax.optimization_barrier((g_got, back, share))
+    g_sum = sum_samples(g_got)
+    swapped = swap(g_sum, "yl")
+    back, swapped = lax.optimization_barrier((back, swapped))
+    pair = pack_sums(g_sum, swapped, share)
     pairs = [pair] + [lax.ppermute(pair, "z", turn(4, d)) for d in (1, 2, 3)]
-    grad_point, grad_atrous = place_grads(place, pairs + [four, swap(four, "yl")])
-
-    b_got = lax.all_to_all(back, ("yh", "x"), 0, 0, tiled=True)
-    input_grad, half = join_features(b_got)
-    other = swap(half, "c")
-    grad_proj = jnp.where(core == 0, jnp.stack([half, other]), jnp.stack([other, half]))
-    grad_proj = grad_proj.astype(F32).reshape(2, 4, 128, 256).transpose(1, 0, 2, 3)
-    grad_proj = grad_proj.reshape(1024, 256) * 0.125
+    input_grad = join_features(lax.all_to_all(back, ("yh", "x"), 0, 0, tiled=True))
+    half = proj_half(place, pairs)
+    grad_point, grad_atrous = place_grads(place, pairs)
+    grad_proj = join_proj(place, half, swap(half, "c"))
 
     return (
         projected.reshape(1, 3, WIDTH, 256),

time: 261 us -> 225 us (0.86)
  waiting for transfers between devices: 128 us -> 97.5 us
  starting transfers between devices: 72.3 us -> 67.2 us
    ppermute x4 -> x3, waiting for transfers between devices: 40.3 us -> 8.29 us  [halved(): return mine + lax.ppermute(theirs.astype(BF16), axis, pairs).astype(F32)]
    all_to_all x1, waiting for transfers between devices: 19.7 us -> 0.01 us  [shards(): lax.all_to_all(back, ('yh', 'x'), 0, 0, tiled=True)]
    ppermute x3, waiting for transfers between devices: 10.4 us -> 25.4 us  [shards(): pairs = [pair] + [lax.ppermute(pair, 'z', turn(4, d)) for d in (1, 2, 3)]]
    ppermute x4 -> x3, starting transfers between devices: 8.56 us -> 2.53 us  [halved(): return mine + lax.ppermute(theirs.astype(BF16), axis, pairs).astype(F32)]
    ppermute x5, waiting for transfers between devices: 9.39 us -> 13.8 us  [the longest x3 9.52 us: added_over_y(): total = total + lax.ppermute(sent, ('yl', 'yh'), pairs).astype(F32)]
    all_to_all x1, waiting for transfers between devices: 0.01 us -> 3.55 us  [shards(): lax.all_to_all(g_part.reshape(16, 16, COLS), ('z', 'yl', 'yh'), 0, 0, til...]
    all_to_all x1, starting transfers between devices: 3.62 us -> 6.97 us  [shards(): lax.all_to_all(back, ('yh', 'x'), 0, 0, tiled=True)]
    ppermute x9 -> x7, waiting for transfers between devices: 8.81 us -> 9.98 us  [swap(): return lax.ppermute(v, axis, turn(2, 1))]
  transfers between devices with their start and end apart: 32 -> 29, of which waited for: 20 -> 17; matrix products, arithmetic and copies ran while one was open for 1% -> 1% of each run, Pallas kernels for 7% -> 9%
where the time goes in v4:
time: 225 us; the launch traced here: 224 us
  waiting for transfers between devices  97.5 us (43%)
  starting transfers between devices  67.2 us (30%)
  Pallas kernels  46.3 us (21%)
  local copies, waits for them, and re-layouts  7.98 us (4%)
  other arithmetic  4.57 us (2%)
    ppermute x3, waiting for transfers between devices, shards(): pairs = [pair] + [lax.ppermute(pair, 'z', turn(4, d)) for d in (1, 2, 3)]  25.4 us
    all_to_all x1, waiting for transfers between devices, shards(): got = lax.all_to_all(partial, ('yh', 'x'), 0, 0, tiled=True)  25 us
    ppermute x7, starting transfers between devices, swap(): return lax.ppermute(v, axis, turn(2, 1))  16.6 us
    pallas_call x1, Pallas kernels, feature_grad(): pl.pallas_call(feature_grad_kernel, out_shape=jax.ShapeDtypeStruct((CHIPS...  12.2 us
    pallas_call x1, Pallas kernels, kernel_grad(): pl.pallas_call(kernel_grad_kernel, out_shape=(jax.ShapeDtypeStruct((8, 2,...  11.6 us
    pallas_call x1, Pallas kernels, forward(): pl.pallas_call(forward_kernel, out_shape=jax.ShapeDtypeStruct((CHIPS, CEL...  10.5 us
    ppermute x7, waiting for transfers between devices, swap(): return lax.ppermute(v, axis, turn(2, 1))  9.98 us
    ppermute x3, waiting for transfers between devices, added_over_y(): total = total + lax.ppermute(sent, ('yl', 'yh'), pairs).astype(F32)  9.52 us
  transfers between devices with their start and end apart: 29, of which 17 were waited for; matrix products, arithmetic and copies ran while one was open for 1% of the time, Pallas kernels for 9%

profile of v4, /device:TPU:1, one launch (start us, length us, event | category | flops | bytes accessed | tf_op | source)
XLA Modules:
  0.0 224.5 jit_solution(1401849039911669330)
XLA Ops:
  14.1 6.3 %all-to-all-start = ((bf16[8,216,512]{2,1,0:T(8,128)(2,1)}), bf16[8,216,512]{2,1,0:T(8,128)(2,1)S(1)}, u32[]{:S(2)}, u32[]{:S(2)}) async-start(bf16[8,216,512]{2,1,0:T(8,128)(2,1)} %shard_map.92), calls=%async_computation | async-start | bytes 3538944 | tf_op jit(solution)/shard_map/all_to_all | solution.py:542
  20.4 3.8 %collective-permute-start.5 = (bf16[4,7,16,512]{3,2,1,0:T(8,128)(2,1)S(1)}, bf16[4,7,16,512]{3,2,1,0:T(8,128)(2,1)S(1)}, u32[]{:S(2)}, u32[]{:S(2)}) collective-permute-start(bf16[4,7,16,512]{3,2,1,0:T(8,128)(2,1)S(1)} %shard_map.94.refs_0_), channel_id=1, source_target_pairs={{0,96},{32,0},{64,32},{96,64},{1,97},{33,1},{65,33},{97,65},{2,98}... | collective-permute-start | bytes 1376264 | tf_op jit(solution)/shard_map/ppermute | solution.py:536
  24.8 2.7 %collective-permute-start.6 = (bf16[4,7,16,512]{3,2,1,0:T(8,128)(2,1)S(1)}, bf16[4,7,16,512]{3,2,1,0:T(8,128)(2,1)S(1)}, u32[]{:S(2)}, u32[]{:S(2)}) collective-permute-start(bf16[4,7,16,512]{3,2,1,0:T(8,128)(2,1)S(1)} %shard_map.94.refs_0_), channel_id=1, source_target_pairs={{0,1},{1,0},{2,3},{3,2},{4,5},{5,4},{6,7},{7,6},{8,9},{9,8},{10,11... | collective-permute-start | bytes 1376264 | tf_op jit(solution)/shard_map/ppermute | solution.py:499
  27.5 6.3 %collective-permute-done.5.refs_3_ = bf16[4,7,16,512]{3,2,1,0:T(8,128)(2,1)S(1)} collective-permute-done((bf16[4,7,16,512]{3,2,1,0:T(8,128)(2,1)S(1)}, bf16[4,7,16,512]{3,2,1,0:T(8,128)(2,1)S(1)}, u32[]{:S(2)}, u32[]{:S(2)}) %collective-permute-start.5) | collective-permute-done | bytes 458784 | tf_op jit(solution)/shard_map/ppermute | solution.py:536
  33.8 10.9 %collective-permute-start.9 = (bf16[4,7,16,512]{3,2,1,0:T(8,128)(2,1)S(1)}, bf16[4,7,16,512]{3,2,1,0:T(8,128)(2,1)S(1)}, u32[]{:S(2)}, u32[]{:S(2)}) collective-permute-start(bf16[4,7,16,512]{3,2,1,0:T(8,128)(2,1)S(1)} %collective-permute-done.5.refs_3_), channel_id=1, source_target_pairs={{0,1},{1,0},{2,3},{3,2},{4,5},{5,4},{6,7},{7,6},{8,9},{9,8},{10,11... | collective-permute-start | bytes 1376264 | tf_op jit(solution)/shard_map/ppermute | solution.py:499
  53.4 10.5 %shard_map.96 = bf16[8,216,512]{2,1,0:T(8,128)(2,1)} custom-call(bf16[8,216,512]{2,1,0:T(8,128)(2,1)} %copy-done, bf16[28,128,512]{2,1,0:T(8,128)(2,1)} %bitcast.17), custom_call_target="tpu_custom_call" | custom-call | flops 6341787648 | bytes 8388608 | tf_op jit(solution)/shard_map/pallas_call | solution.py:193
  63.8 6.8 %all-to-all-start.1 = ((bf16[8,216,512]{2,1,0:T(8,128)(2,1)}), bf16[8,216,512]{2,1,0:T(8,128)(2,1)S(1)}, u32[]{:S(2)}, u32[]{:S(2)}) async-start(bf16[8,216,512]{2,1,0:T(8,128)(2,1)} %shard_map.96), calls=%async_computation.1 | async-start | bytes 3538944 | tf_op jit(solution)/shard_map/all_to_all | solution.py:545
  70.7 25.0 %all-to-all-done.1.got = bf16[8,216,512]{2,1,0:T(8,128)(2,1)S(1)} async-done(((bf16[8,216,512]{2,1,0:T(8,128)(2,1)}), bf16[8,216,512]{2,1,0:T(8,128)(2,1)S(1)}, u32[]{:S(2)}, u32[]{:S(2)}) %all-to-all-start.1) | async-done | bytes 1769504 | tf_op jit(solution)/shard_map/all_to_all | solution.py:545
  99.1 4.9 %all-to-all-start.2 = ((bf16[8,216,512]{2,1,0:T(8,128)(2,1)}), bf16[8,216,512]{2,1,0:T(8,128)(2,1)}, u32[]{:S(2)}, u32[]{:S(2)}) async-start(bf16[8,216,512]{2,1,0:T(8,128)(2,1)} %copy-done.4), calls=%async_computation.2 | async-start | bytes 3538944 | tf_op jit(solution)/shard_map/all_to_all | solution.py:548
  105.5 4.9 %collective-permute-done.11 = bf16[256,256]{1,0:T(8,128)(2,1)S(1)} collective-permute-done((bf16[256,256]{1,0:T(8,128)(2,1)S(1)}, bf16[256,256]{1,0:T(8,128)(2,1)S(1)}, u32[]{:S(2)}, u32[]{:S(2)}) %collective-permute-start.11) | collective-permute-done | bytes 131104 | tf_op jit(solution)/shard_map/ppermute | solution.py:514
  111.8 3.4 %collective-permute-done.12 = bf16[128,256]{1,0:T(8,128)(2,1)S(1)} collective-permute-done((bf16[128,256]{1,0:T(8,128)(2,1)S(1)}, bf16[128,256]{1,0:T(8,128)(2,1)S(1)}, u32[]{:S(2)}, u32[]{:S(2)}) %collective-permute-start.12) | collective-permute-done | bytes 65568 | tf_op jit(solution)/shard_map/ppermute | solution.py:514
  121.4 3.8 %collective-permute-done.15 = bf16[128,256]{1,0:T(8,128)(2,1)S(1)} collective-permute-done((bf16[128,256]{1,0:T(8,128)(2,1)S(1)}, bf16[128,256]{1,0:T(8,128)(2,1)S(1)}, u32[]{:S(2)}, u32[]{:S(2)}) %collective-permute-start.15) | collective-permute-done | bytes 65568 | tf_op jit(solution)/shard_map/ppermute | solution.py:525
  125.2 5.7 %collective-permute-done.13 = bf16[128,256]{1,0:T(8,128)(2,1)S(1)} collective-permute-done((bf16[128,256]{1,0:T(8,128)(2,1)S(1)}, bf16[128,256]{1,0:T(8,128)(2,1)S(1)}, u32[]{:S(2)}, u32[]{:S(2)}) %collective-permute-start.13) | collective-permute-done | bytes 65568 | tf_op jit(solution)/shard_map/ppermute | solution.py:525
  131.0 11.6 %shard_map.99 = (bf16[8,2,16,3584]{3,2,1,0:T(8,128)(2,1)}, bf16[8,2,16,3584]{3,2,1,0:T(8,128)(2,1)}) custom-call(bf16[8,216,512]{2,1,0:T(8,128)(2,1)} %all-to-all-done.2.got, bf16[4,128,1792]{2,1,0:T(8,128)(2,1)} %copy-done.3), custom_call_target="tpu_custom_call" | custom-call | flops 6341787648 | bytes 8388608 | tf_op jit(solution)/shard_map/pallas_call | solution.py:329
  143.1 3.6 %collective-permute-done.16 = bf16[8,2,16,3584]{3,2,1,0:T(8,128)(2,1)S(1)} collective-permute-done((bf16[8,2,16,3584]{3,2,1,0:T(8,128)(2,1)}, bf16[8,2,16,3584]{3,2,1,0:T(8,128)(2,1)S(1)}, u32[]{:S(2)}, u32[]{:S(2)}) %collective-permute-start.16) | collective-permute-done | bytes 1835040 | tf_op jit(solution)/shard_map/ppermute | solution.py:499
  146.7 3.3 %add_convert_fusion = bf16[8,2,16,3584]{3,2,1,0:T(8,128)(2,1)} fusion(bf16[8,2,16,3584]{3,2,1,0:T(8,128)(2,1)S(1)} %collective-permute-done.16, bf16[8,2,16,3584]{3,2,1,0:T(8,128)(2,1)} %get-tuple-element.35), kind=kLoop, calls=%fused_computation | loop fusion | flops 3670016 | bytes 5505024 | tf_op jit(solution)/shard_map/convert_element_type | solution.py:559
  150.0 3.7 %all-to-all-start.3 = ((bf16[16,16,3584]{2,1,0:T(8,128)(2,1)}), bf16[16,16,3584]{2,1,0:T(8,128)(2,1)S(1)}, u32[]{:S(2)}, u32[]{:S(2)}) async-start(bf16[16,16,3584]{2,1,0:T(8,128)(2,1)} %bitcast.24), calls=%async_computation.3 | async-start | bytes 3670016 | tf_op jit(solution)/shard_map/all_to_all | solution.py:560
  153.7 12.2 %shard_map.100 = bf16[8,216,512]{2,1,0:T(8,128)(2,1)} custom-call(bf16[8,216,512]{2,1,0:T(8,128)(2,1)} %all-to-all-done.2.got, bf16[28,128,512]{2,1,0:T(8,128)(2,1)} %bitcast.18), custom_call_target="tpu_custom_call" | custom-call | flops 6341787648 | bytes 8388608 | tf_op jit(solution)/shard_map/pallas_call | solution.py:374
  169.5 2.6 %collective-permute-start.18 = (bf16[128,256]{1,0:T(8,128)(2,1)S(1)}, bf16[128,256]{1,0:T(8,128)(2,1)S(1)}, u32[]{:S(2)}, u32[]{:S(2)}) collective-permute-start(bf16[128,256]{1,0:T(8,128)(2,1)S(1)} %fusion), channel_id=1, source_target_pairs={{0,6},{2,4},{4,2},{6,0},{1,7},{3,5},{5,3},{7,1},{8,14},{10,12},{12... | collective-permute-start | bytes 196616 | tf_op jit(solution)/shard_map/ppermute | solution.py:518
  174.2 3.5 %all-to-all-done.3.got = bf16[16,16,3584]{2,1,0:T(8,128)(2,1)S(1)} async-done(((bf16[16,16,3584]{2,1,0:T(8,128)(2,1)}), bf16[16,16,3584]{2,1,0:T(8,128)(2,1)S(1)}, u32[]{:S(2)}, u32[]{:S(2)}) %all-to-all-start.3) | async-done | bytes 1835040 | tf_op jit(solution)/shard_map/all_to_all | solution.py:560
  179.1 4.9 %collective-permute-done.19.other = bf16[2,16,3584]{2,1,0:T(8,128)(2,1)S(1)} collective-permute-done((bf16[2,16,3584]{2,1,0:T(8,128)(2,1)S(1)}, bf16[2,16,3584]{2,1,0:T(8,128)(2,1)S(1)}, u32[]{:S(2)}, u32[]{:S(2)}) %collective-permute-start.19) | collective-permute-done | bytes 229408 | tf_op jit(solution)/shard_map/ppermute | solution.py:499
  184.0 7.0 %all-to-all-start.4 = ((bf16[8,216,512]{2,1,0:T(8,128)(2,1)}), bf16[8,216,512]{2,1,0:T(8,128)(2,1)S(1)}, u32[]{:S(2)}, u32[]{:S(2)}) async-start(bf16[8,216,512]{2,1,0:T(8,128)(2,1)} %shard_map.100), calls=%async_computation.4 | async-start | bytes 3538944 | tf_op jit(solution)/shard_map/all_to_all | solution.py:574
  192.6 9.4 %collective-permute-done.22.refs_3_.b3 = bf16[2,2,16,4096]{3,2,1,0:T(8,128)(2,1)S(1)} collective-permute-done((bf16[2,2,16,4096]{3,2,1,0:T(8,128)(2,1)S(1)}, bf16[2,2,16,4096]{3,2,1,0:T(8,128)(2,1)S(1)}, u32[]{:S(2)}, u32[]{:S(2)}) %collective-permute-start.22) | collective-permute-done | bytes 524320 | tf_op jit(solution)/shard_map/ppermute | solution.py:573
  203.7 14.3 %collective-permute-done.20.refs_1_.b1 = bf16[2,2,16,4096]{3,2,1,0:T(8,128)(2,1)S(1)} collective-permute-done((bf16[2,2,16,4096]{3,2,1,0:T(8,128)(2,1)S(1)}, bf16[2,2,16,4096]{3,2,1,0:T(8,128)(2,1)S(1)}, u32[]{:S(2)}, u32[]{:S(2)}) %collective-permute-start.20) | collective-permute-done | bytes 524320 | tf_op jit(solution)/shard_map/ppermute | solution.py:573
  (82 shorter events, 52.7 us)
Async XLA Ops:
  4.0 7.1 %collective-permute-start = (bf16[7,16,512]{2,1,0:T(8,128)(2,1)S(1)}, bf16[7,16,512]{2,1,0:T(8,128)(2,1)S(1)}, u32[]{:S(2)}, u32[]{:S(2)}) collective-permute-start(bf16[7,16,512]{2,1,0:T(8,128)(2,1)S(1)} %get-tuple-element.27), channel_id=1, source_target_pairs={{0,2},{2,4},{4,6},{6,0},{1,3},{3,5},{5,7},{7,1},{8,10},{10,12},{12... | collective-permute-start | bytes 344072 | tf_op jit(solution)/shard_map/ppermute | solution.py:534
  6.1 7.5 %collective-permute-start.1 = (bf16[7,16,512]{2,1,0:T(8,128)(2,1)S(1)}, bf16[7,16,512]{2,1,0:T(8,128)(2,1)S(1)}, u32[]{:S(2)}, u32[]{:S(2)}) collective-permute-start(bf16[7,16,512]{2,1,0:T(8,128)(2,1)S(1)} %get-tuple-element.28), channel_id=1, source_target_pairs={{0,4},{2,6},{4,0},{6,2},{1,5},{3,7},{5,1},{7,3},{8,12},{10,14},{12... | collective-permute-start | bytes 344072 | tf_op jit(solution)/shard_map/ppermute | solution.py:534
  8.5 5.0 %collective-permute-start.2 = (bf16[7,16,512]{2,1,0:T(8,128)(2,1)S(1)}, bf16[7,16,512]{2,1,0:T(8,128)(2,1)S(1)}, u32[]{:S(2)}, u32[]{:S(2)}) collective-permute-start(bf16[7,16,512]{2,1,0:T(8,128)(2,1)S(1)} %get-tuple-element.29), channel_id=1, source_target_pairs={{0,6},{2,0},{4,2},{6,4},{1,7},{3,1},{5,3},{7,5},{8,14},{10,8},{12,... | collective-permute-start | bytes 344072 | tf_op jit(solution)/shard_map/ppermute | solution.py:534
  14.1 38.0 %all-to-all-start = ((bf16[8,216,512]{2,1,0:T(8,128)(2,1)}), bf16[8,216,512]{2,1,0:T(8,128)(2,1)S(1)}, u32[]{:S(2)}, u32[]{:S(2)}) async-start(bf16[8,216,512]{2,1,0:T(8,128)(2,1)} %shard_map.92), calls=%async_computation | async-start | bytes 3538944 | tf_op jit(solution)/shard_map/all_to_all | solution.py:542
  20.4 13.4 %collective-permute-start.5 = (bf16[4,7,16,512]{3,2,1,0:T(8,128)(2,1)S(1)}, bf16[4,7,16,512]{3,2,1,0:T(8,128)(2,1)S(1)}, u32[]{:S(2)}, u32[]{:S(2)}) collective-permute-start(bf16[4,7,16,512]{3,2,1,0:T(8,128)(2,1)S(1)} %shard_map.94.refs_0_), channel_id=1, source_target_pairs={{0,96},{32,0},{64,32},{96,64},{1,97},{33,1},{65,33},{97,65},{2,98}... | collective-permute-start | bytes 1376264 | tf_op jit(solution)/shard_map/ppermute | solution.py:536
  24.1 20.6 %collective-permute-start.4 = (bf16[4,7,16,512]{3,2,1,0:T(8,128)(2,1)S(1)}, bf16[4,7,16,512]{3,2,1,0:T(8,128)(2,1)S(1)}, u32[]{:S(2)}, u32[]{:S(2)}) collective-permute-start(bf16[4,7,16,512]{3,2,1,0:T(8,128)(2,1)S(1)} %shard_map.94.refs_0_), channel_id=1, source_target_pairs={{0,64},{32,96},{64,0},{96,32},{1,65},{33,97},{65,1},{97,33},{2,66}... | collective-permute-start | bytes 1376264 | tf_op jit(solution)/shard_map/ppermute | solution.py:536
  24.1 23.1 %collective-permute-start.3 = (bf16[4,7,16,512]{3,2,1,0:T(8,128)(2,1)S(1)}, bf16[4,7,16,512]{3,2,1,0:T(8,128)(2,1)S(1)}, u32[]{:S(2)}, u32[]{:S(2)}) collective-permute-start(bf16[4,7,16,512]{3,2,1,0:T(8,128)(2,1)S(1)} %shard_map.94.refs_0_), channel_id=1, source_target_pairs={{0,32},{32,64},{64,96},{96,0},{1,33},{33,65},{65,97},{97,1},{2,34}... | collective-permute-start | bytes 1376264 | tf_op jit(solution)/shard_map/ppermute | solution.py:536
  24.8 23.3 %collective-permute-start.6 = (bf16[4,7,16,512]{3,2,1,0:T(8,128)(2,1)S(1)}, bf16[4,7,16,512]{3,2,1,0:T(8,128)(2,1)S(1)}, u32[]{:S(2)}, u32[]{:S(2)}) collective-permute-start(bf16[4,7,16,512]{3,2,1,0:T(8,128)(2,1)S(1)} %shard_map.94.refs_0_), channel_id=1, source_target_pairs={{0,1},{1,0},{2,3},{3,2},{4,5},{5,4},{6,7},{7,6},{8,9},{9,8},{10,11... | collective-permute-start | bytes 1376264 | tf_op jit(solution)/shard_map/ppermute | solution.py:499
  33.8 14.3 %collective-permute-start.9 = (bf16[4,7,16,512]{3,2,1,0:T(8,128)(2,1)S(1)}, bf16[4,7,16,512]{3,2,1,0:T(8,128)(2,1)S(1)}, u32[]{:S(2)}, u32[]{:S(2)}) collective-permute-start(bf16[4,7,16,512]{3,2,1,0:T(8,128)(2,1)S(1)} %collective-permute-done.5.refs_3_), channel_id=1, source_target_pairs={{0,1},{1,0},{2,3},{3,2},{4,5},{5,4},{6,7},{7,6},{8,9},{9,8},{10,11... | collective-permute-start | bytes 1376264 | tf_op jit(solution)/shard_map/ppermute | solution.py:499
  63.8 31.9 %all-to-all-start.1 = ((bf16[8,216,512]{2,1,0:T(8,128)(2,1)}), bf16[8,216,512]{2,1,0:T(8,128)(2,1)S(1)}, u32[]{:S(2)}, u32[]{:S(2)}) async-start(bf16[8,216,512]{2,1,0:T(8,128)(2,1)} %shard_map.96), calls=%async_computation.1 | async-start | bytes 3538944 | tf_op jit(solution)/shard_map/all_to_all | solution.py:545
  98.2 5.8 %collective-permute-start.10 = (bf16[512,256]{1,0:T(8,128)(2,1)S(1)}, bf16[512,256]{1,0:T(8,128)(2,1)}, u32[]{:S(2)}, u32[]{:S(2)}) collective-permute-start(bf16[512,256]{1,0:T(8,128)(2,1)S(1)} %dynamic-slice_convert_fusion), channel_id=1, source_target_pairs={{0,1},{1,0},{2,3},{3,2},{4,5},{5,4},{6,7},{7,6},{8,9},{9,8},{10,11... | collective-permute-start | bytes 786440 | tf_op jit(solution)/shard_map/ppermute | solution.py:514
  99.1 31.9 %all-to-all-start.2 = ((bf16[8,216,512]{2,1,0:T(8,128)(2,1)}), bf16[8,216,512]{2,1,0:T(8,128)(2,1)}, u32[]{:S(2)}, u32[]{:S(2)}) async-start(bf16[8,216,512]{2,1,0:T(8,128)(2,1)} %copy-done.4), calls=%async_computation.2 | async-start | bytes 3538944 | tf_op jit(solution)/shard_map/all_to_all | solution.py:548
  105.2 5.1 %collective-permute-start.11 = (bf16[256,256]{1,0:T(8,128)(2,1)S(1)}, bf16[256,256]{1,0:T(8,128)(2,1)S(1)}, u32[]{:S(2)}, u32[]{:S(2)}) collective-permute-start(bf16[256,256]{1,0:T(8,128)(2,1)S(1)} %dynamic-slice_convert_fusion.1), channel_id=1, source_target_pairs={{0,32},{32,0},{64,96},{96,64},{1,33},{33,1},{65,97},{97,65},{2,34}... | collective-permute-start | bytes 393224 | tf_op jit(solution)/shard_map/ppermute | solution.py:514
  110.4 4.8 %collective-permute-start.12 = (bf16[128,256]{1,0:T(8,128)(2,1)S(1)}, bf16[128,256]{1,0:T(8,128)(2,1)S(1)}, u32[]{:S(2)}, u32[]{:S(2)}) collective-permute-start(bf16[128,256]{1,0:T(8,128)(2,1)S(1)} %dynamic-slice_convert_fusion.2), channel_id=1, source_target_pairs={{0,96},{32,64},{64,32},{96,0},{1,97},{33,65},{65,33},{97,1},{2,98}... | collective-permute-start | bytes 196616 | tf_op jit(solution)/shard_map/ppermute | solution.py:514
  115.2 10.0 %collective-permute-start.15 = (bf16[128,256]{1,0:T(8,128)(2,1)S(1)}, bf16[128,256]{1,0:T(8,128)(2,1)S(1)}, u32[]{:S(2)}, u32[]{:S(2)}) collective-permute-start(bf16[128,256]{1,0:T(8,128)(2,1)S(1)} %fusion.1), channel_id=1, source_target_pairs={{0,24},{8,16},{16,8},{24,0},{1,25},{9,17},{17,9},{25,1},{2,26},{10... | collective-permute-start | bytes 196616 | tf_op jit(solution)/shard_map/ppermute | solution.py:525
  117.7 7.5 %collective-permute-start.14 = (bf16[128,256]{1,0:T(8,128)(2,1)S(1)}, bf16[128,256]{1,0:T(8,128)(2,1)S(1)}, u32[]{:S(2)}, u32[]{:S(2)}) collective-permute-start(bf16[128,256]{1,0:T(8,128)(2,1)S(1)} %fusion.1), channel_id=1, source_target_pairs={{0,16},{8,24},{16,0},{24,8},{1,17},{9,25},{17,1},{25,9},{2,18},{10... | collective-permute-start | bytes 196616 | tf_op jit(solution)/shard_map/ppermute | solution.py:525
  117.7 13.2 %collective-permute-start.13 = (bf16[128,256]{1,0:T(8,128)(2,1)S(1)}, bf16[128,256]{1,0:T(8,128)(2,1)S(1)}, u32[]{:S(2)}, u32[]{:S(2)}) collective-permute-start(bf16[128,256]{1,0:T(8,128)(2,1)S(1)} %fusion.1), channel_id=1, source_target_pairs={{0,8},{8,0},{16,24},{24,16},{1,9},{9,1},{17,25},{25,17},{2,10},{10... | collective-permute-start | bytes 196616 | tf_op jit(solution)/shard_map/ppermute | solution.py:525
  150.0 27.8 %all-to-all-start.3 = ((bf16[16,16,3584]{2,1,0:T(8,128)(2,1)}), bf16[16,16,3584]{2,1,0:T(8,128)(2,1)S(1)}, u32[]{:S(2)}, u32[]{:S(2)}) async-start(bf16[16,16,3584]{2,1,0:T(8,128)(2,1)} %bitcast.24), calls=%async_computation.3 | async-start | bytes 3670016 | tf_op jit(solution)/shard_map/all_to_all | solution.py:560
  169.5 4.7 %collective-permute-start.18 = (bf16[128,256]{1,0:T(8,128)(2,1)S(1)}, bf16[128,256]{1,0:T(8,128)(2,1)S(1)}, u32[]{:S(2)}, u32[]{:S(2)}) collective-permute-start(bf16[128,256]{1,0:T(8,128)(2,1)S(1)} %fusion), channel_id=1, source_target_pairs={{0,6},{2,4},{4,2},{6,0},{1,7},{3,5},{5,3},{7,1},{8,14},{10,12},{12... | collective-permute-start | bytes 196616 | tf_op jit(solution)/shard_map/ppermute | solution.py:518
  178.0 6.0 %collective-permute-start.19 = (bf16[2,16,3584]{2,1,0:T(8,128)(2,1)S(1)}, bf16[2,16,3584]{2,1,0:T(8,128)(2,1)S(1)}, u32[]{:S(2)}, u32[]{:S(2)}) collective-permute-start(bf16[2,16,3584]{2,1,0:T(8,128)(2,1)S(1)} %shard_map.101.mine), channel_id=1, source_target_pairs={{0,16},{16,0},{1,17},{17,1},{2,18},{18,2},{3,19},{19,3},{4,20},{20... | collective-permute-start | bytes 688136 | tf_op jit(solution)/shard_map/ppermute | solution.py:499
  184.0 39.4 %all-to-all-start.4 = ((bf16[8,216,512]{2,1,0:T(8,128)(2,1)}), bf16[8,216,512]{2,1,0:T(8,128)(2,1)S(1)}, u32[]{:S(2)}, u32[]{:S(2)}) async-start(bf16[8,216,512]{2,1,0:T(8,128)(2,1)} %shard_map.100), calls=%async_computation.4 | async-start | bytes 3538944 | tf_op jit(solution)/shard_map/all_to_all | solution.py:574
  191.0 10.9 %collective-permute-start.22 = (bf16[2,2,16,4096]{3,2,1,0:T(8,128)(2,1)S(1)}, bf16[2,2,16,4096]{3,2,1,0:T(8,128)(2,1)S(1)}, u32[]{:S(2)}, u32[]{:S(2)}) collective-permute-start(bf16[2,2,16,4096]{3,2,1,0:T(8,128)(2,1)S(1)} %shard_map.103.refs_0_.b0), channel_id=1, source_target_pairs={{0,96},{32,0},{64,32},{96,64},{1,97},{33,1},{65,33},{97,65},{2,98}... | collective-permute-start | bytes 1572872 | tf_op jit(solution)/shard_map/ppermute | solution.py:573
  191.4 12.3 %collective-permute-start.21 = (bf16[2,2,16,4096]{3,2,1,0:T(8,128)(2,1)S(1)}, bf16[2,2,16,4096]{3,2,1,0:T(8,128)(2,1)S(1)}, u32[]{:S(2)}, u32[]{:S(2)}) collective-permute-start(bf16[2,2,16,4096]{3,2,1,0:T(8,128)(2,1)S(1)} %shard_map.103.refs_0_.b0), channel_id=1, source_target_pairs={{0,64},{32,96},{64,0},{96,32},{1,65},{33,97},{65,1},{97,33},{2,66}... | collective-permute-start | bytes 1572872 | tf_op jit(solution)/shard_map/ppermute | solution.py:573
  191.8 26.2 %collective-permute-start.20 = (bf16[2,2,16,4096]{3,2,1,0:T(8,128)(2,1)S(1)}, bf16[2,2,16,4096]{3,2,1,0:T(8,128)(2,1)S(1)}, u32[]{:S(2)}, u32[]{:S(2)}) collective-permute-start(bf16[2,2,16,4096]{3,2,1,0:T(8,128)(2,1)S(1)} %shard_map.103.refs_0_.b0), channel_id=1, source_target_pairs={{0,32},{32,64},{64,96},{96,0},{1,33},{33,65},{65,97},{97,1},{2,34}... | collective-permute-start | bytes 1572872 | tf_op jit(solution)/shard_map/ppermute | solution.py:573
  (15 other events, 84.7 us)

commit v5 on v4

--- a/solution.py
+++ b/solution.py
@@ -20,6 +20,7 @@
 F32 = jnp.float32
 VMEM = pl.BlockSpec(memory_space=pltpu.VMEM)
 SMEM = pl.BlockSpec(memory_space=pltpu.SMEM)
+ANY = pl.BlockSpec(memory_space=pl.ANY)
 
 
 def tap_of(g, ky, kx):
@@ -64,13 +65,15 @@
         for yh in range(2):
             part = x[:, (yh * 4 + col) * 256 : (yh * 4 + col + 1) * 256]
             for dest in range(2):
-                out[dest * 4 + col, :, yh * 256 : (yh + 1) * 256] = part
+                out[dest * 4 + col, :CELLS, yh * 256 : (yh + 1) * 256] = part
+    for chip in range(CHIPS):
+        out[chip, CELLS:] = jnp.zeros((PADDED - CELLS, K), BF16)
 
 
 def split_features(x):
     return pl.pallas_call(
         split_features_kernel,
-        out_shape=jax.ShapeDtypeStruct((CHIPS, CELLS, K), BF16),
+        out_shape=jax.ShapeDtypeStruct((CHIPS, PADDED, K), BF16),
         in_specs=[VMEM],
         out_specs=VMEM,
         compiler_params=params(16),
@@ -98,7 +101,7 @@
     return pl.pallas_call(
         split_weights_kernel,
         out_shape=(jax.ShapeDtypeStruct((QUARTER, 16, K), BF16),) * 4,
-        in_specs=[SMEM, VMEM, pl.BlockSpec(memory_space=pl.ANY)],
+        in_specs=[SMEM, VMEM, ANY],
         out_specs=(VMEM,) * 4,
         scratch_shapes=[pltpu.VMEM((QUARTER + 1, 16, 2048), BF16), pltpu.SemaphoreType.DMA],
         compiler_params=params(16),
@@ -106,28 +109,14 @@
     )(place, point, atrous)
 
 
-def join_weights_kernel(place, *refs):
-    out = refs[8]
-    z, me = place[0], place[2]
-    for which in range(2):
-        c = me if which == 0 else 1 - me
-        for d in range(4):
-            quarter = lax.rem(z + 4 - d, 4)
-            block = refs[which * 4 + d]
-            for x in range(4):
-                for t in range(QUARTER):
-                    out[quarter * QUARTER + t, x, c] = block[x, t]
-
-
-def join_weights(place, blocks):
-    return pl.pallas_call(
-        join_weights_kernel,
-        out_shape=jax.ShapeDtypeStruct((TAPS, 4, 2, 16, K), BF16),
-        in_specs=[SMEM] + [VMEM] * 8,
-        out_specs=VMEM,
-        compiler_params=params(24),
-        cost_estimate=cost(0, 8 << 20),
-    )(place, *blocks)
+WEIGHTS = (2, 4, 4, QUARTER, 16, K)
+
+
+def weights_of(wt, taps):
+    rows = []
+    for t in taps:
+        rows += [wt[c, t // QUARTER, x, t % QUARTER] for x in range(4) for c in range(2)]
+    return jnp.concatenate(rows, 0)
 
 
 def stack_columns_kernel(place, b0, b1, b2, b3, out):
@@ -146,10 +135,13 @@
     )(place, *blocks)
 
 
-def forward_kernel(x, wt, out, xs, acc):
-    for j in range(CHIPS):
-        xs[j, :CELLS] = x[j]
-        xs[j, CELLS:] = jnp.zeros((PADDED - CELLS, K), BF16)
+def forward_kernel(place, x, *refs):
+    blocks, (out, kept, done, acc, out_sem, wt, w_sem) = refs[:8], refs[8:]
+    for n, block in enumerate(blocks):
+        c = place[2] if n < 4 else 1 - place[2]
+        wt[c, lax.rem(place[0] + 4 - n % 4, 4)] = block[...]
+    keep = pltpu.make_async_copy(wt, kept, w_sem)
+    keep.start()
 
     def span(g, ky):
         return max(0, ky * (g + 1)), CHIPS + min(0, ky * (g + 1))
@@ -157,8 +149,8 @@
     for pair in PAIRS:
         begin = min(span(g, ky)[0] for _, g, ky, _ in pair)
         end = max(span(g, ky)[1] for _, g, ky, _ in pair)
-        rows = xs[begin:end].reshape((end - begin) * PADDED, K)
-        right = jnp.concatenate([wt[t] for t, _, _, _ in pair], 0)
+        rows = x[begin:end].reshape((end - begin) * PADDED, K)
+        right = weights_of(wt, [tap[0] for tap in pair])
         y = lax.dot_general(rows, right, (((1,), (1,)), ((), ())), preferred_element_type=F32)
         y = y.reshape(end - begin, PADDED, 256)
         for half, (_, g, ky, kx) in enumerate(pair):
@@ -183,25 +175,35 @@
                 + jnp.where(column >= d, minus, 0.0)
                 + jnp.where(column < WIDTH - d, plus, 0.0)
             )
-        out[j] = jnp.concatenate(parts, 1).astype(BF16)[:CELLS]
+        done[j] = jnp.concatenate(parts, 1).astype(BF16)[:CELLS]
+        pltpu.make_async_copy(done.at[j], out.at[j], out_sem.at[j]).start()
         return 0
 
     lax.fori_loop(0, CHIPS, finish, 0)
-
-
-def forward(x, wt):
+    for j in range(CHIPS):
+        pltpu.make_async_copy(done.at[j], out.at[j], out_sem.at[j]).wait()
+    keep.wait()
+
+
+def forward(place, x, blocks):
     return pl.pallas_call(
         forward_kernel,
-        out_shape=jax.ShapeDtypeStruct((CHIPS, CELLS, 512), BF16),
-        in_specs=[VMEM] * 2,
-        out_specs=VMEM,
+        out_shape=(
+            jax.ShapeDtypeStruct((CHIPS, CELLS, 512), BF16),
+            jax.ShapeDtypeStruct(WEIGHTS, BF16),
+        ),
+        in_specs=[SMEM] + [VMEM] * 9,
+        out_specs=(ANY,) * 2,
         scratch_shapes=[
-            pltpu.VMEM((CHIPS, PADDED, K), BF16),
+            pltpu.VMEM((CHIPS, CELLS, 512), BF16),
             pltpu.VMEM((10, CHIPS, PADDED, 128), F32),
+            pltpu.SemaphoreType.DMA((CHIPS,)),
+            pltpu.VMEM(WEIGHTS, BF16),
+            pltpu.SemaphoreType.DMA,
         ],
         compiler_params=params(56),
         cost_estimate=CONV_COST,
-    )(x, wt)
+    )(place, x, *blocks)
 
 
 def sigmoid(v):
@@ -285,11 +287,8 @@
     return v.reshape(count * PADDED, 128)
 
 
-def turn_features_kernel(place, x, out, xs):
-    for j in range(CHIPS):
-        xs[j, :CELLS] = x[j]
-        xs[j, CELLS:] = jnp.zeros((PADDED - CELLS, K), BF16)
-    flat = xs[...].reshape(CHIPS * PADDED, K)
+def turn_features_kernel(place, x, out):
+    flat = x[...].reshape(CHIPS * PADDED, K)
     for yh in range(2):
         for core in range(2):
             lanes = slice((yh * 2 + core) * 128, (yh * 2 + core + 1) * 128)
@@ -305,36 +304,70 @@
         out_shape=jax.ShapeDtypeStruct((4, 128, CHIPS * PADDED), BF16),
         in_specs=[SMEM, VMEM],
         out_specs=VMEM,
-        scratch_shapes=[pltpu.VMEM((CHIPS, PADDED, K), BF16)],
         compiler_params=params(32),
         cost_estimate=cost(0, 8 << 20),
     )(place, x)
 
 
-def kernel_grad_kernel(got, xt, keep, send, moved, point):
+def kernel_grad_kernel(got, xt, keep, send, kept, sent, xs, x_sem, out_sem, moved, point):
+    load = pltpu.make_async_copy(xt, xs, x_sem)
+    load.start()
     spread(got, moved, point)
-    left = xt[...].reshape(K, CHIPS * PADDED)
+    load.wait()
+    left = xs[...].reshape(K, CHIPS * PADDED)
+    stores = []
     for pair in PAIRS:
         right = jnp.concatenate([spread_columns(moved, point, tap, 0, CHIPS) for tap in pair], 1)
         part = jnp.dot(left, right, preferred_element_type=F32).astype(BF16)
         for half, tap in enumerate(pair):
-            cols = slice(tap[0] * 128, (tap[0] + 1) * 128)
+            cols = pl.ds(tap[0] * 128, 128)
             block = part[:, half * 128 : (half + 1) * 128].reshape(2, 2, 8, 16, 128)
-            for yh in range(2):
-                keep[:, yh, :, cols] = block[0, yh]
-                send[:, yh, :, cols] = block[1, yh]
+            for n, (local, out) in enumerate(((kept, keep), (sent, send))):
+                for yh in range(2):
+                    local[:, yh, :, cols] = block[n, yh]
+                view = (slice(None), slice(None), slice(None), cols)
+                stores.append(
+                    pltpu.make_async_copy(local.at[view], out.at[view], out_sem.at[n, tap[0]])
+                )
+                stores[-1].start()
+    for copy in stores:
+        copy.wait()
 
 
 def kernel_grad(got, xt):
+    local = pltpu.VMEM((8, 2, 16, COLS), BF16)
     return pl.pallas_call(
         kernel_grad_kernel,
         out_shape=(jax.ShapeDtypeStruct((8, 2, 16, COLS), BF16),) * 2,
-        in_specs=[VMEM, VMEM],
-        out_specs=(VMEM,) * 2,
-        scratch_shapes=SPREAD,
+        in_specs=[VMEM, ANY],
+        out_specs=(ANY,) * 2,
+        scratch_shapes=[
+            local,
+            local,
+            pltpu.VMEM((4, 128, CHIPS * PADDED), BF16),
+            pltpu.SemaphoreType.DMA,
+            pltpu.SemaphoreType.DMA((2, TAPS)),
+        ]
+        + SPREAD,
         compiler_params=params(56),
         cost_estimate=CONV_COST,
     )(got, xt)
+
+
+def add_cores_kernel(mine, other, out):
+    out[...] = (mine[...].astype(F32) + other[...].astype(F32)).astype(BF16)
+
+
+def add_cores(mine, other):
+    spec = pl.BlockSpec((2, 2, 16, COLS), lambda i: (i, 0, 0, 0))
+    return pl.pallas_call(
+        add_cores_kernel,
+        grid=(4,),
+        out_shape=jax.ShapeDtypeStruct((8, 2, 16, COLS), BF16),
+        in_specs=[spec] * 2,
+        out_specs=spec,
+        compiler_params=params(16),
+    )(mine, other)
 
 
 def sum_samples_kernel(got, out):
@@ -355,13 +388,16 @@
     )(got)
 
 
-def feature_grad_kernel(got, wt, out, moved, point):
+def feature_grad_kernel(got, kept, out, moved, point, wt, w_sem):
+    load = pltpu.make_async_copy(kept, wt, w_sem)
+    load.start()
     spread(got, moved, point)
+    load.wait()
     taps = [tap for pair in PAIRS for tap in pair]
 
     def step(i, _):
         left = jnp.concatenate([spread_columns(moved, point, tap, 2 * i, 2) for tap in taps], 1)
-        right = jnp.concatenate([wt[tap[0]] for tap in taps], 0)
+        right = weights_of(wt, [tap[0] for tap in taps])
         part = jnp.dot(left, right, preferred_element_type=F32).astype(BF16)
         for sub in range(2):
             out[2 * i + sub] = part[sub * PADDED : sub * PADDED + CELLS]
@@ -370,16 +406,16 @@
     lax.fori_loop(0, CHIPS // 2, step, 0)
 
 
-def feature_grad(got, wt):
+def feature_grad(got, kept):
     return pl.pallas_call(
         feature_grad_kernel,
         out_shape=jax.ShapeDtypeStruct((CHIPS, CELLS, K), BF16),
-        in_specs=[VMEM] * 2,
-        out_specs=VMEM,
-        scratch_shapes=SPREAD,
+        in_specs=[VMEM, ANY],
+        out_specs=VMEM,
+        scratch_shapes=SPREAD + [pltpu.VMEM(WEIGHTS, BF16), pltpu.SemaphoreType.DMA],
         compiler_params=params(56),
         cost_estimate=CONV_COST,
-    )(got, wt)
+    )(got, kept)
 
 
 def pack_sums_kernel(mine, other, proj, out):
@@ -535,13 +571,12 @@
     quarter = stack_columns(place, from_x)
     quarters = [quarter] + [lax.ppermute(quarter, "z", turn(4, d)) for d in (1, 2, 3)]
     blocks = quarters + [swap(v, "c") for v in quarters]
-    wt = join_weights(place, blocks).reshape(TAPS, 128, K)
 
     x_send = split_features(features.reshape(CELLS, 2048))
     x_send, quarter = lax.optimization_barrier((x_send, quarter))
     x = lax.all_to_all(x_send, ("yh", "x"), 0, 0, tiled=True)
 
-    partial = forward(x, wt)
+    partial, wt = forward(place, x, blocks)
     got = lax.all_to_all(partial, ("yh", "x"), 0, 0, tiled=True)
     proj = proj_weight.reshape(4, 2, 128, 256).transpose(1, 0, 2, 3).reshape(1024, 256)
     projected, d_send, proj_part = middle(got, proj, cotangent.reshape(CELLS, 256))
@@ -556,7 +591,7 @@
     dpre, share = lax.optimization_barrier((dpre, share))
 
     keep, send = kernel_grad(dpre, xt)
-    g_part = (keep.astype(F32) + swap(send, "c").astype(F32)).astype(BF16)
+    g_part = add_cores(keep, swap(send, "c"))
     g_got = lax.all_to_all(g_part.reshape(16, 16, COLS), ("z", "yl", "yh"), 0, 0, tiled=True)
 
     dpre, _ = lax.optimization_barrier((dpre, g_part))

time: 225 us -> 223 us (level)
  local copies, waits for them, and re-layouts: 7.98 us -> 12.5 us
  waiting for transfers between devices: 97.5 us -> 93.6 us
  other arithmetic: 4.57 us -> 1.13 us
  starting transfers between devices: 67.2 us -> 70.1 us
    ppermute x7, starting transfers between devices: 16.6 us -> 12.6 us  [swap(): return lax.ppermute(v, axis, turn(2, 1))]
    unnamed x20 -> x44, local copies, waits for them, and re-layouts: 7.79 us -> 11.6 us
    convert_element_type x1 -> x0, other arithmetic: 3.32 us -> none  [shards(): g_part = (keep.astype(F32) + swap(send, 'c').astype(F32)).astype(BF16)]
    ppermute x3, waiting for transfers between devices: 25.4 us -> 22.7 us  [shards(): pairs = [pair] + [lax.ppermute(pair, 'z', turn(4, d)) for d in (1, 2, 3)]]
    ppermute x3, waiting for transfers between devices: 8.85 us -> 11.4 us  [shards(): lax.ppermute(quarter, 'z', turn(4, d))]
  transfers between devices with their start and end apart: 29 -> 29, of which waited for: 17 -> 17; matrix products, arithmetic and copies ran while one was open for 1% -> 1% of each run, Pallas kernels for 9% -> 8%
where the time goes in v5:
time: 223 us
  waiting for transfers between devices  93.6 us (42%)
  starting transfers between devices  70.1 us (31%)
  Pallas kernels  44.3 us (20%)
  local copies, waits for them, and re-layouts  12.5 us (6%)
    all_to_all x1, waiting for transfers between devices, shards(): got = lax.all_to_all(partial, ('yh', 'x'), 0, 0, tiled=True)  25 us
    ppermute x3, waiting for transfers between devices, shards(): pairs = [pair] + [lax.ppermute(pair, 'z', turn(4, d)) for d in (1, 2, 3)]  22.7 us
    ppermute x7, starting transfers between devices, swap(): return lax.ppermute(v, axis, turn(2, 1))  12.6 us
    pallas_call x1, Pallas kernels, feature_grad(): pl.pallas_call(feature_grad_kernel, out_shape=jax.ShapeDtypeStruct((CHIPS...  12 us
    unnamed x44, local copies, waits for them, and re-layouts  11.6 us
    pallas_call x1, Pallas kernels, kernel_grad(): pl.pallas_call(kernel_grad_kernel, out_shape=(jax.ShapeDtypeStruct((8, 2,...  11.5 us
    ppermute x3, waiting for transfers between devices, shards(): lax.ppermute(quarter, 'z', turn(4, d))  11.4 us
    pallas_call x1, Pallas kernels, forward(): pl.pallas_call(forward_kernel, out_shape=(jax.ShapeDtypeStruct((CHIPS, CE...  10.2 us
  transfers between devices with their start and end apart: 29, of which 17 were waited for; matrix products, arithmetic and copies ran while one was open for 1% of the time, Pallas kernels for 8%

profile of v5, /device:TPU:1, one launch (start us, length us, event | category | flops | bytes accessed | tf_op | source)
XLA Modules:
  0.0 222.5 jit_solution(1483564641215698957)
XLA Ops:
  14.1 6.3 %all-to-all-start = ((bf16[8,224,512]{2,1,0:T(8,128)(2,1)}), bf16[8,224,512]{2,1,0:T(8,128)(2,1)S(1)}, u32[]{:S(2)}, u32[]{:S(2)}) async-start(bf16[8,224,512]{2,1,0:T(8,128)(2,1)} %copy-done.2), calls=%async_computation | async-start | bytes 3670016 | tf_op jit(solution)/shard_map/all_to_all | solution.py:577
  22.0 3.3 %collective-permute-start.4 = (bf16[4,7,16,512]{3,2,1,0:T(8,128)(2,1)S(1)}, bf16[4,7,16,512]{3,2,1,0:T(8,128)(2,1)S(1)}, u32[]{:S(2)}, u32[]{:S(2)}) collective-permute-start(bf16[4,7,16,512]{3,2,1,0:T(8,128)(2,1)S(1)} %shard_map.94.refs_0_), channel_id=1, source_target_pairs={{0,64},{32,96},{64,0},{96,32},{1,65},{33,97},{65,1},{97,33},{2,66}... | collective-permute-start | bytes 1376264 | tf_op jit(solution)/shard_map/ppermute | solution.py:572
  28.8 4.4 %collective-permute-done.3.refs_1_ = bf16[4,7,16,512]{3,2,1,0:T(8,128)(2,1)S(1)} collective-permute-done((bf16[4,7,16,512]{3,2,1,0:T(8,128)(2,1)S(1)}, bf16[4,7,16,512]{3,2,1,0:T(8,128)(2,1)S(1)}, u32[]{:S(2)}, u32[]{:S(2)}) %collective-permute-start.3) | collective-permute-done | bytes 458784 | tf_op jit(solution)/shard_map/ppermute | solution.py:572
  33.1 3.7 %collective-permute-start.7 = (bf16[4,7,16,512]{3,2,1,0:T(8,128)(2,1)S(1)}, bf16[4,7,16,512]{3,2,1,0:T(8,128)(2,1)S(1)}, u32[]{:S(2)}, u32[]{:S(2)}) collective-permute-start(bf16[4,7,16,512]{3,2,1,0:T(8,128)(2,1)S(1)} %collective-permute-done.3.refs_1_), channel_id=1, source_target_pairs={{0,1},{1,0},{2,3},{3,2},{4,5},{5,4},{6,7},{7,6},{8,9},{9,8},{10,11... | collective-permute-start | bytes 1376264 | tf_op jit(solution)/shard_map/ppermute | solution.py:535
  36.8 7.0 %collective-permute-done.4.refs_2_ = bf16[4,7,16,512]{3,2,1,0:T(8,128)(2,1)S(1)} collective-permute-done((bf16[4,7,16,512]{3,2,1,0:T(8,128)(2,1)S(1)}, bf16[4,7,16,512]{3,2,1,0:T(8,128)(2,1)S(1)}, u32[]{:S(2)}, u32[]{:S(2)}) %collective-permute-start.4) | collective-permute-done | bytes 458784 | tf_op jit(solution)/shard_map/ppermute | solution.py:572
  43.9 2.8 %collective-permute-start.8 = (bf16[4,7,16,512]{3,2,1,0:T(8,128)(2,1)S(1)}, bf16[4,7,16,512]{3,2,1,0:T(8,128)(2,1)S(1)}, u32[]{:S(2)}, u32[]{:S(2)}) collective-permute-start(bf16[4,7,16,512]{3,2,1,0:T(8,128)(2,1)S(1)} %collective-permute-done.4.refs_2_), channel_id=1, source_target_pairs={{0,1},{1,0},{2,3},{3,2},{4,5},{5,4},{6,7},{7,6},{8,9},{9,8},{10,11... | collective-permute-start | bytes 1376264 | tf_op jit(solution)/shard_map/ppermute | solution.py:535
  50.2 10.2 %shard_map.95 = (bf16[8,216,512]{2,1,0:T(8,128)(2,1)}, bf16[2,4,4,7,16,512]{5,4,3,2,1,0:T(8,128)(2,1)}) custom-call(s32[5]{0:T(128)} %copy-done.12, bf16[8,224,512]{2,1,0:T(8,128)(2,1)} %copy-done, bf16[4,7,16,512]{3,2,1,0:T(8,128)(2,1)} %copy-done.9, bf16[4,7,16,512]{3,2,1,0:T(8,128)(2,1)} %copy-done.16, bf16[4,7,16,512]{3,2,1,0:T(8,128)(2,1)} %copy-done.17, ...), custom_call_target="tpu_custom_call" | custom-call | flops 6341787648 | bytes 8388608 | tf_op jit(solution)/shard_map/pallas_call | solution.py:189
  60.5 6.8 %all-to-all-start.1 = ((bf16[8,216,512]{2,1,0:T(8,128)(2,1)}), bf16[8,216,512]{2,1,0:T(8,128)(2,1)S(1)}, u32[]{:S(2)}, u32[]{:S(2)}) async-start(bf16[8,216,512]{2,1,0:T(8,128)(2,1)} %get-tuple-element.33), calls=%async_computation.1 | async-start | bytes 3538944 | tf_op jit(solution)/shard_map/all_to_all | solution.py:580
  67.3 25.0 %all-to-all-done.1.got = bf16[8,216,512]{2,1,0:T(8,128)(2,1)S(1)} async-done(((bf16[8,216,512]{2,1,0:T(8,128)(2,1)}), bf16[8,216,512]{2,1,0:T(8,128)(2,1)S(1)}, u32[]{:S(2)}, u32[]{:S(2)}) %all-to-all-start.1) | async-done | bytes 1769504 | tf_op jit(solution)/shard_map/all_to_all | solution.py:580
  96.3 4.9 %all-to-all-start.2 = ((bf16[8,216,512]{2,1,0:T(8,128)(2,1)}), bf16[8,216,512]{2,1,0:T(8,128)(2,1)}, u32[]{:S(2)}, u32[]{:S(2)}) async-start(bf16[8,216,512]{2,1,0:T(8,128)(2,1)} %copy-done.6), calls=%async_computation.2 | async-start | bytes 3538944 | tf_op jit(solution)/shard_map/all_to_all | solution.py:583
  103.6 3.7 %collective-permute-done.11 = bf16[256,256]{1,0:T(8,128)(2,1)S(1)} collective-permute-done((bf16[256,256]{1,0:T(8,128)(2,1)S(1)}, bf16[256,256]{1,0:T(8,128)(2,1)S(1)}, u32[]{:S(2)}, u32[]{:S(2)}) %collective-permute-start.11) | collective-permute-done | bytes 131104 | tf_op jit(solution)/shard_map/ppermute | solution.py:550
  119.4 3.1 %collective-permute-done.15 = bf16[128,256]{1,0:T(8,128)(2,1)S(1)} collective-permute-done((bf16[128,256]{1,0:T(8,128)(2,1)S(1)}, bf16[128,256]{1,0:T(8,128)(2,1)S(1)}, u32[]{:S(2)}, u32[]{:S(2)}) %collective-permute-start.15) | collective-permute-done | bytes 65568 | tf_op jit(solution)/shard_map/ppermute | solution.py:561
  122.5 5.7 %collective-permute-done.13 = bf16[128,256]{1,0:T(8,128)(2,1)S(1)} collective-permute-done((bf16[128,256]{1,0:T(8,128)(2,1)S(1)}, bf16[128,256]{1,0:T(8,128)(2,1)S(1)}, u32[]{:S(2)}, u32[]{:S(2)}) %collective-permute-start.13) | collective-permute-done | bytes 65568 | tf_op jit(solution)/shard_map/ppermute | solution.py:561
  128.2 11.5 %shard_map.98 = (bf16[8,2,16,3584]{3,2,1,0:T(8,128)(2,1)}, bf16[8,2,16,3584]{3,2,1,0:T(8,128)(2,1)}) custom-call(bf16[8,216,512]{2,1,0:T(8,128)(2,1)} %all-to-all-done.2.got, bf16[4,128,1792]{2,1,0:T(8,128)(2,1)} %copy-done.4), custom_call_target="tpu_custom_call" | custom-call | flops 6341787648 | bytes 8388608 | tf_op jit(solution)/shard_map/pallas_call | solution.py:339
  140.3 3.6 %collective-permute-done.16.other = bf16[8,2,16,3584]{3,2,1,0:T(8,128)(2,1)S(1)} collective-permute-done((bf16[8,2,16,3584]{3,2,1,0:T(8,128)(2,1)}, bf16[8,2,16,3584]{3,2,1,0:T(8,128)(2,1)S(1)}, u32[]{:S(2)}, u32[]{:S(2)}) %collective-permute-start.16) | collective-permute-done | bytes 1835040 | tf_op jit(solution)/shard_map/ppermute | solution.py:535
  147.1 3.8 %all-to-all-start.3 = ((bf16[16,16,3584]{2,1,0:T(8,128)(2,1)}), bf16[16,16,3584]{2,1,0:T(8,128)(2,1)S(1)}, u32[]{:S(2)}, u32[]{:S(2)}) async-start(bf16[16,16,3584]{2,1,0:T(8,128)(2,1)} %bitcast.16), calls=%async_computation.3 | async-start | bytes 3670016 | tf_op jit(solution)/shard_map/all_to_all | solution.py:595
  151.0 12.0 %shard_map.100 = bf16[8,216,512]{2,1,0:T(8,128)(2,1)} custom-call(bf16[8,216,512]{2,1,0:T(8,128)(2,1)} %all-to-all-done.2.got, bf16[2,4,4,7,16,512]{5,4,3,2,1,0:T(8,128)(2,1)} %get-tuple-element.41.kept), custom_call_target="tpu_custom_call" | custom-call | flops 6341787648 | bytes 8388608 | tf_op jit(solution)/shard_map/pallas_call | solution.py:410
  166.5 3.6 %collective-permute-start.18 = (bf16[128,256]{1,0:T(8,128)(2,1)S(1)}, bf16[128,256]{1,0:T(8,128)(2,1)S(1)}, u32[]{:S(2)}, u32[]{:S(2)}) collective-permute-start(bf16[128,256]{1,0:T(8,128)(2,1)S(1)} %fusion), channel_id=1, source_target_pairs={{0,6},{2,4},{4,2},{6,0},{1,7},{3,5},{5,3},{7,1},{8,14},{10,12},{12... | collective-permute-start | bytes 196616 | tf_op jit(solution)/shard_map/ppermute | solution.py:554
  172.1 2.8 %all-to-all-done.3.got = bf16[16,16,3584]{2,1,0:T(8,128)(2,1)S(1)} async-done(((bf16[16,16,3584]{2,1,0:T(8,128)(2,1)}), bf16[16,16,3584]{2,1,0:T(8,128)(2,1)S(1)}, u32[]{:S(2)}, u32[]{:S(2)}) %all-to-all-start.3) | async-done | bytes 1835040 | tf_op jit(solution)/shard_map/all_to_all | solution.py:595
  175.9 5.0 %collective-permute-done.19.other = bf16[2,16,3584]{2,1,0:T(8,128)(2,1)S(1)} collective-permute-done((bf16[2,16,3584]{2,1,0:T(8,128)(2,1)S(1)}, bf16[2,16,3584]{2,1,0:T(8,128)(2,1)S(1)}, u32[]{:S(2)}, u32[]{:S(2)}) %collective-permute-start.19) | collective-permute-done | bytes 229408 | tf_op jit(solution)/shard_map/ppermute | solution.py:535
  180.8 8.2 %all-to-all-start.4 = ((bf16[8,216,512]{2,1,0:T(8,128)(2,1)}), bf16[8,216,512]{2,1,0:T(8,128)(2,1)S(1)}, u32[]{:S(2)}, u32[]{:S(2)}) async-start(bf16[8,216,512]{2,1,0:T(8,128)(2,1)} %shard_map.100), calls=%async_computation.4 | async-start | bytes 3538944 | tf_op jit(solution)/shard_map/all_to_all | solution.py:609
  191.9 10.8 %collective-permute-done.20.refs_1_.b1 = bf16[2,2,16,4096]{3,2,1,0:T(8,128)(2,1)S(1)} collective-permute-done((bf16[2,2,16,4096]{3,2,1,0:T(8,128)(2,1)S(1)}, bf16[2,2,16,4096]{3,2,1,0:T(8,128)(2,1)S(1)}, u32[]{:S(2)}, u32[]{:S(2)}) %collective-permute-start.20) | collective-permute-done | bytes 524320 | tf_op jit(solution)/shard_map/ppermute | solution.py:608
  202.7 8.1 %collective-permute-done.21.refs_2_.b2 = bf16[2,2,16,4096]{3,2,1,0:T(8,128)(2,1)S(1)} collective-permute-done((bf16[2,2,16,4096]{3,2,1,0:T(8,128)(2,1)S(1)}, bf16[2,2,16,4096]{3,2,1,0:T(8,128)(2,1)S(1)}, u32[]{:S(2)}, u32[]{:S(2)}) %collective-permute-start.21) | collective-permute-done | bytes 524320 | tf_op jit(solution)/shard_map/ppermute | solution.py:608
  210.8 3.8 %collective-permute-done.22.refs_3_.b3 = bf16[2,2,16,4096]{3,2,1,0:T(8,128)(2,1)S(1)} collective-permute-done((bf16[2,2,16,4096]{3,2,1,0:T(8,128)(2,1)S(1)}, bf16[2,2,16,4096]{3,2,1,0:T(8,128)(2,1)S(1)}, u32[]{:S(2)}, u32[]{:S(2)}) %collective-permute-start.22) | collective-permute-done | bytes 524320 | tf_op jit(solution)/shard_map/ppermute | solution.py:608
  (105 shorter events, 61.5 us)
Async XLA Ops:
  4.0 7.1 %collective-permute-start = (bf16[7,16,512]{2,1,0:T(8,128)(2,1)S(1)}, bf16[7,16,512]{2,1,0:T(8,128)(2,1)S(1)}, u32[]{:S(2)}, u32[]{:S(2)}) collective-permute-start(bf16[7,16,512]{2,1,0:T(8,128)(2,1)S(1)} %get-tuple-element.29), channel_id=1, source_target_pairs={{0,2},{2,4},{4,6},{6,0},{1,3},{3,5},{5,7},{7,1},{8,10},{10,12},{12... | collective-permute-start | bytes 344072 | tf_op jit(solution)/shard_map/ppermute | solution.py:570
  6.1 7.5 %collective-permute-start.1 = (bf16[7,16,512]{2,1,0:T(8,128)(2,1)S(1)}, bf16[7,16,512]{2,1,0:T(8,128)(2,1)S(1)}, u32[]{:S(2)}, u32[]{:S(2)}) collective-permute-start(bf16[7,16,512]{2,1,0:T(8,128)(2,1)S(1)} %get-tuple-element.30), channel_id=1, source_target_pairs={{0,4},{2,6},{4,0},{6,2},{1,5},{3,7},{5,1},{7,3},{8,12},{10,14},{12... | collective-permute-start | bytes 344072 | tf_op jit(solution)/shard_map/ppermute | solution.py:570
  8.5 5.0 %collective-permute-start.2 = (bf16[7,16,512]{2,1,0:T(8,128)(2,1)S(1)}, bf16[7,16,512]{2,1,0:T(8,128)(2,1)S(1)}, u32[]{:S(2)}, u32[]{:S(2)}) collective-permute-start(bf16[7,16,512]{2,1,0:T(8,128)(2,1)S(1)} %get-tuple-element.31), channel_id=1, source_target_pairs={{0,6},{2,0},{4,2},{6,4},{1,7},{3,1},{5,3},{7,5},{8,14},{10,8},{12,... | collective-permute-start | bytes 344072 | tf_op jit(solution)/shard_map/ppermute | solution.py:570
  14.1 34.8 %all-to-all-start = ((bf16[8,224,512]{2,1,0:T(8,128)(2,1)}), bf16[8,224,512]{2,1,0:T(8,128)(2,1)S(1)}, u32[]{:S(2)}, u32[]{:S(2)}) async-start(bf16[8,224,512]{2,1,0:T(8,128)(2,1)} %copy-done.2), calls=%async_computation | async-start | bytes 3670016 | tf_op jit(solution)/shard_map/all_to_all | solution.py:577
  20.4 12.7 %collective-permute-start.3 = (bf16[4,7,16,512]{3,2,1,0:T(8,128)(2,1)S(1)}, bf16[4,7,16,512]{3,2,1,0:T(8,128)(2,1)S(1)}, u32[]{:S(2)}, u32[]{:S(2)}) collective-permute-start(bf16[4,7,16,512]{3,2,1,0:T(8,128)(2,1)S(1)} %shard_map.94.refs_0_), channel_id=1, source_target_pairs={{0,32},{32,64},{64,96},{96,0},{1,33},{33,65},{65,97},{97,1},{2,34}... | collective-permute-start | bytes 1376264 | tf_op jit(solution)/shard_map/ppermute | solution.py:572
  22.0 21.8 %collective-permute-start.4 = (bf16[4,7,16,512]{3,2,1,0:T(8,128)(2,1)S(1)}, bf16[4,7,16,512]{3,2,1,0:T(8,128)(2,1)S(1)}, u32[]{:S(2)}, u32[]{:S(2)}) collective-permute-start(bf16[4,7,16,512]{3,2,1,0:T(8,128)(2,1)S(1)} %shard_map.94.refs_0_), channel_id=1, source_target_pairs={{0,64},{32,96},{64,0},{96,32},{1,65},{33,97},{65,1},{97,33},{2,66}... | collective-permute-start | bytes 1376264 | tf_op jit(solution)/shard_map/ppermute | solution.py:572
  25.3 21.3 %collective-permute-start.5 = (bf16[4,7,16,512]{3,2,1,0:T(8,128)(2,1)S(1)}, bf16[4,7,16,512]{3,2,1,0:T(8,128)(2,1)S(1)}, u32[]{:S(2)}, u32[]{:S(2)}) collective-permute-start(bf16[4,7,16,512]{3,2,1,0:T(8,128)(2,1)S(1)} %shard_map.94.refs_0_), channel_id=1, source_target_pairs={{0,96},{32,0},{64,32},{96,64},{1,97},{33,1},{65,33},{97,65},{2,98}... | collective-permute-start | bytes 1376264 | tf_op jit(solution)/shard_map/ppermute | solution.py:572
  26.1 20.7 %collective-permute-start.6 = (bf16[4,7,16,512]{3,2,1,0:T(8,128)(2,1)S(1)}, bf16[4,7,16,512]{3,2,1,0:T(8,128)(2,1)S(1)}, u32[]{:S(2)}, u32[]{:S(2)}) collective-permute-start(bf16[4,7,16,512]{3,2,1,0:T(8,128)(2,1)S(1)} %shard_map.94.refs_0_), channel_id=1, source_target_pairs={{0,1},{1,0},{2,3},{3,2},{4,5},{5,4},{6,7},{7,6},{8,9},{9,8},{10,11... | collective-permute-start | bytes 1376264 | tf_op jit(solution)/shard_map/ppermute | solution.py:535
  33.1 13.6 %collective-permute-start.7 = (bf16[4,7,16,512]{3,2,1,0:T(8,128)(2,1)S(1)}, bf16[4,7,16,512]{3,2,1,0:T(8,128)(2,1)S(1)}, u32[]{:S(2)}, u32[]{:S(2)}) collective-permute-start(bf16[4,7,16,512]{3,2,1,0:T(8,128)(2,1)S(1)} %collective-permute-done.3.refs_1_), channel_id=1, source_target_pairs={{0,1},{1,0},{2,3},{3,2},{4,5},{5,4},{6,7},{7,6},{8,9},{9,8},{10,11... | collective-permute-start | bytes 1376264 | tf_op jit(solution)/shard_map/ppermute | solution.py:535
  60.5 31.9 %all-to-all-start.1 = ((bf16[8,216,512]{2,1,0:T(8,128)(2,1)}), bf16[8,216,512]{2,1,0:T(8,128)(2,1)S(1)}, u32[]{:S(2)}, u32[]{:S(2)}) async-start(bf16[8,216,512]{2,1,0:T(8,128)(2,1)} %get-tuple-element.33), calls=%async_computation.1 | async-start | bytes 3538944 | tf_op jit(solution)/shard_map/all_to_all | solution.py:580
  95.5 5.7 %collective-permute-start.10 = (bf16[512,256]{1,0:T(8,128)(2,1)}, bf16[512,256]{1,0:T(8,128)(2,1)S(1)}, u32[]{:S(2)}, u32[]{:S(2)}) collective-permute-start(bf16[512,256]{1,0:T(8,128)(2,1)} %dynamic-slice_convert_fusion), channel_id=1, source_target_pairs={{0,1},{1,0},{2,3},{3,2},{4,5},{5,4},{6,7},{7,6},{8,9},{9,8},{10,11... | collective-permute-start | bytes 786440 | tf_op jit(solution)/shard_map/ppermute | solution.py:550
  96.3 31.9 %all-to-all-start.2 = ((bf16[8,216,512]{2,1,0:T(8,128)(2,1)}), bf16[8,216,512]{2,1,0:T(8,128)(2,1)}, u32[]{:S(2)}, u32[]{:S(2)}) async-start(bf16[8,216,512]{2,1,0:T(8,128)(2,1)} %copy-done.6), calls=%async_computation.2 | async-start | bytes 3538944 | tf_op jit(solution)/shard_map/all_to_all | solution.py:583
  102.1 5.2 %collective-permute-start.11 = (bf16[256,256]{1,0:T(8,128)(2,1)S(1)}, bf16[256,256]{1,0:T(8,128)(2,1)S(1)}, u32[]{:S(2)}, u32[]{:S(2)}) collective-permute-start(bf16[256,256]{1,0:T(8,128)(2,1)S(1)} %dynamic-slice_convert_fusion.1), channel_id=1, source_target_pairs={{0,32},{32,0},{64,96},{96,64},{1,33},{33,1},{65,97},{97,65},{2,34}... | collective-permute-start | bytes 393224 | tf_op jit(solution)/shard_map/ppermute | solution.py:550
  108.3 4.8 %collective-permute-start.12 = (bf16[128,256]{1,0:T(8,128)(2,1)S(1)}, bf16[128,256]{1,0:T(8,128)(2,1)S(1)}, u32[]{:S(2)}, u32[]{:S(2)}) collective-permute-start(bf16[128,256]{1,0:T(8,128)(2,1)S(1)} %dynamic-slice_convert_fusion.2), channel_id=1, source_target_pairs={{0,96},{32,64},{64,32},{96,0},{1,97},{33,65},{65,33},{97,1},{2,98}... | collective-permute-start | bytes 196616 | tf_op jit(solution)/shard_map/ppermute | solution.py:550
  113.1 9.3 %collective-permute-start.15 = (bf16[128,256]{1,0:T(8,128)(2,1)S(1)}, bf16[128,256]{1,0:T(8,128)(2,1)S(1)}, u32[]{:S(2)}, u32[]{:S(2)}) collective-permute-start(bf16[128,256]{1,0:T(8,128)(2,1)S(1)} %fusion.1), channel_id=1, source_target_pairs={{0,24},{8,16},{16,8},{24,0},{1,25},{9,17},{17,9},{25,1},{2,26},{10... | collective-permute-start | bytes 196616 | tf_op jit(solution)/shard_map/ppermute | solution.py:561
  115.6 6.8 %collective-permute-start.14 = (bf16[128,256]{1,0:T(8,128)(2,1)S(1)}, bf16[128,256]{1,0:T(8,128)(2,1)S(1)}, u32[]{:S(2)}, u32[]{:S(2)}) collective-permute-start(bf16[128,256]{1,0:T(8,128)(2,1)S(1)} %fusion.1), channel_id=1, source_target_pairs={{0,16},{8,24},{16,0},{24,8},{1,17},{9,25},{17,1},{25,9},{2,18},{10... | collective-permute-start | bytes 196616 | tf_op jit(solution)/shard_map/ppermute | solution.py:561
  115.6 12.5 %collective-permute-start.13 = (bf16[128,256]{1,0:T(8,128)(2,1)S(1)}, bf16[128,256]{1,0:T(8,128)(2,1)S(1)}, u32[]{:S(2)}, u32[]{:S(2)}) collective-permute-start(bf16[128,256]{1,0:T(8,128)(2,1)S(1)} %fusion.1), channel_id=1, source_target_pairs={{0,8},{8,0},{16,24},{24,16},{1,9},{9,1},{17,25},{25,17},{2,10},{10... | collective-permute-start | bytes 196616 | tf_op jit(solution)/shard_map/ppermute | solution.py:561
  147.1 27.7 %all-to-all-start.3 = ((bf16[16,16,3584]{2,1,0:T(8,128)(2,1)}), bf16[16,16,3584]{2,1,0:T(8,128)(2,1)S(1)}, u32[]{:S(2)}, u32[]{:S(2)}) async-start(bf16[16,16,3584]{2,1,0:T(8,128)(2,1)} %bitcast.16), calls=%async_computation.3 | async-start | bytes 3670016 | tf_op jit(solution)/shard_map/all_to_all | solution.py:595
  166.5 5.5 %collective-permute-start.18 = (bf16[128,256]{1,0:T(8,128)(2,1)S(1)}, bf16[128,256]{1,0:T(8,128)(2,1)S(1)}, u32[]{:S(2)}, u32[]{:S(2)}) collective-permute-start(bf16[128,256]{1,0:T(8,128)(2,1)S(1)} %fusion), channel_id=1, source_target_pairs={{0,6},{2,4},{4,2},{6,0},{1,7},{3,5},{5,3},{7,1},{8,14},{10,12},{12... | collective-permute-start | bytes 196616 | tf_op jit(solution)/shard_map/ppermute | solution.py:554
  175.1 5.7 %collective-permute-start.19 = (bf16[2,16,3584]{2,1,0:T(8,128)(2,1)S(1)}, bf16[2,16,3584]{2,1,0:T(8,128)(2,1)S(1)}, u32[]{:S(2)}, u32[]{:S(2)}) collective-permute-start(bf16[2,16,3584]{2,1,0:T(8,128)(2,1)S(1)} %shard_map.101.mine), channel_id=1, source_target_pairs={{0,16},{16,0},{1,17},{17,1},{2,18},{18,2},{3,19},{19,3},{4,20},{20... | collective-permute-start | bytes 688136 | tf_op jit(solution)/shard_map/ppermute | solution.py:535
  180.8 40.6 %all-to-all-start.4 = ((bf16[8,216,512]{2,1,0:T(8,128)(2,1)}), bf16[8,216,512]{2,1,0:T(8,128)(2,1)S(1)}, u32[]{:S(2)}, u32[]{:S(2)}) async-start(bf16[8,216,512]{2,1,0:T(8,128)(2,1)} %shard_map.100), calls=%async_computation.4 | async-start | bytes 3538944 | tf_op jit(solution)/shard_map/all_to_all | solution.py:609
  189.1 13.6 %collective-permute-start.20 = (bf16[2,2,16,4096]{3,2,1,0:T(8,128)(2,1)S(1)}, bf16[2,2,16,4096]{3,2,1,0:T(8,128)(2,1)S(1)}, u32[]{:S(2)}, u32[]{:S(2)}) collective-permute-start(bf16[2,2,16,4096]{3,2,1,0:T(8,128)(2,1)S(1)} %shard_map.103.refs_0_.b0), channel_id=1, source_target_pairs={{0,32},{32,64},{64,96},{96,0},{1,33},{33,65},{65,97},{97,1},{2,34}... | collective-permute-start | bytes 1572872 | tf_op jit(solution)/shard_map/ppermute | solution.py:608
  189.2 21.6 %collective-permute-start.21 = (bf16[2,2,16,4096]{3,2,1,0:T(8,128)(2,1)S(1)}, bf16[2,2,16,4096]{3,2,1,0:T(8,128)(2,1)S(1)}, u32[]{:S(2)}, u32[]{:S(2)}) collective-permute-start(bf16[2,2,16,4096]{3,2,1,0:T(8,128)(2,1)S(1)} %shard_map.103.refs_0_.b0), channel_id=1, source_target_pairs={{0,64},{32,96},{64,0},{96,32},{1,65},{33,97},{65,1},{97,33},{2,66}... | collective-permute-start | bytes 1572872 | tf_op jit(solution)/shard_map/ppermute | solution.py:608
  190.2 24.4 %collective-permute-start.22 = (bf16[2,2,16,4096]{3,2,1,0:T(8,128)(2,1)S(1)}, bf16[2,2,16,4096]{3,2,1,0:T(8,128)(2,1)S(1)}, u32[]{:S(2)}, u32[]{:S(2)}) collective-permute-start(bf16[2,2,16,4096]{3,2,1,0:T(8,128)(2,1)S(1)} %shard_map.103.refs_0_.b0), channel_id=1, source_target_pairs={{0,96},{32,0},{64,32},{96,64},{1,97},{33,1},{65,33},{97,65},{2,98}... | collective-permute-start | bytes 1572872 | tf_op jit(solution)/shard_map/ppermute | solution.py:608
  (27 other events, 180.0 us)

commit v6 on v5

--- a/solution.py
+++ b/solution.py
@@ -31,13 +31,11 @@
     def tap(g, ky, kx):
         return (tap_of(g, ky, kx), g, ky, kx)
 
-    pairs = [((0, -1, 0, 0), tap(0, 0, 0)), (tap(1, 0, 0), tap(2, 0, 0))]
-    for ky in (0, -1, 1):
-        for g in range(3):
-            pairs.append((tap(g, ky, -1), tap(g, ky, 1)))
-    for ky in (-1, 1):
-        pairs.append((tap(0, ky, 0), tap(1, ky, 0)))
-    pairs.append((tap(2, -1, 0), tap(2, 1, 0)))
+    sides = [[(tap(g, ky, -1), tap(g, ky, 1)) for ky in (0, -1, 1)] for g in range(3)]
+    pairs = [((0, -1, 0, 0), tap(0, 0, 0))] + sides[0] + sides[1]
+    pairs += [(tap(1, 0, 0), tap(2, 0, 0))]
+    pairs += [(tap(0, ky, 0), tap(1, ky, 0)) for ky in (-1, 1)]
+    pairs += sides[2] + [(tap(2, -1, 0), tap(2, 1, 0))]
     return pairs
 
 
@@ -136,12 +134,22 @@
 
 
 def forward_kernel(place, x, *refs):
-    blocks, (out, kept, done, acc, out_sem, wt, w_sem) = refs[:8], refs[8:]
+    blocks, (out, kept, xt, done, acc, out_sem, wt, w_sem, turned, x_sem) = refs[:8], refs[8:]
     for n, block in enumerate(blocks):
         c = place[2] if n < 4 else 1 - place[2]
         wt[c, lax.rem(place[0] + 4 - n % 4, 4)] = block[...]
     keep = pltpu.make_async_copy(wt, kept, w_sem)
     keep.start()
+    flat = x[...].reshape(CHIPS * PADDED, K)
+    for n in range(7):
+        for yh in range(2):
+            for core in range(2):
+                lane = (yh * 2 + core) * 128
+                away = jnp.where(place[2] == core, 0, 1)
+                block = flat[n * 256 : (n + 1) * 256, lane : lane + 128]
+                turned[2 * away + yh, :, n * 256 : (n + 1) * 256] = block.T
+    turn_out = pltpu.make_async_copy(turned, xt, x_sem)
+    turn_out.start()
 
     def span(g, ky):
         return max(0, ky * (g + 1)), CHIPS + min(0, ky * (g + 1))
@@ -183,6 +191,7 @@
     for j in range(CHIPS):
         pltpu.make_async_copy(done.at[j], out.at[j], out_sem.at[j]).wait()
     keep.wait()
+    turn_out.wait()
 
 
 def forward(place, x, blocks):
@@ -191,17 +200,20 @@
         out_shape=(
             jax.ShapeDtypeStruct((CHIPS, CELLS, 512), BF16),
             jax.ShapeDtypeStruct(WEIGHTS, BF16),
+            jax.ShapeDtypeStruct((4, 128, CHIPS * PADDED), BF16),
         ),
         in_specs=[SMEM] + [VMEM] * 9,
-        out_specs=(ANY,) * 2,
+        out_specs=(ANY,) * 3,
         scratch_shapes=[
             pltpu.VMEM((CHIPS, CELLS, 512), BF16),
             pltpu.VMEM((10, CHIPS, PADDED, 128), F32),
             pltpu.SemaphoreType.DMA((CHIPS,)),
             pltpu.VMEM(WEIGHTS, BF16),
             pltpu.SemaphoreType.DMA,
+            pltpu.VMEM((4, 128, CHIPS * PADDED), BF16),
+            pltpu.SemaphoreType.DMA,
         ],
-        compiler_params=params(56),
+        compiler_params=params(51),
         cost_estimate=CONV_COST,
     )(place, x, *blocks)
 
@@ -255,24 +267,37 @@
 SPREAD = [pltpu.VMEM((9, CHIPS + 2 * HALO, PADDED, 128), BF16), pltpu.VMEM((CHIPS, PADDED, 128), BF16)]
 
 
+def spread_point(got, point, j):
+    point[j, :CELLS] = got[j, :, :128]
+    point[j, CELLS:] = jnp.zeros((PADDED - CELLS, 128), BF16)
+
+
+def spread_branch(got, moved, column, g, j):
+    d = DILATIONS[g]
+    v = got[j, :, (g + 1) * 128 : (g + 2) * 128]
+    wide = v.astype(F32)
+    minus = jnp.where(column < WIDTH - d, pltpu.roll(wide, CELLS - d, 0), 0.0)
+    plus = jnp.where(column >= d, pltpu.roll(wide, d, 0), 0.0)
+    for kx, part in enumerate((minus.astype(BF16), v, plus.astype(BF16))):
+        moved[3 * g + kx, HALO + j, :CELLS] = part
+        moved[3 * g + kx, HALO + j, CELLS:] = jnp.zeros((PADDED - CELLS, 128), BF16)
+
+
+def spread_edges(moved, g):
+    for n in range(3 * g, 3 * g + 3):
+        moved[n, :HALO] = jnp.zeros((HALO, PADDED, 128), BF16)
+        moved[n, HALO + CHIPS :] = jnp.zeros((HALO, PADDED, 128), BF16)
+
+
 def spread(got, moved, point):
     column = cell_column(CELLS)
-    for n in range(9):
-        moved[n, :HALO] = jnp.zeros((HALO, PADDED, 128), BF16)
-        moved[n, HALO + CHIPS :] = jnp.zeros((HALO, PADDED, 128), BF16)
-    tail = jnp.zeros((PADDED - CELLS, 128), BF16)
+    for g in range(3):
+        spread_edges(moved, g)
 
     def step(j, _):
-        point[j, :CELLS] = got[j, :, :128]
-        point[j, CELLS:] = tail
-        for g, d in enumerate(DILATIONS):
-            v = got[j, :, (g + 1) * 128 : (g + 2) * 128]
-            wide = v.astype(F32)
-            minus = jnp.where(column < WIDTH - d, pltpu.roll(wide, CELLS - d, 0), 0.0)
-            plus = jnp.where(column >= d, pltpu.roll(wide, d, 0), 0.0)
-            for kx, part in enumerate((minus.astype(BF16), v, plus.astype(BF16))):
-                moved[3 * g + kx, HALO + j, :CELLS] = part
-                moved[3 * g + kx, HALO + j, CELLS:] = tail
+        spread_point(got, point, j)
+        for g in range(3):
+            spread_branch(got, moved, column, g, j)
         return 0
 
     lax.fori_loop(0, CHIPS, step, 0)
@@ -287,69 +312,57 @@
     return v.reshape(count * PADDED, 128)
 
 
-def turn_features_kernel(place, x, out):
-    flat = x[...].reshape(CHIPS * PADDED, K)
-    for yh in range(2):
-        for core in range(2):
-            lanes = slice((yh * 2 + core) * 128, (yh * 2 + core + 1) * 128)
-            away = jnp.where(place[2] == core, 0, 1)
-            for n in range(7):
-                block = flat[n * 256 : (n + 1) * 256, lanes]
-                out[2 * away + yh, :, n * 256 : (n + 1) * 256] = block.T
-
-
-def turn_features(place, x):
-    return pl.pallas_call(
-        turn_features_kernel,
-        out_shape=jax.ShapeDtypeStruct((4, 128, CHIPS * PADDED), BF16),
-        in_specs=[SMEM, VMEM],
-        out_specs=VMEM,
-        compiler_params=params(32),
-        cost_estimate=cost(0, 8 << 20),
-    )(place, x)
-
-
-def kernel_grad_kernel(got, xt, keep, send, kept, sent, xs, x_sem, out_sem, moved, point):
+def kernel_grad_kernel(got, xt, keep, send, again, sent, xs, x_sem, g_sem, out_sem, moved, point):
     load = pltpu.make_async_copy(xt, xs, x_sem)
     load.start()
-    spread(got, moved, point)
-    load.wait()
-    left = xs[...].reshape(K, CHIPS * PADDED)
+    copy_got = pltpu.make_async_copy(got, again, g_sem)
+    copy_got.start()
+    column = cell_column(CELLS)
     stores = []
-    for pair in PAIRS:
+    ready = -1
+    for index, pair in enumerate(PAIRS):
+        for g in range(ready + 1, max(tap[1] for tap in pair) + 1):
+            spread_edges(moved, g)
+            for j in range(CHIPS):
+                if g == 0:
+                    spread_point(got, point, j)
+                spread_branch(got, moved, column, g, j)
+            ready = g
+        if index == 0:
+            load.wait()
+        left = xs[...].reshape(K, CHIPS * PADDED)
         right = jnp.concatenate([spread_columns(moved, point, tap, 0, CHIPS) for tap in pair], 1)
         part = jnp.dot(left, right, preferred_element_type=F32).astype(BF16)
         for half, tap in enumerate(pair):
             cols = pl.ds(tap[0] * 128, 128)
             block = part[:, half * 128 : (half + 1) * 128].reshape(2, 2, 8, 16, 128)
-            for n, (local, out) in enumerate(((kept, keep), (sent, send))):
-                for yh in range(2):
-                    local[:, yh, :, cols] = block[n, yh]
-                view = (slice(None), slice(None), slice(None), cols)
-                stores.append(
-                    pltpu.make_async_copy(local.at[view], out.at[view], out_sem.at[n, tap[0]])
-                )
-                stores[-1].start()
+            for yh in range(2):
+                keep[:, yh, :, cols] = block[0, yh]
+                sent[:, yh, :, cols] = block[1, yh]
+            view = (slice(None), slice(None), slice(None), cols)
+            stores.append(pltpu.make_async_copy(sent.at[view], send.at[view], out_sem.at[tap[0]]))
+            stores[-1].start()
     for copy in stores:
         copy.wait()
+    copy_got.wait()
 
 
 def kernel_grad(got, xt):
-    local = pltpu.VMEM((8, 2, 16, COLS), BF16)
     return pl.pallas_call(
         kernel_grad_kernel,
-        out_shape=(jax.ShapeDtypeStruct((8, 2, 16, COLS), BF16),) * 2,
+        out_shape=(jax.ShapeDtypeStruct((8, 2, 16, COLS), BF16),) * 2
+        + (jax.ShapeDtypeStruct((CHIPS, CELLS, 512), BF16),),
         in_specs=[VMEM, ANY],
-        out_specs=(ANY,) * 2,
+        out_specs=(VMEM, ANY, ANY),
         scratch_shapes=[
-            local,
-            local,
+            pltpu.VMEM((8, 2, 16, COLS), BF16),
             pltpu.VMEM((4, 128, CHIPS * PADDED), BF16),
             pltpu.SemaphoreType.DMA,
-            pltpu.SemaphoreType.DMA((2, TAPS)),
+            pltpu.SemaphoreType.DMA,
+            pltpu.SemaphoreType.DMA((TAPS,)),
         ]
         + SPREAD,
-        compiler_params=params(56),
+        compiler_params=params(48),
         cost_estimate=CONV_COST,
     )(got, xt)
 
@@ -576,12 +589,11 @@
     x_send, quarter = lax.optimization_barrier((x_send, quarter))
     x = lax.all_to_all(x_send, ("yh", "x"), 0, 0, tiled=True)
 
-    partial, wt = forward(place, x, blocks)
+    partial, wt, xt = forward(place, x, blocks)
     got = lax.all_to_all(partial, ("yh", "x"), 0, 0, tiled=True)
     proj = proj_weight.reshape(4, 2, 128, 256).transpose(1, 0, 2, 3).reshape(1024, 256)
     projected, d_send, proj_part = middle(got, proj, cotangent.reshape(CELLS, 256))
     dpre = lax.all_to_all(d_send, ("yh", "x"), 0, 0, tiled=True)
-    xt = turn_features(place, x)
 
     core, layer = lax.axis_index("c"), lax.axis_index("z")
     share = halved(proj_part, "c", turn(2, 1), core)
@@ -590,7 +602,7 @@
     share = added_over_y(share)
     dpre, share = lax.optimization_barrier((dpre, share))
 
-    keep, send = kernel_grad(dpre, xt)
+    keep, send, dpre = kernel_grad(dpre, xt)
     g_part = add_cores(keep, swap(send, "c"))
     g_got = lax.all_to_all(g_part.reshape(16, 16, COLS), ("z", "yl", "yh"), 0, 0, tiled=True)
 

time: 223 us -> 218 us (0.978)
  waiting for transfers between devices: 93.6 us -> 101 us
  local copies, waits for them, and re-layouts: 12.5 us -> 5.54 us
  starting transfers between devices: 70.1 us -> 65.9 us
    unnamed x44 -> x18, local copies, waits for them, and re-layouts: 11.6 us -> 5.35 us
    ppermute x3, waiting for transfers between devices: 8.82 us -> 12.3 us  [added_over_y(): total = total + lax.ppermute(sent, ('yl', 'yh'), pairs).astype(F32)]
    ppermute x3, starting transfers between devices: 4.51 us -> 1.54 us  [halved(): return mine + lax.ppermute(theirs.astype(BF16), axis, pairs).astype(F32)]
    ppermute x3, waiting for transfers between devices: 6.27 us -> 8.59 us  [halved(): return mine + lax.ppermute(theirs.astype(BF16), axis, pairs).astype(F32)]
  transfers between devices with their start and end apart: 29 -> 29, of which waited for: 17 -> 18; matrix products, arithmetic and copies ran while one was open for 1% -> 1% of each run, Pallas kernels for 8% -> 8%
where the time goes in v6:
time: 218 us; the launch traced here: 217 us
  waiting for transfers between devices  101 us (46%)
  starting transfers between devices  65.9 us (30%)
  Pallas kernels  42.5 us (19%)
  local copies, waits for them, and re-layouts  5.54 us (3%)
    all_to_all x1, waiting for transfers between devices, shards(): got = lax.all_to_all(partial, ('yh', 'x'), 0, 0, tiled=True)  25 us
    ppermute x3, waiting for transfers between devices, shards(): pairs = [pair] + [lax.ppermute(pair, 'z', turn(4, d)) for d in (1, 2, 3)]  22.5 us
    ppermute x7, starting transfers between devices, swap(): return lax.ppermute(v, axis, turn(2, 1))  12.8 us
    ppermute x3, waiting for transfers between devices, added_over_y(): total = total + lax.ppermute(sent, ('yl', 'yh'), pairs).astype(F32)  12.3 us
    pallas_call x1, Pallas kernels, feature_grad(): pl.pallas_call(feature_grad_kernel, out_shape=jax.ShapeDtypeStruct((CHIPS...  12 us
    ppermute x3, waiting for transfers between devices, shards(): lax.ppermute(quarter, 'z', turn(4, d))  11.6 us
    ppermute x7, waiting for transfers between devices, swap(): return lax.ppermute(v, axis, turn(2, 1))  10.8 us
    pallas_call x1, Pallas kernels, forward(): pl.pallas_call(forward_kernel, out_shape=(jax.ShapeDtypeStruct((CHIPS, CE...  9.89 us
  transfers between devices with their start and end apart: 29, of which 18 were waited for; matrix products, arithmetic and copies ran while one was open for 1% of the time, Pallas kernels for 8%

profile of v6, /device:TPU:1, one launch (start us, length us, event | category | flops | bytes accessed | tf_op | source)
XLA Modules:
  0.0 217.4 jit_solution(1259608669291408410)
XLA Ops:
  14.1 6.3 %all-to-all-start = ((bf16[8,224,512]{2,1,0:T(8,128)(2,1)}), bf16[8,224,512]{2,1,0:T(8,128)(2,1)}, u32[]{:S(2)}, u32[]{:S(2)}) async-start(bf16[8,224,512]{2,1,0:T(8,128)(2,1)} %shard_map.92), calls=%async_computation | async-start | bytes 3670016 | tf_op jit(solution)/shard_map/all_to_all | solution.py:590
  22.0 3.3 %collective-permute-start.4 = (bf16[4,7,16,512]{3,2,1,0:T(8,128)(2,1)S(1)}, bf16[4,7,16,512]{3,2,1,0:T(8,128)(2,1)S(1)}, u32[]{:S(2)}, u32[]{:S(2)}) collective-permute-start(bf16[4,7,16,512]{3,2,1,0:T(8,128)(2,1)S(1)} %shard_map.94.refs_0_), channel_id=1, source_target_pairs={{0,64},{32,96},{64,0},{96,32},{1,65},{33,97},{65,1},{97,33},{2,66}... | collective-permute-start | bytes 1376264 | tf_op jit(solution)/shard_map/ppermute | solution.py:585
  28.7 4.5 %collective-permute-done.3.refs_1_ = bf16[4,7,16,512]{3,2,1,0:T(8,128)(2,1)S(1)} collective-permute-done((bf16[4,7,16,512]{3,2,1,0:T(8,128)(2,1)S(1)}, bf16[4,7,16,512]{3,2,1,0:T(8,128)(2,1)S(1)}, u32[]{:S(2)}, u32[]{:S(2)}) %collective-permute-start.3) | collective-permute-done | bytes 458784 | tf_op jit(solution)/shard_map/ppermute | solution.py:585
  33.2 3.6 %collective-permute-start.7 = (bf16[4,7,16,512]{3,2,1,0:T(8,128)(2,1)S(1)}, bf16[4,7,16,512]{3,2,1,0:T(8,128)(2,1)S(1)}, u32[]{:S(2)}, u32[]{:S(2)}) collective-permute-start(bf16[4,7,16,512]{3,2,1,0:T(8,128)(2,1)S(1)} %collective-permute-done.3.refs_1_), channel_id=1, source_target_pairs={{0,1},{1,0},{2,3},{3,2},{4,5},{5,4},{6,7},{7,6},{8,9},{9,8},{10,11... | collective-permute-start | bytes 1376264 | tf_op jit(solution)/shard_map/ppermute | solution.py:548
  36.8 7.1 %collective-permute-done.4.refs_2_ = bf16[4,7,16,512]{3,2,1,0:T(8,128)(2,1)S(1)} collective-permute-done((bf16[4,7,16,512]{3,2,1,0:T(8,128)(2,1)S(1)}, bf16[4,7,16,512]{3,2,1,0:T(8,128)(2,1)S(1)}, u32[]{:S(2)}, u32[]{:S(2)}) %collective-permute-start.4) | collective-permute-done | bytes 458784 | tf_op jit(solution)/shard_map/ppermute | solution.py:585
  49.4 9.9 %shard_map.95 = (bf16[8,216,512]{2,1,0:T(8,128)(2,1)}, bf16[2,4,4,7,16,512]{5,4,3,2,1,0:T(8,128)(2,1)}, bf16[4,128,1792]{2,1,0:T(8,128)(2,1)}) custom-call(s32[5]{0:T(128)S(1)} %stack.23.place, bf16[8,224,512]{2,1,0:T(8,128)(2,1)} %all-to-all-done.x, bf16[4,7,16,512]{3,2,1,0:T(8,128)(2,1)S(1)} %shard_map.94.refs_0_, ...), custom_call_target="tpu_custom_call" | custom-call | flops 6341787648 | bytes 8388608 | tf_op jit(solution)/shard_map/pallas_call | solution.py:198
  59.3 6.8 %all-to-all-start.1 = ((bf16[8,216,512]{2,1,0:T(8,128)(2,1)}), bf16[8,216,512]{2,1,0:T(8,128)(2,1)S(1)}, u32[]{:S(2)}, u32[]{:S(2)}) async-start(bf16[8,216,512]{2,1,0:T(8,128)(2,1)} %get-tuple-element.35), calls=%async_computation.1 | async-start | bytes 3538944 | tf_op jit(solution)/shard_map/all_to_all | solution.py:593
  66.2 25.0 %all-to-all-done.1.got = bf16[8,216,512]{2,1,0:T(8,128)(2,1)S(1)} async-done(((bf16[8,216,512]{2,1,0:T(8,128)(2,1)}), bf16[8,216,512]{2,1,0:T(8,128)(2,1)S(1)}, u32[]{:S(2)}, u32[]{:S(2)}) %all-to-all-start.1) | async-done | bytes 1769504 | tf_op jit(solution)/shard_map/all_to_all | solution.py:593
  94.6 4.9 %all-to-all-start.2 = ((bf16[8,216,512]{2,1,0:T(8,128)(2,1)}), bf16[8,216,512]{2,1,0:T(8,128)(2,1)S(1)}, u32[]{:S(2)}, u32[]{:S(2)}) async-start(bf16[8,216,512]{2,1,0:T(8,128)(2,1)} %copy-done.1), calls=%async_computation.2 | async-start | bytes 3538944 | tf_op jit(solution)/shard_map/all_to_all | solution.py:596
  100.7 4.8 %collective-permute-done.11 = bf16[256,256]{1,0:T(8,128)(2,1)S(1)} collective-permute-done((bf16[256,256]{1,0:T(8,128)(2,1)S(1)}, bf16[256,256]{1,0:T(8,128)(2,1)S(1)}, u32[]{:S(2)}, u32[]{:S(2)}) %collective-permute-start.11) | collective-permute-done | bytes 131104 | tf_op jit(solution)/shard_map/ppermute | solution.py:563
  106.0 3.8 %collective-permute-done.12 = bf16[128,256]{1,0:T(8,128)(2,1)S(1)} collective-permute-done((bf16[128,256]{1,0:T(8,128)(2,1)S(1)}, bf16[128,256]{1,0:T(8,128)(2,1)S(1)}, u32[]{:S(2)}, u32[]{:S(2)}) %collective-permute-start.12) | collective-permute-done | bytes 65568 | tf_op jit(solution)/shard_map/ppermute | solution.py:563
  109.9 3.0 %collective-permute-start.15 = (bf16[128,256]{1,0:T(8,128)(2,1)S(1)}, bf16[128,256]{1,0:T(8,128)(2,1)S(1)}, u32[]{:S(2)}, u32[]{:S(2)}) collective-permute-start(bf16[128,256]{1,0:T(8,128)(2,1)S(1)} %fusion.1), channel_id=1, source_target_pairs={{0,24},{8,16},{16,8},{24,0},{1,25},{9,17},{17,9},{25,1},{2,26},{10... | collective-permute-start | bytes 196616 | tf_op jit(solution)/shard_map/ppermute | solution.py:574
  114.2 6.5 %collective-permute-done.15 = bf16[128,256]{1,0:T(8,128)(2,1)S(1)} collective-permute-done((bf16[128,256]{1,0:T(8,128)(2,1)S(1)}, bf16[128,256]{1,0:T(8,128)(2,1)S(1)}, u32[]{:S(2)}, u32[]{:S(2)}) %collective-permute-start.15) | collective-permute-done | bytes 65568 | tf_op jit(solution)/shard_map/ppermute | solution.py:574
  120.7 5.8 %collective-permute-done.13 = bf16[128,256]{1,0:T(8,128)(2,1)S(1)} collective-permute-done((bf16[128,256]{1,0:T(8,128)(2,1)S(1)}, bf16[128,256]{1,0:T(8,128)(2,1)S(1)}, u32[]{:S(2)}, u32[]{:S(2)}) %collective-permute-start.13) | collective-permute-done | bytes 65568 | tf_op jit(solution)/shard_map/ppermute | solution.py:574
  126.5 9.8 %shard_map.97 = (bf16[8,2,16,3584]{3,2,1,0:T(8,128)(2,1)S(1)}, bf16[8,2,16,3584]{3,2,1,0:T(8,128)(2,1)}, bf16[8,216,512]{2,1,0:T(8,128)(2,1)S(1)}) custom-call(bf16[8,216,512]{2,1,0:T(8,128)(2,1)S(1)} %all-to-all-done.2.got, bf16[4,128,1792]{2,1,0:T(8,128)(2,1)} %get-tuple-element.40.xt), custom_call_target="tpu_custom_call" | custom-call | flops 6341787648 | bytes 8388608 | tf_op jit(solution)/shard_map/pallas_call | solution.py:351
  137.0 3.6 %collective-permute-done.16.other = bf16[8,2,16,3584]{3,2,1,0:T(8,128)(2,1)S(1)} collective-permute-done((bf16[8,2,16,3584]{3,2,1,0:T(8,128)(2,1)}, bf16[8,2,16,3584]{3,2,1,0:T(8,128)(2,1)S(1)}, u32[]{:S(2)}, u32[]{:S(2)}) %collective-permute-start.16) | collective-permute-done | bytes 1835040 | tf_op jit(solution)/shard_map/ppermute | solution.py:548
  142.3 3.7 %all-to-all-start.3 = ((bf16[16,16,3584]{2,1,0:T(8,128)(2,1)}), bf16[16,16,3584]{2,1,0:T(8,128)(2,1)S(1)}, u32[]{:S(2)}, u32[]{:S(2)}) async-start(bf16[16,16,3584]{2,1,0:T(8,128)(2,1)} %bitcast.16), calls=%async_computation.3 | async-start | bytes 3670016 | tf_op jit(solution)/shard_map/all_to_all | solution.py:607
  146.0 12.0 %shard_map.99 = bf16[8,216,512]{2,1,0:T(8,128)(2,1)} custom-call(bf16[8,216,512]{2,1,0:T(8,128)(2,1)} %copy-done.6, bf16[2,4,4,7,16,512]{5,4,3,2,1,0:T(8,128)(2,1)} %get-tuple-element.45.kept), custom_call_target="tpu_custom_call" | custom-call | flops 6341787648 | bytes 8388608 | tf_op jit(solution)/shard_map/pallas_call | solution.py:423
  166.3 3.7 %all-to-all-done.3.got = bf16[16,16,3584]{2,1,0:T(8,128)(2,1)S(1)} async-done(((bf16[16,16,3584]{2,1,0:T(8,128)(2,1)}), bf16[16,16,3584]{2,1,0:T(8,128)(2,1)S(1)}, u32[]{:S(2)}, u32[]{:S(2)}) %all-to-all-start.3) | async-done | bytes 1835040 | tf_op jit(solution)/shard_map/all_to_all | solution.py:607
  171.3 4.9 %collective-permute-done.19.other = bf16[2,16,3584]{2,1,0:T(8,128)(2,1)S(1)} collective-permute-done((bf16[2,16,3584]{2,1,0:T(8,128)(2,1)S(1)}, bf16[2,16,3584]{2,1,0:T(8,128)(2,1)S(1)}, u32[]{:S(2)}, u32[]{:S(2)}) %collective-permute-start.19) | collective-permute-done | bytes 229408 | tf_op jit(solution)/shard_map/ppermute | solution.py:548
  176.3 7.6 %all-to-all-start.4 = ((bf16[8,216,512]{2,1,0:T(8,128)(2,1)}), bf16[8,216,512]{2,1,0:T(8,128)(2,1)S(1)}, u32[]{:S(2)}, u32[]{:S(2)}) async-start(bf16[8,216,512]{2,1,0:T(8,128)(2,1)} %shard_map.99), calls=%async_computation.4 | async-start | bytes 3538944 | tf_op jit(solution)/shard_map/all_to_all | solution.py:621
  186.7 10.7 %collective-permute-done.20.refs_1_.b1 = bf16[2,2,16,4096]{3,2,1,0:T(8,128)(2,1)S(1)} collective-permute-done((bf16[2,2,16,4096]{3,2,1,0:T(8,128)(2,1)S(1)}, bf16[2,2,16,4096]{3,2,1,0:T(8,128)(2,1)S(1)}, u32[]{:S(2)}, u32[]{:S(2)}) %collective-permute-start.20) | collective-permute-done | bytes 524320 | tf_op jit(solution)/shard_map/ppermute | solution.py:620
  197.3 9.0 %collective-permute-done.21.refs_2_.b2 = bf16[2,2,16,4096]{3,2,1,0:T(8,128)(2,1)S(1)} collective-permute-done((bf16[2,2,16,4096]{3,2,1,0:T(8,128)(2,1)S(1)}, bf16[2,2,16,4096]{3,2,1,0:T(8,128)(2,1)S(1)}, u32[]{:S(2)}, u32[]{:S(2)}) %collective-permute-start.21) | collective-permute-done | bytes 524320 | tf_op jit(solution)/shard_map/ppermute | solution.py:620
  206.3 2.9 %collective-permute-done.22.refs_3_.b3 = bf16[2,2,16,4096]{3,2,1,0:T(8,128)(2,1)S(1)} collective-permute-done((bf16[2,2,16,4096]{3,2,1,0:T(8,128)(2,1)S(1)}, bf16[2,2,16,4096]{3,2,1,0:T(8,128)(2,1)S(1)}, u32[]{:S(2)}, u32[]{:S(2)}) %collective-permute-start.22) | collective-permute-done | bytes 524320 | tf_op jit(solution)/shard_map/ppermute | solution.py:620
  (78 shorter events, 53.2 us)
Async XLA Ops:
  3.9 7.1 %collective-permute-start = (bf16[7,16,512]{2,1,0:T(8,128)(2,1)S(1)}, bf16[7,16,512]{2,1,0:T(8,128)(2,1)S(1)}, u32[]{:S(2)}, u32[]{:S(2)}) collective-permute-start(bf16[7,16,512]{2,1,0:T(8,128)(2,1)S(1)} %get-tuple-element.31), channel_id=1, source_target_pairs={{0,2},{2,4},{4,6},{6,0},{1,3},{3,5},{5,7},{7,1},{8,10},{10,12},{12... | collective-permute-start | bytes 344072 | tf_op jit(solution)/shard_map/ppermute | solution.py:583
  6.1 7.5 %collective-permute-start.1 = (bf16[7,16,512]{2,1,0:T(8,128)(2,1)S(1)}, bf16[7,16,512]{2,1,0:T(8,128)(2,1)S(1)}, u32[]{:S(2)}, u32[]{:S(2)}) collective-permute-start(bf16[7,16,512]{2,1,0:T(8,128)(2,1)S(1)} %get-tuple-element.32), channel_id=1, source_target_pairs={{0,4},{2,6},{4,0},{6,2},{1,5},{3,7},{5,1},{7,3},{8,12},{10,14},{12... | collective-permute-start | bytes 344072 | tf_op jit(solution)/shard_map/ppermute | solution.py:583
  8.5 5.0 %collective-permute-start.2 = (bf16[7,16,512]{2,1,0:T(8,128)(2,1)S(1)}, bf16[7,16,512]{2,1,0:T(8,128)(2,1)S(1)}, u32[]{:S(2)}, u32[]{:S(2)}) collective-permute-start(bf16[7,16,512]{2,1,0:T(8,128)(2,1)S(1)} %get-tuple-element.33), channel_id=1, source_target_pairs={{0,6},{2,0},{4,2},{6,4},{1,7},{3,1},{5,3},{7,5},{8,14},{10,8},{12,... | collective-permute-start | bytes 344072 | tf_op jit(solution)/shard_map/ppermute | solution.py:583
  14.1 34.7 %all-to-all-start = ((bf16[8,224,512]{2,1,0:T(8,128)(2,1)}), bf16[8,224,512]{2,1,0:T(8,128)(2,1)}, u32[]{:S(2)}, u32[]{:S(2)}) async-start(bf16[8,224,512]{2,1,0:T(8,128)(2,1)} %shard_map.92), calls=%async_computation | async-start | bytes 3670016 | tf_op jit(solution)/shard_map/all_to_all | solution.py:590
  20.4 12.8 %collective-permute-start.3 = (bf16[4,7,16,512]{3,2,1,0:T(8,128)(2,1)S(1)}, bf16[4,7,16,512]{3,2,1,0:T(8,128)(2,1)S(1)}, u32[]{:S(2)}, u32[]{:S(2)}) collective-permute-start(bf16[4,7,16,512]{3,2,1,0:T(8,128)(2,1)S(1)} %shard_map.94.refs_0_), channel_id=1, source_target_pairs={{0,32},{32,64},{64,96},{96,0},{1,33},{33,65},{65,97},{97,1},{2,34}... | collective-permute-start | bytes 1376264 | tf_op jit(solution)/shard_map/ppermute | solution.py:585
  22.0 21.9 %collective-permute-start.4 = (bf16[4,7,16,512]{3,2,1,0:T(8,128)(2,1)S(1)}, bf16[4,7,16,512]{3,2,1,0:T(8,128)(2,1)S(1)}, u32[]{:S(2)}, u32[]{:S(2)}) collective-permute-start(bf16[4,7,16,512]{3,2,1,0:T(8,128)(2,1)S(1)} %shard_map.94.refs_0_), channel_id=1, source_target_pairs={{0,64},{32,96},{64,0},{96,32},{1,65},{33,97},{65,1},{97,33},{2,66}... | collective-permute-start | bytes 1376264 | tf_op jit(solution)/shard_map/ppermute | solution.py:585
  25.3 21.3 %collective-permute-start.5 = (bf16[4,7,16,512]{3,2,1,0:T(8,128)(2,1)S(1)}, bf16[4,7,16,512]{3,2,1,0:T(8,128)(2,1)S(1)}, u32[]{:S(2)}, u32[]{:S(2)}) collective-permute-start(bf16[4,7,16,512]{3,2,1,0:T(8,128)(2,1)S(1)} %shard_map.94.refs_0_), channel_id=1, source_target_pairs={{0,96},{32,0},{64,32},{96,64},{1,97},{33,1},{65,33},{97,65},{2,98}... | collective-permute-start | bytes 1376264 | tf_op jit(solution)/shard_map/ppermute | solution.py:585
  26.0 20.6 %collective-permute-start.6 = (bf16[4,7,16,512]{3,2,1,0:T(8,128)(2,1)S(1)}, bf16[4,7,16,512]{3,2,1,0:T(8,128)(2,1)S(1)}, u32[]{:S(2)}, u32[]{:S(2)}) collective-permute-start(bf16[4,7,16,512]{3,2,1,0:T(8,128)(2,1)S(1)} %shard_map.94.refs_0_), channel_id=1, source_target_pairs={{0,1},{1,0},{2,3},{3,2},{4,5},{5,4},{6,7},{7,6},{8,9},{9,8},{10,11... | collective-permute-start | bytes 1376264 | tf_op jit(solution)/shard_map/ppermute | solution.py:548
  33.2 13.4 %collective-permute-start.7 = (bf16[4,7,16,512]{3,2,1,0:T(8,128)(2,1)S(1)}, bf16[4,7,16,512]{3,2,1,0:T(8,128)(2,1)S(1)}, u32[]{:S(2)}, u32[]{:S(2)}) collective-permute-start(bf16[4,7,16,512]{3,2,1,0:T(8,128)(2,1)S(1)} %collective-permute-done.3.refs_1_), channel_id=1, source_target_pairs={{0,1},{1,0},{2,3},{3,2},{4,5},{5,4},{6,7},{7,6},{8,9},{9,8},{10,11... | collective-permute-start | bytes 1376264 | tf_op jit(solution)/shard_map/ppermute | solution.py:548
  59.3 31.9 %all-to-all-start.1 = ((bf16[8,216,512]{2,1,0:T(8,128)(2,1)}), bf16[8,216,512]{2,1,0:T(8,128)(2,1)S(1)}, u32[]{:S(2)}, u32[]{:S(2)}) async-start(bf16[8,216,512]{2,1,0:T(8,128)(2,1)} %get-tuple-element.35), calls=%async_computation.1 | async-start | bytes 3538944 | tf_op jit(solution)/shard_map/all_to_all | solution.py:593
  93.7 5.8 %collective-permute-start.10 = (bf16[512,256]{1,0:T(8,128)(2,1)S(1)}, bf16[512,256]{1,0:T(8,128)(2,1)}, u32[]{:S(2)}, u32[]{:S(2)}) collective-permute-start(bf16[512,256]{1,0:T(8,128)(2,1)S(1)} %dynamic-slice_convert_fusion), channel_id=1, source_target_pairs={{0,1},{1,0},{2,3},{3,2},{4,5},{5,4},{6,7},{7,6},{8,9},{9,8},{10,11... | collective-permute-start | bytes 786440 | tf_op jit(solution)/shard_map/ppermute | solution.py:563
  94.6 31.9 %all-to-all-start.2 = ((bf16[8,216,512]{2,1,0:T(8,128)(2,1)}), bf16[8,216,512]{2,1,0:T(8,128)(2,1)S(1)}, u32[]{:S(2)}, u32[]{:S(2)}) async-start(bf16[8,216,512]{2,1,0:T(8,128)(2,1)} %copy-done.1), calls=%async_computation.2 | async-start | bytes 3538944 | tf_op jit(solution)/shard_map/all_to_all | solution.py:596
  100.5 4.9 %collective-permute-start.11 = (bf16[256,256]{1,0:T(8,128)(2,1)S(1)}, bf16[256,256]{1,0:T(8,128)(2,1)S(1)}, u32[]{:S(2)}, u32[]{:S(2)}) collective-permute-start(bf16[256,256]{1,0:T(8,128)(2,1)S(1)} %dynamic-slice_convert_fusion.1), channel_id=1, source_target_pairs={{0,32},{32,0},{64,96},{96,64},{1,33},{33,1},{65,97},{97,65},{2,34}... | collective-permute-start | bytes 393224 | tf_op jit(solution)/shard_map/ppermute | solution.py:563
  109.9 10.8 %collective-permute-start.15 = (bf16[128,256]{1,0:T(8,128)(2,1)S(1)}, bf16[128,256]{1,0:T(8,128)(2,1)S(1)}, u32[]{:S(2)}, u32[]{:S(2)}) collective-permute-start(bf16[128,256]{1,0:T(8,128)(2,1)S(1)} %fusion.1), channel_id=1, source_target_pairs={{0,24},{8,16},{16,8},{24,0},{1,25},{9,17},{17,9},{25,1},{2,26},{10... | collective-permute-start | bytes 196616 | tf_op jit(solution)/shard_map/ppermute | solution.py:574
  112.9 7.8 %collective-permute-start.14 = (bf16[128,256]{1,0:T(8,128)(2,1)S(1)}, bf16[128,256]{1,0:T(8,128)(2,1)S(1)}, u32[]{:S(2)}, u32[]{:S(2)}) collective-permute-start(bf16[128,256]{1,0:T(8,128)(2,1)S(1)} %fusion.1), channel_id=1, source_target_pairs={{0,16},{8,24},{16,0},{24,8},{1,17},{9,25},{17,1},{25,9},{2,18},{10... | collective-permute-start | bytes 196616 | tf_op jit(solution)/shard_map/ppermute | solution.py:574
  112.9 13.6 %collective-permute-start.13 = (bf16[128,256]{1,0:T(8,128)(2,1)S(1)}, bf16[128,256]{1,0:T(8,128)(2,1)S(1)}, u32[]{:S(2)}, u32[]{:S(2)}) collective-permute-start(bf16[128,256]{1,0:T(8,128)(2,1)S(1)} %fusion.1), channel_id=1, source_target_pairs={{0,8},{8,0},{16,24},{24,16},{1,9},{9,1},{17,25},{25,17},{2,10},{10... | collective-permute-start | bytes 196616 | tf_op jit(solution)/shard_map/ppermute | solution.py:574
  142.3 27.8 %all-to-all-start.3 = ((bf16[16,16,3584]{2,1,0:T(8,128)(2,1)}), bf16[16,16,3584]{2,1,0:T(8,128)(2,1)S(1)}, u32[]{:S(2)}, u32[]{:S(2)}) async-start(bf16[16,16,3584]{2,1,0:T(8,128)(2,1)} %bitcast.16), calls=%async_computation.3 | async-start | bytes 3670016 | tf_op jit(solution)/shard_map/all_to_all | solution.py:607
  161.6 4.7 %collective-permute-start.18 = (bf16[128,256]{1,0:T(8,128)(2,1)S(1)}, bf16[128,256]{1,0:T(8,128)(2,1)S(1)}, u32[]{:S(2)}, u32[]{:S(2)}) collective-permute-start(bf16[128,256]{1,0:T(8,128)(2,1)S(1)} %fusion), channel_id=1, source_target_pairs={{0,6},{2,4},{4,2},{6,0},{1,7},{3,5},{5,3},{7,1},{8,14},{10,12},{12... | collective-permute-start | bytes 196616 | tf_op jit(solution)/shard_map/ppermute | solution.py:567
  170.3 6.0 %collective-permute-start.19 = (bf16[2,16,3584]{2,1,0:T(8,128)(2,1)S(1)}, bf16[2,16,3584]{2,1,0:T(8,128)(2,1)S(1)}, u32[]{:S(2)}, u32[]{:S(2)}) collective-permute-start(bf16[2,16,3584]{2,1,0:T(8,128)(2,1)S(1)} %shard_map.100.mine), channel_id=1, source_target_pairs={{0,16},{16,0},{1,17},{17,1},{2,18},{18,2},{3,19},{19,3},{4,20},{20... | collective-permute-start | bytes 688136 | tf_op jit(solution)/shard_map/ppermute | solution.py:548
  176.3 40.0 %all-to-all-start.4 = ((bf16[8,216,512]{2,1,0:T(8,128)(2,1)}), bf16[8,216,512]{2,1,0:T(8,128)(2,1)S(1)}, u32[]{:S(2)}, u32[]{:S(2)}) async-start(bf16[8,216,512]{2,1,0:T(8,128)(2,1)} %shard_map.99), calls=%async_computation.4 | async-start | bytes 3538944 | tf_op jit(solution)/shard_map/all_to_all | solution.py:621
  183.9 13.4 %collective-permute-start.20 = (bf16[2,2,16,4096]{3,2,1,0:T(8,128)(2,1)S(1)}, bf16[2,2,16,4096]{3,2,1,0:T(8,128)(2,1)S(1)}, u32[]{:S(2)}, u32[]{:S(2)}) collective-permute-start(bf16[2,2,16,4096]{3,2,1,0:T(8,128)(2,1)S(1)} %shard_map.102.refs_0_.b0), channel_id=1, source_target_pairs={{0,32},{32,64},{64,96},{96,0},{1,33},{33,65},{65,97},{97,1},{2,34}... | collective-permute-start | bytes 1572872 | tf_op jit(solution)/shard_map/ppermute | solution.py:620
  184.0 22.3 %collective-permute-start.21 = (bf16[2,2,16,4096]{3,2,1,0:T(8,128)(2,1)S(1)}, bf16[2,2,16,4096]{3,2,1,0:T(8,128)(2,1)S(1)}, u32[]{:S(2)}, u32[]{:S(2)}) collective-permute-start(bf16[2,2,16,4096]{3,2,1,0:T(8,128)(2,1)S(1)} %shard_map.102.refs_0_.b0), channel_id=1, source_target_pairs={{0,64},{32,96},{64,0},{96,32},{1,65},{33,97},{65,1},{97,33},{2,66}... | collective-permute-start | bytes 1572872 | tf_op jit(solution)/shard_map/ppermute | solution.py:620
  185.5 23.7 %collective-permute-start.22 = (bf16[2,2,16,4096]{3,2,1,0:T(8,128)(2,1)S(1)}, bf16[2,2,16,4096]{3,2,1,0:T(8,128)(2,1)S(1)}, u32[]{:S(2)}, u32[]{:S(2)}) collective-permute-start(bf16[2,2,16,4096]{3,2,1,0:T(8,128)(2,1)S(1)} %shard_map.102.refs_0_.b0), channel_id=1, source_target_pairs={{0,96},{32,0},{64,32},{96,64},{1,97},{33,1},{65,33},{97,65},{2,98}... | collective-permute-start | bytes 1572872 | tf_op jit(solution)/shard_map/ppermute | solution.py:620
  209.8 4.9 %collective-permute-start.23 = (bf16[512,256]{1,0:T(8,128)(2,1)S(1)}, bf16[512,256]{1,0:T(8,128)(2,1)S(1)}, u32[]{:S(2)}, u32[]{:S(2)}) collective-permute-start(bf16[512,256]{1,0:T(8,128)(2,1)S(1)} %shard_map.104.mine), channel_id=1, source_target_pairs={{0,1},{1,0},{2,3},{3,2},{4,5},{5,4},{6,7},{7,6},{8,9},{9,8},{10,11... | collective-permute-start | bytes 786440 | tf_op jit(solution)/shard_map/ppermute | solution.py:548
  (14 other events, 74.6 us)

commit v7 on v6

--- a/solution.py
+++ b/solution.py
@@ -451,8 +451,12 @@
     )(mine, other, proj)
 
 
+def side_of(refs, d, l):
+    return refs[2 + l] if d == 2 else refs[(0, 1, 2, 4)[d]].at[l]
+
+
 def place_grads_kernel(place, *refs):
-    point, atrous = refs[4], refs[5]
+    point, atrous = refs[5], refs[6]
     z, yl = place[0], place[3]
     for d in range(4):
         for l in range(2):
@@ -461,7 +465,7 @@
             for yh in range(2):
                 cols = slice(yh * 128, (yh + 1) * 128)
                 for t in range(TAPS):
-                    part = refs[d][l, yh, :, t * 128 : (t + 1) * 128].astype(F32) * 0.125
+                    part = side_of(refs, d, l)[yh, :, t * 128 : (t + 1) * 128].astype(F32) * 0.125
                     if t == 0:
                         point[rows, cols] = part
                     else:
@@ -475,14 +479,15 @@
             jax.ShapeDtypeStruct((128, 256), F32),
             jax.ShapeDtypeStruct((27, 128, 256), F32),
         ),
-        in_specs=[SMEM] + [VMEM] * 4,
+        in_specs=[SMEM] + [VMEM] * 5,
         out_specs=(VMEM,) * 2,
         compiler_params=params(40),
     )(place, *blocks)
 
 
-def proj_half_kernel(place, b0, b1, b2, b3, out):
-    for d, block in enumerate((b0, b1, b2, b3)):
+def proj_half_kernel(place, *refs):
+    out = refs[5]
+    for d in range(4):
         z = lax.rem(place[0] + 4 - d, 4)
         row = gray(z) * 256 + (z >> 1) * 128
         for n in range(2):
@@ -490,14 +495,14 @@
                 for half in range(2):
                     at = pl.multiple_of(row + half * 64 + n * 32 + yh * 16, 16)
                     lane = COLS + half * 256
-                    out[pl.ds(at, 16), :] = block[n, yh, :, lane : lane + 256]
+                    out[pl.ds(at, 16), :] = side_of(refs, d, n)[yh, :, lane : lane + 256]
 
 
 def proj_half(place, blocks):
     return pl.pallas_call(
         proj_half_kernel,
         out_shape=jax.ShapeDtypeStruct((512, 256), BF16),
-        in_specs=[SMEM] + [VMEM] * 4,
+        in_specs=[SMEM] + [VMEM] * 5,
         out_specs=VMEM,
         compiler_params=params(24),
     )(place, *blocks)
@@ -617,7 +622,9 @@
     swapped = swap(g_sum, "yl")
     back, swapped = lax.optimization_barrier((back, swapped))
     pair = pack_sums(g_sum, swapped, share)
-    pairs = [pair] + [lax.ppermute(pair, "z", turn(4, d)) for d in (1, 2, 3)]
+    below, above = lax.ppermute(pair, "z", turn(4, 1)), lax.ppermute(pair, "z", turn(4, 3))
+    opposite = [lax.ppermute(above[0], "z", turn(4, 3)), lax.ppermute(below[1], "z", turn(4, 1))]
+    pairs = [pair, below, *opposite, above]
     input_grad = join_features(lax.all_to_all(back, ("yh", "x"), 0, 0, tiled=True))
     half = proj_half(place, pairs)
     grad_point, grad_atrous = place_grads(place, pairs)

time: 218 us -> 212 us (0.972)
  waiting for transfers between devices: 101 us -> 92.1 us
  starting transfers between devices: 65.9 us -> 69.4 us
    ppermute x3 -> x4, waiting for transfers between devices: 22.5 us -> 8.95 us  [the longest x1 3.4 us: shards(): lax.ppermute(below[1], 'z', turn(4, 1))]
    all_to_all x1, waiting for transfers between devices: 0.01 us -> 4.24 us  [shards(): lax.all_to_all(back, ('yh', 'x'), 0, 0, tiled=True)]
    ppermute x7, starting transfers between devices: 12.8 us -> 15.3 us  [swap(): return lax.ppermute(v, axis, turn(2, 1))]
  transfers between devices with their start and end apart: 29 -> 30, of which waited for: 18 -> 19; matrix products, arithmetic and copies ran while one was open for 1% -> 1% of each run, Pallas kernels for 8% -> 9%
where the time goes in v7:
time: 212 us
  waiting for transfers between devices  92.1 us (43%)
  starting transfers between devices  69.4 us (33%)
  Pallas kernels  42.5 us (20%)
  local copies, waits for them, and re-layouts  5.58 us (3%)
    all_to_all x1, waiting for transfers between devices, shards(): got = lax.all_to_all(partial, ('yh', 'x'), 0, 0, tiled=True)  25 us
    ppermute x7, starting transfers between devices, swap(): return lax.ppermute(v, axis, turn(2, 1))  15.3 us
    ppermute x3, waiting for transfers between devices, added_over_y(): total = total + lax.ppermute(sent, ('yl', 'yh'), pairs).astype(F32)  12.3 us
    pallas_call x1, Pallas kernels, feature_grad(): pl.pallas_call(feature_grad_kernel, out_shape=jax.ShapeDtypeStruct((CHIPS...  12 us
    ppermute x3, waiting for transfers between devices, shards(): lax.ppermute(quarter, 'z', turn(4, d))  11.6 us
    ppermute x7, waiting for transfers between devices, swap(): return lax.ppermute(v, axis, turn(2, 1))  10.8 us
    pallas_call x1, Pallas kernels, forward(): pl.pallas_call(forward_kernel, out_shape=(jax.ShapeDtypeStruct((CHIPS, CE...  9.9 us
    pallas_call x1, Pallas kernels, kernel_grad(): pl.pallas_call(kernel_grad_kernel, out_shape=(jax.ShapeDtypeStruct((8, 2,...  9.85 us
  transfers between devices with their start and end apart: 30, of which 19 were waited for; matrix products, arithmetic and copies ran while one was open for 1% of the time, Pallas kernels for 9%

profile of v7, /device:TPU:1, one launch (start us, length us, event | category | flops | bytes accessed | tf_op | source)
XLA Modules:
  0.0 211.6 jit_solution(8857027121292799130)
XLA Ops:
  14.1 6.3 %all-to-all-start = ((bf16[8,224,512]{2,1,0:T(8,128)(2,1)}), bf16[8,224,512]{2,1,0:T(8,128)(2,1)}, u32[]{:S(2)}, u32[]{:S(2)}) async-start(bf16[8,224,512]{2,1,0:T(8,128)(2,1)} %shard_map.92), calls=%async_computation | async-start | bytes 3670016 | tf_op jit(solution)/shard_map/all_to_all | solution.py:595
  22.0 3.3 %collective-permute-start.4 = (bf16[4,7,16,512]{3,2,1,0:T(8,128)(2,1)S(1)}, bf16[4,7,16,512]{3,2,1,0:T(8,128)(2,1)S(1)}, u32[]{:S(2)}, u32[]{:S(2)}) collective-permute-start(bf16[4,7,16,512]{3,2,1,0:T(8,128)(2,1)S(1)} %shard_map.94.refs_0_), channel_id=1, source_target_pairs={{0,64},{32,96},{64,0},{96,32},{1,65},{33,97},{65,1},{97,33},{2,66}... | collective-permute-start | bytes 1376264 | tf_op jit(solution)/shard_map/ppermute | solution.py:590
  28.7 4.5 %collective-permute-done.3.refs_1_ = bf16[4,7,16,512]{3,2,1,0:T(8,128)(2,1)S(1)} collective-permute-done((bf16[4,7,16,512]{3,2,1,0:T(8,128)(2,1)S(1)}, bf16[4,7,16,512]{3,2,1,0:T(8,128)(2,1)S(1)}, u32[]{:S(2)}, u32[]{:S(2)}) %collective-permute-start.3) | collective-permute-done | bytes 458784 | tf_op jit(solution)/shard_map/ppermute | solution.py:590
  33.2 3.6 %collective-permute-start.7 = (bf16[4,7,16,512]{3,2,1,0:T(8,128)(2,1)S(1)}, bf16[4,7,16,512]{3,2,1,0:T(8,128)(2,1)S(1)}, u32[]{:S(2)}, u32[]{:S(2)}) collective-permute-start(bf16[4,7,16,512]{3,2,1,0:T(8,128)(2,1)S(1)} %collective-permute-done.3.refs_1_), channel_id=1, source_target_pairs={{0,1},{1,0},{2,3},{3,2},{4,5},{5,4},{6,7},{7,6},{8,9},{9,8},{10,11... | collective-permute-start | bytes 1376264 | tf_op jit(solution)/shard_map/ppermute | solution.py:553
  36.8 7.1 %collective-permute-done.4.refs_2_ = bf16[4,7,16,512]{3,2,1,0:T(8,128)(2,1)S(1)} collective-permute-done((bf16[4,7,16,512]{3,2,1,0:T(8,128)(2,1)S(1)}, bf16[4,7,16,512]{3,2,1,0:T(8,128)(2,1)S(1)}, u32[]{:S(2)}, u32[]{:S(2)}) %collective-permute-start.4) | collective-permute-done | bytes 458784 | tf_op jit(solution)/shard_map/ppermute | solution.py:590
  49.4 9.9 %shard_map.95 = (bf16[8,216,512]{2,1,0:T(8,128)(2,1)}, bf16[2,4,4,7,16,512]{5,4,3,2,1,0:T(8,128)(2,1)}, bf16[4,128,1792]{2,1,0:T(8,128)(2,1)}) custom-call(s32[5]{0:T(128)S(1)} %stack.23.place, bf16[8,224,512]{2,1,0:T(8,128)(2,1)} %all-to-all-done.x, bf16[4,7,16,512]{3,2,1,0:T(8,128)(2,1)S(1)} %shard_map.94.refs_0_, ...), custom_call_target="tpu_custom_call" | custom-call | flops 6341787648 | bytes 8388608 | tf_op jit(solution)/shard_map/pallas_call | solution.py:198
  59.3 6.8 %all-to-all-start.1 = ((bf16[8,216,512]{2,1,0:T(8,128)(2,1)}), bf16[8,216,512]{2,1,0:T(8,128)(2,1)S(1)}, u32[]{:S(2)}, u32[]{:S(2)}) async-start(bf16[8,216,512]{2,1,0:T(8,128)(2,1)} %get-tuple-element.35), calls=%async_computation.1 | async-start | bytes 3538944 | tf_op jit(solution)/shard_map/all_to_all | solution.py:598
  66.2 25.0 %all-to-all-done.1.got = bf16[8,216,512]{2,1,0:T(8,128)(2,1)S(1)} async-done(((bf16[8,216,512]{2,1,0:T(8,128)(2,1)}), bf16[8,216,512]{2,1,0:T(8,128)(2,1)S(1)}, u32[]{:S(2)}, u32[]{:S(2)}) %all-to-all-start.1) | async-done | bytes 1769504 | tf_op jit(solution)/shard_map/all_to_all | solution.py:598
  94.6 4.9 %all-to-all-start.2 = ((bf16[8,216,512]{2,1,0:T(8,128)(2,1)}), bf16[8,216,512]{2,1,0:T(8,128)(2,1)S(1)}, u32[]{:S(2)}, u32[]{:S(2)}) async-start(bf16[8,216,512]{2,1,0:T(8,128)(2,1)} %copy-done.1), calls=%async_computation.2 | async-start | bytes 3538944 | tf_op jit(solution)/shard_map/all_to_all | solution.py:601
  100.7 4.8 %collective-permute-done.11 = bf16[256,256]{1,0:T(8,128)(2,1)S(1)} collective-permute-done((bf16[256,256]{1,0:T(8,128)(2,1)S(1)}, bf16[256,256]{1,0:T(8,128)(2,1)S(1)}, u32[]{:S(2)}, u32[]{:S(2)}) %collective-permute-start.11) | collective-permute-done | bytes 131104 | tf_op jit(solution)/shard_map/ppermute | solution.py:568
  106.0 3.8 %collective-permute-done.12 = bf16[128,256]{1,0:T(8,128)(2,1)S(1)} collective-permute-done((bf16[128,256]{1,0:T(8,128)(2,1)S(1)}, bf16[128,256]{1,0:T(8,128)(2,1)S(1)}, u32[]{:S(2)}, u32[]{:S(2)}) %collective-permute-start.12) | collective-permute-done | bytes 65568 | tf_op jit(solution)/shard_map/ppermute | solution.py:568
  114.2 6.5 %collective-permute-done.15 = bf16[128,256]{1,0:T(8,128)(2,1)S(1)} collective-permute-done((bf16[128,256]{1,0:T(8,128)(2,1)S(1)}, bf16[128,256]{1,0:T(8,128)(2,1)S(1)}, u32[]{:S(2)}, u32[]{:S(2)}) %collective-permute-start.15) | collective-permute-done | bytes 65568 | tf_op jit(solution)/shard_map/ppermute | solution.py:579
  120.7 5.8 %collective-permute-done.13 = bf16[128,256]{1,0:T(8,128)(2,1)S(1)} collective-permute-done((bf16[128,256]{1,0:T(8,128)(2,1)S(1)}, bf16[128,256]{1,0:T(8,128)(2,1)S(1)}, u32[]{:S(2)}, u32[]{:S(2)}) %collective-permute-start.13) | collective-permute-done | bytes 65568 | tf_op jit(solution)/shard_map/ppermute | solution.py:579
  126.5 9.9 %shard_map.97 = (bf16[8,2,16,3584]{3,2,1,0:T(8,128)(2,1)S(1)}, bf16[8,2,16,3584]{3,2,1,0:T(8,128)(2,1)}, bf16[8,216,512]{2,1,0:T(8,128)(2,1)S(1)}) custom-call(bf16[8,216,512]{2,1,0:T(8,128)(2,1)S(1)} %all-to-all-done.2.got, bf16[4,128,1792]{2,1,0:T(8,128)(2,1)} %get-tuple-element.40.xt), custom_call_target="tpu_custom_call" | custom-call | flops 6341787648 | bytes 8388608 | tf_op jit(solution)/shard_map/pallas_call | solution.py:351
  137.0 3.6 %collective-permute-done.16.other = bf16[8,2,16,3584]{3,2,1,0:T(8,128)(2,1)S(1)} collective-permute-done((bf16[8,2,16,3584]{3,2,1,0:T(8,128)(2,1)}, bf16[8,2,16,3584]{3,2,1,0:T(8,128)(2,1)S(1)}, u32[]{:S(2)}, u32[]{:S(2)}) %collective-permute-start.16) | collective-permute-done | bytes 1835040 | tf_op jit(solution)/shard_map/ppermute | solution.py:553
  142.3 3.7 %all-to-all-start.3 = ((bf16[16,16,3584]{2,1,0:T(8,128)(2,1)}), bf16[16,16,3584]{2,1,0:T(8,128)(2,1)S(1)}, u32[]{:S(2)}, u32[]{:S(2)}) async-start(bf16[16,16,3584]{2,1,0:T(8,128)(2,1)} %bitcast.20), calls=%async_computation.3 | async-start | bytes 3670016 | tf_op jit(solution)/shard_map/all_to_all | solution.py:612
  146.0 12.0 %shard_map.99 = bf16[8,216,512]{2,1,0:T(8,128)(2,1)} custom-call(bf16[8,216,512]{2,1,0:T(8,128)(2,1)} %copy-done.6, bf16[2,4,4,7,16,512]{5,4,3,2,1,0:T(8,128)(2,1)} %get-tuple-element.45.kept), custom_call_target="tpu_custom_call" | custom-call | flops 6341787648 | bytes 8388608 | tf_op jit(solution)/shard_map/pallas_call | solution.py:423
  166.3 3.7 %all-to-all-done.3.got = bf16[16,16,3584]{2,1,0:T(8,128)(2,1)S(1)} async-done(((bf16[16,16,3584]{2,1,0:T(8,128)(2,1)}), bf16[16,16,3584]{2,1,0:T(8,128)(2,1)S(1)}, u32[]{:S(2)}, u32[]{:S(2)}) %all-to-all-start.3) | async-done | bytes 1835040 | tf_op jit(solution)/shard_map/all_to_all | solution.py:612
  171.4 4.9 %collective-permute-done.19.other = bf16[2,16,3584]{2,1,0:T(8,128)(2,1)S(1)} collective-permute-done((bf16[2,16,3584]{2,1,0:T(8,128)(2,1)S(1)}, bf16[2,16,3584]{2,1,0:T(8,128)(2,1)S(1)}, u32[]{:S(2)}, u32[]{:S(2)}) %collective-permute-start.19) | collective-permute-done | bytes 229408 | tf_op jit(solution)/shard_map/ppermute | solution.py:553
  177.9 7.6 %all-to-all-start.4 = ((bf16[8,216,512]{2,1,0:T(8,128)(2,1)}), bf16[8,216,512]{2,1,0:T(8,128)(2,1)S(1)}, u32[]{:S(2)}, u32[]{:S(2)}) async-start(bf16[8,216,512]{2,1,0:T(8,128)(2,1)} %shard_map.99), calls=%async_computation.4 | async-start | bytes 3538944 | tf_op jit(solution)/shard_map/all_to_all | solution.py:628
  190.0 3.3 %collective-permute-done.22.refs_2_ = bf16[2,16,4096]{2,1,0:T(8,128)(2,1)S(1)} collective-permute-done((bf16[2,16,4096]{2,1,0:T(8,128)(2,1)S(1)}, bf16[2,16,4096]{2,1,0:T(8,128)(2,1)S(1)}, u32[]{:S(2)}, u32[]{:S(2)}) %collective-permute-start.22) | collective-permute-done | bytes 262176 | tf_op jit(solution)/shard_map/ppermute | solution.py:626
  193.3 3.4 %collective-permute-done.23.refs_3_ = bf16[2,16,4096]{2,1,0:T(8,128)(2,1)S(1)} collective-permute-done((bf16[2,16,4096]{2,1,0:T(8,128)(2,1)S(1)}, bf16[2,16,4096]{2,1,0:T(8,128)(2,1)S(1)}, u32[]{:S(2)}, u32[]{:S(2)}) %collective-permute-start.23) | collective-permute-done | bytes 262176 | tf_op jit(solution)/shard_map/ppermute | solution.py:626
  197.3 4.8 %collective-permute-start.24 = (bf16[512,256]{1,0:T(8,128)(2,1)S(1)}, bf16[512,256]{1,0:T(8,128)(2,1)S(1)}, u32[]{:S(2)}, u32[]{:S(2)}) collective-permute-start(bf16[512,256]{1,0:T(8,128)(2,1)S(1)} %shard_map.104.mine), channel_id=1, source_target_pairs={{0,1},{1,0},{2,3},{3,2},{4,5},{5,4},{6,7},{7,6},{8,9},{9,8},{10,11... | collective-permute-start | bytes 786440 | tf_op jit(solution)/shard_map/ppermute | solution.py:553
  206.2 4.2 %all-to-all-done.4.got = bf16[8,216,512]{2,1,0:T(8,128)(2,1)S(1)} async-done(((bf16[8,216,512]{2,1,0:T(8,128)(2,1)}), bf16[8,216,512]{2,1,0:T(8,128)(2,1)S(1)}, u32[]{:S(2)}, u32[]{:S(2)}) %all-to-all-start.4) | async-done | bytes 1769504 | tf_op jit(solution)/shard_map/all_to_all | solution.py:628
  (82 shorter events, 57.3 us)
Async XLA Ops:
  3.9 7.1 %collective-permute-start = (bf16[7,16,512]{2,1,0:T(8,128)(2,1)S(1)}, bf16[7,16,512]{2,1,0:T(8,128)(2,1)S(1)}, u32[]{:S(2)}, u32[]{:S(2)}) collective-permute-start(bf16[7,16,512]{2,1,0:T(8,128)(2,1)S(1)} %get-tuple-element.31), channel_id=1, source_target_pairs={{0,2},{2,4},{4,6},{6,0},{1,3},{3,5},{5,7},{7,1},{8,10},{10,12},{12... | collective-permute-start | bytes 344072 | tf_op jit(solution)/shard_map/ppermute | solution.py:588
  6.1 7.5 %collective-permute-start.1 = (bf16[7,16,512]{2,1,0:T(8,128)(2,1)S(1)}, bf16[7,16,512]{2,1,0:T(8,128)(2,1)S(1)}, u32[]{:S(2)}, u32[]{:S(2)}) collective-permute-start(bf16[7,16,512]{2,1,0:T(8,128)(2,1)S(1)} %get-tuple-element.32), channel_id=1, source_target_pairs={{0,4},{2,6},{4,0},{6,2},{1,5},{3,7},{5,1},{7,3},{8,12},{10,14},{12... | collective-permute-start | bytes 344072 | tf_op jit(solution)/shard_map/ppermute | solution.py:588
  8.5 5.0 %collective-permute-start.2 = (bf16[7,16,512]{2,1,0:T(8,128)(2,1)S(1)}, bf16[7,16,512]{2,1,0:T(8,128)(2,1)S(1)}, u32[]{:S(2)}, u32[]{:S(2)}) collective-permute-start(bf16[7,16,512]{2,1,0:T(8,128)(2,1)S(1)} %get-tuple-element.33), channel_id=1, source_target_pairs={{0,6},{2,0},{4,2},{6,4},{1,7},{3,1},{5,3},{7,5},{8,14},{10,8},{12,... | collective-permute-start | bytes 344072 | tf_op jit(solution)/shard_map/ppermute | solution.py:588
  14.1 34.7 %all-to-all-start = ((bf16[8,224,512]{2,1,0:T(8,128)(2,1)}), bf16[8,224,512]{2,1,0:T(8,128)(2,1)}, u32[]{:S(2)}, u32[]{:S(2)}) async-start(bf16[8,224,512]{2,1,0:T(8,128)(2,1)} %shard_map.92), calls=%async_computation | async-start | bytes 3670016 | tf_op jit(solution)/shard_map/all_to_all | solution.py:595
  20.4 12.8 %collective-permute-start.3 = (bf16[4,7,16,512]{3,2,1,0:T(8,128)(2,1)S(1)}, bf16[4,7,16,512]{3,2,1,0:T(8,128)(2,1)S(1)}, u32[]{:S(2)}, u32[]{:S(2)}) collective-permute-start(bf16[4,7,16,512]{3,2,1,0:T(8,128)(2,1)S(1)} %shard_map.94.refs_0_), channel_id=1, source_target_pairs={{0,32},{32,64},{64,96},{96,0},{1,33},{33,65},{65,97},{97,1},{2,34}... | collective-permute-start | bytes 1376264 | tf_op jit(solution)/shard_map/ppermute | solution.py:590
  22.0 21.9 %collective-permute-start.4 = (bf16[4,7,16,512]{3,2,1,0:T(8,128)(2,1)S(1)}, bf16[4,7,16,512]{3,2,1,0:T(8,128)(2,1)S(1)}, u32[]{:S(2)}, u32[]{:S(2)}) collective-permute-start(bf16[4,7,16,512]{3,2,1,0:T(8,128)(2,1)S(1)} %shard_map.94.refs_0_), channel_id=1, source_target_pairs={{0,64},{32,96},{64,0},{96,32},{1,65},{33,97},{65,1},{97,33},{2,66}... | collective-permute-start | bytes 1376264 | tf_op jit(solution)/shard_map/ppermute | solution.py:590
  25.3 21.3 %collective-permute-start.5 = (bf16[4,7,16,512]{3,2,1,0:T(8,128)(2,1)S(1)}, bf16[4,7,16,512]{3,2,1,0:T(8,128)(2,1)S(1)}, u32[]{:S(2)}, u32[]{:S(2)}) collective-permute-start(bf16[4,7,16,512]{3,2,1,0:T(8,128)(2,1)S(1)} %shard_map.94.refs_0_), channel_id=1, source_target_pairs={{0,96},{32,0},{64,32},{96,64},{1,97},{33,1},{65,33},{97,65},{2,98}... | collective-permute-start | bytes 1376264 | tf_op jit(solution)/shard_map/ppermute | solution.py:590
  26.0 20.6 %collective-permute-start.6 = (bf16[4,7,16,512]{3,2,1,0:T(8,128)(2,1)S(1)}, bf16[4,7,16,512]{3,2,1,0:T(8,128)(2,1)S(1)}, u32[]{:S(2)}, u32[]{:S(2)}) collective-permute-start(bf16[4,7,16,512]{3,2,1,0:T(8,128)(2,1)S(1)} %shard_map.94.refs_0_), channel_id=1, source_target_pairs={{0,1},{1,0},{2,3},{3,2},{4,5},{5,4},{6,7},{7,6},{8,9},{9,8},{10,11... | collective-permute-start | bytes 1376264 | tf_op jit(solution)/shard_map/ppermute | solution.py:553
  33.2 13.4 %collective-permute-start.7 = (bf16[4,7,16,512]{3,2,1,0:T(8,128)(2,1)S(1)}, bf16[4,7,16,512]{3,2,1,0:T(8,128)(2,1)S(1)}, u32[]{:S(2)}, u32[]{:S(2)}) collective-permute-start(bf16[4,7,16,512]{3,2,1,0:T(8,128)(2,1)S(1)} %collective-permute-done.3.refs_1_), channel_id=1, source_target_pairs={{0,1},{1,0},{2,3},{3,2},{4,5},{5,4},{6,7},{7,6},{8,9},{9,8},{10,11... | collective-permute-start | bytes 1376264 | tf_op jit(solution)/shard_map/ppermute | solution.py:553
  59.3 31.9 %all-to-all-start.1 = ((bf16[8,216,512]{2,1,0:T(8,128)(2,1)}), bf16[8,216,512]{2,1,0:T(8,128)(2,1)S(1)}, u32[]{:S(2)}, u32[]{:S(2)}) async-start(bf16[8,216,512]{2,1,0:T(8,128)(2,1)} %get-tuple-element.35), calls=%async_computation.1 | async-start | bytes 3538944 | tf_op jit(solution)/shard_map/all_to_all | solution.py:598
  93.7 5.8 %collective-permute-start.10 = (bf16[512,256]{1,0:T(8,128)(2,1)S(1)}, bf16[512,256]{1,0:T(8,128)(2,1)}, u32[]{:S(2)}, u32[]{:S(2)}) collective-permute-start(bf16[512,256]{1,0:T(8,128)(2,1)S(1)} %dynamic-slice_convert_fusion), channel_id=1, source_target_pairs={{0,1},{1,0},{2,3},{3,2},{4,5},{5,4},{6,7},{7,6},{8,9},{9,8},{10,11... | collective-permute-start | bytes 786440 | tf_op jit(solution)/shard_map/ppermute | solution.py:568
  94.6 31.9 %all-to-all-start.2 = ((bf16[8,216,512]{2,1,0:T(8,128)(2,1)}), bf16[8,216,512]{2,1,0:T(8,128)(2,1)S(1)}, u32[]{:S(2)}, u32[]{:S(2)}) async-start(bf16[8,216,512]{2,1,0:T(8,128)(2,1)} %copy-done.1), calls=%async_computation.2 | async-start | bytes 3538944 | tf_op jit(solution)/shard_map/all_to_all | solution.py:601
  100.6 4.9 %collective-permute-start.11 = (bf16[256,256]{1,0:T(8,128)(2,1)S(1)}, bf16[256,256]{1,0:T(8,128)(2,1)S(1)}, u32[]{:S(2)}, u32[]{:S(2)}) collective-permute-start(bf16[256,256]{1,0:T(8,128)(2,1)S(1)} %dynamic-slice_convert_fusion.1), channel_id=1, source_target_pairs={{0,32},{32,0},{64,96},{96,64},{1,33},{33,1},{65,97},{97,65},{2,34}... | collective-permute-start | bytes 393224 | tf_op jit(solution)/shard_map/ppermute | solution.py:568
  109.9 10.8 %collective-permute-start.15 = (bf16[128,256]{1,0:T(8,128)(2,1)S(1)}, bf16[128,256]{1,0:T(8,128)(2,1)S(1)}, u32[]{:S(2)}, u32[]{:S(2)}) collective-permute-start(bf16[128,256]{1,0:T(8,128)(2,1)S(1)} %fusion.1), channel_id=1, source_target_pairs={{0,24},{8,16},{16,8},{24,0},{1,25},{9,17},{17,9},{25,1},{2,26},{10... | collective-permute-start | bytes 196616 | tf_op jit(solution)/shard_map/ppermute | solution.py:579
  112.9 7.8 %collective-permute-start.14 = (bf16[128,256]{1,0:T(8,128)(2,1)S(1)}, bf16[128,256]{1,0:T(8,128)(2,1)S(1)}, u32[]{:S(2)}, u32[]{:S(2)}) collective-permute-start(bf16[128,256]{1,0:T(8,128)(2,1)S(1)} %fusion.1), channel_id=1, source_target_pairs={{0,16},{8,24},{16,0},{24,8},{1,17},{9,25},{17,1},{25,9},{2,18},{10... | collective-permute-start | bytes 196616 | tf_op jit(solution)/shard_map/ppermute | solution.py:579
  112.9 13.6 %collective-permute-start.13 = (bf16[128,256]{1,0:T(8,128)(2,1)S(1)}, bf16[128,256]{1,0:T(8,128)(2,1)S(1)}, u32[]{:S(2)}, u32[]{:S(2)}) collective-permute-start(bf16[128,256]{1,0:T(8,128)(2,1)S(1)} %fusion.1), channel_id=1, source_target_pairs={{0,8},{8,0},{16,24},{24,16},{1,9},{9,1},{17,25},{25,17},{2,10},{10... | collective-permute-start | bytes 196616 | tf_op jit(solution)/shard_map/ppermute | solution.py:579
  142.3 27.8 %all-to-all-start.3 = ((bf16[16,16,3584]{2,1,0:T(8,128)(2,1)}), bf16[16,16,3584]{2,1,0:T(8,128)(2,1)S(1)}, u32[]{:S(2)}, u32[]{:S(2)}) async-start(bf16[16,16,3584]{2,1,0:T(8,128)(2,1)} %bitcast.20), calls=%async_computation.3 | async-start | bytes 3670016 | tf_op jit(solution)/shard_map/all_to_all | solution.py:612
  170.3 6.0 %collective-permute-start.19 = (bf16[2,16,3584]{2,1,0:T(8,128)(2,1)S(1)}, bf16[2,16,3584]{2,1,0:T(8,128)(2,1)S(1)}, u32[]{:S(2)}, u32[]{:S(2)}) collective-permute-start(bf16[2,16,3584]{2,1,0:T(8,128)(2,1)S(1)} %shard_map.100.mine), channel_id=1, source_target_pairs={{0,16},{16,0},{1,17},{17,1},{2,18},{18,2},{3,19},{19,3},{4,20},{20... | collective-permute-start | bytes 688136 | tf_op jit(solution)/shard_map/ppermute | solution.py:553
  176.3 11.4 %collective-permute-start.21 = (bf16[2,2,16,4096]{3,2,1,0:T(8,128)(2,1)S(1)}, bf16[2,2,16,4096]{3,2,1,0:T(8,128)(2,1)S(1)}, u32[]{:S(2)}, u32[]{:S(2)}) collective-permute-start(bf16[2,2,16,4096]{3,2,1,0:T(8,128)(2,1)S(1)} %shard_map.102.refs_0_), channel_id=1, source_target_pairs={{0,96},{32,0},{64,32},{96,64},{1,97},{33,1},{65,33},{97,65},{2,98}... | collective-permute-start | bytes 1572872 | tf_op jit(solution)/shard_map/ppermute | solution.py:625
  177.8 12.1 %collective-permute-start.20 = (bf16[2,2,16,4096]{3,2,1,0:T(8,128)(2,1)S(1)}, bf16[2,2,16,4096]{3,2,1,0:T(8,128)(2,1)S(1)}, u32[]{:S(2)}, u32[]{:S(2)}) collective-permute-start(bf16[2,2,16,4096]{3,2,1,0:T(8,128)(2,1)S(1)} %shard_map.102.refs_0_), channel_id=1, source_target_pairs={{0,32},{32,64},{64,96},{96,0},{1,33},{33,65},{65,97},{97,1},{2,34}... | collective-permute-start | bytes 1572872 | tf_op jit(solution)/shard_map/ppermute | solution.py:625
  177.9 32.6 %all-to-all-start.4 = ((bf16[8,216,512]{2,1,0:T(8,128)(2,1)}), bf16[8,216,512]{2,1,0:T(8,128)(2,1)S(1)}, u32[]{:S(2)}, u32[]{:S(2)}) async-start(bf16[8,216,512]{2,1,0:T(8,128)(2,1)} %shard_map.99), calls=%async_computation.4 | async-start | bytes 3538944 | tf_op jit(solution)/shard_map/all_to_all | solution.py:628
  187.7 5.6 %collective-permute-start.22 = (bf16[2,16,4096]{2,1,0:T(8,128)(2,1)S(1)}, bf16[2,16,4096]{2,1,0:T(8,128)(2,1)S(1)}, u32[]{:S(2)}, u32[]{:S(2)}) collective-permute-start(bf16[2,16,4096]{2,1,0:T(8,128)(2,1)S(1)} %slice_bitcast_fusion.1), channel_id=1, source_target_pairs={{0,96},{32,0},{64,32},{96,64},{1,97},{33,1},{65,33},{97,65},{2,98}... | collective-permute-start | bytes 786440 | tf_op jit(solution)/shard_map/ppermute | solution.py:626
  189.9 6.8 %collective-permute-start.23 = (bf16[2,16,4096]{2,1,0:T(8,128)(2,1)S(1)}, bf16[2,16,4096]{2,1,0:T(8,128)(2,1)S(1)}, u32[]{:S(2)}, u32[]{:S(2)}) collective-permute-start(bf16[2,16,4096]{2,1,0:T(8,128)(2,1)S(1)} %slice_bitcast_fusion), channel_id=1, source_target_pairs={{0,32},{32,64},{64,96},{96,0},{1,33},{33,65},{65,97},{97,1},{2,34}... | collective-permute-start | bytes 786440 | tf_op jit(solution)/shard_map/ppermute | solution.py:626
  197.3 7.4 %collective-permute-start.24 = (bf16[512,256]{1,0:T(8,128)(2,1)S(1)}, bf16[512,256]{1,0:T(8,128)(2,1)S(1)}, u32[]{:S(2)}, u32[]{:S(2)}) collective-permute-start(bf16[512,256]{1,0:T(8,128)(2,1)S(1)} %shard_map.104.mine), channel_id=1, source_target_pairs={{0,1},{1,0},{2,3},{3,2},{4,5},{5,4},{6,7},{7,6},{8,9},{9,8},{10,11... | collective-permute-start | bytes 786440 | tf_op jit(solution)/shard_map/ppermute | solution.py:553
  (15 other events, 79.3 us)

commit v8 on v7

--- a/solution.py
+++ b/solution.py
@@ -79,32 +79,24 @@
     )(x)
 
 
-def split_weights_kernel(place, point, atrous, out0, out1, out2, out3, taps, sem):
-    z, x = place[0], place[1]
-    begin = jnp.where(z == 0, 0, QUARTER * z - 1)
-    copy = pltpu.make_async_copy(atrous.at[pl.ds(begin, QUARTER)], taps.at[pl.ds(1, QUARTER)], sem)
-    copy.start()
-    taps[0] = point[...]
-    copy.wait()
-    first = jnp.where(z == 0, 0, 1)
+def split_weights_kernel(place, taps, out0, out1, out2, out3):
     for d, out in enumerate((out0, out1, out2, out3)):
-        col = lax.rem(x + d, 4)
+        col = lax.rem(place[1] + d, 4)
         for yh in range(2):
             lanes = pl.ds(pl.multiple_of((yh * 4 + col) * 256, 256), 256)
             for t in range(QUARTER):
-                out[t, :, yh * 256 : (yh + 1) * 256] = taps[first + t, :, lanes]
-
-
-def split_weights(place, point, atrous):
+                out[t, :, yh * 256 : (yh + 1) * 256] = taps[t, :, lanes]
+
+
+def split_weights(place, taps):
     return pl.pallas_call(
         split_weights_kernel,
         out_shape=(jax.ShapeDtypeStruct((QUARTER, 16, K), BF16),) * 4,
-        in_specs=[SMEM, VMEM, ANY],
+        in_specs=[SMEM, VMEM],
         out_specs=(VMEM,) * 4,
-        scratch_shapes=[pltpu.VMEM((QUARTER + 1, 16, 2048), BF16), pltpu.SemaphoreType.DMA],
         compiler_params=params(16),
         cost_estimate=cost(0, 1 << 20),
-    )(place, point, atrous)
+    )(place, taps)
 
 
 WEIGHTS = (2, 4, 4, QUARTER, 16, K)
@@ -134,10 +126,11 @@
 
 
 def forward_kernel(place, x, *refs):
-    blocks, (out, kept, xt, done, acc, out_sem, wt, w_sem, turned, x_sem) = refs[:8], refs[8:]
+    blocks, (out, kept, xt, done, acc, out_sem, wt, w_sem, turned, x_sem) = refs[:10], refs[10:]
     for n, block in enumerate(blocks):
-        c = place[2] if n < 4 else 1 - place[2]
-        wt[c, lax.rem(place[0] + 4 - n % 4, 4)] = block[...]
+        c = place[2] if n < 5 else 1 - place[2]
+        d, begin = ((0, 0), (1, 0), (2, 0), (2, 2), (3, 0))[n % 5]
+        wt[c, lax.rem(place[0] + 4 - d, 4), begin : begin + block.shape[0]] = block[...]
     keep = pltpu.make_async_copy(wt, kept, w_sem)
     keep.start()
     flat = x[...].reshape(CHIPS * PADDED, K)
@@ -202,7 +195,7 @@
             jax.ShapeDtypeStruct(WEIGHTS, BF16),
             jax.ShapeDtypeStruct((4, 128, CHIPS * PADDED), BF16),
         ),
-        in_specs=[SMEM] + [VMEM] * 9,
+        in_specs=[SMEM] + [VMEM] * 11,
         out_specs=(ANY,) * 3,
         scratch_shapes=[
             pltpu.VMEM((CHIPS, CELLS, 512), BF16),
@@ -572,22 +565,19 @@
     return v + lax.ppermute(v.astype(BF16), axis, pairs).astype(F32)
 
 
-def added_over_y(v):
-    total, sent = v, v.astype(BF16)
-    for l, h in ((0, 1), (1, 0), (1, 1)):
-        pairs = [(2 * i + j, 2 * ((i + l) % 2) + (j + h) % 2) for i in range(2) for j in range(2)]
-        total = total + lax.ppermute(sent, ("yl", "yh"), pairs).astype(F32)
-    return total
-
-
 def shards(features, atrous_weight, point_weight, proj_weight, cotangent):
     place = jnp.stack([lax.axis_index(a) for a in ("z", "x", "c", "yl", "yh")]).astype(jnp.int32)
 
     atrous_t = jnp.transpose(atrous_weight, (0, 2, 1))
-    parts = split_weights(place, jnp.transpose(point_weight, (1, 0)), atrous_t)
+    z = lax.axis_index("z")
+    taps = lax.dynamic_slice_in_dim(atrous_t, jnp.maximum(QUARTER * z - 1, 0), QUARTER, 0)
+    with_point = jnp.concatenate([jnp.transpose(point_weight, (1, 0))[None], taps[: QUARTER - 1]], 0)
+    parts = split_weights(place, jnp.where(z == 0, with_point, taps))
     from_x = [parts[0]] + [lax.ppermute(parts[d], "x", turn(4, d)) for d in (1, 2, 3)]
     quarter = stack_columns(place, from_x)
-    quarters = [quarter] + [lax.ppermute(quarter, "z", turn(4, d)) for d in (1, 2, 3)]
+    below, above = (lax.ppermute(quarter, "z", turn(4, d)) for d in (1, 3))
+    opposite = [lax.ppermute(above[:2], "z", turn(4, 3)), lax.ppermute(below[2:], "z", turn(4, 1))]
+    quarters = [quarter, below, *opposite, above]
     blocks = quarters + [swap(v, "c") for v in quarters]
 
     x_send = split_features(features.reshape(CELLS, 2048))
@@ -604,11 +594,15 @@
     share = halved(proj_part, "c", turn(2, 1), core)
     share = halved(share, "z", BESIDE, gray(layer))
     share = halved(share, "z", ACROSS, layer >> 1)
-    share = added_over_y(share)
     dpre, share = lax.optimization_barrier((dpre, share))
+    share = added(share, "yh", turn(2, 1))
 
     keep, send, dpre = kernel_grad(dpre, xt)
-    g_part = add_cores(keep, swap(send, "c"))
+    send, share = lax.optimization_barrier((send, share))
+    other = swap(send, "c")
+    share = added(share, "yl", turn(2, 1))
+    other, share = lax.optimization_barrier((other, share))
+    g_part = add_cores(keep, other)
     g_got = lax.all_to_all(g_part.reshape(16, 16, COLS), ("z", "yl", "yh"), 0, 0, tiled=True)
 
     dpre, _ = lax.optimization_barrier((dpre, g_part))

time: 212 us -> 204 us (0.962)
  waiting for transfers between devices: 92.1 us -> 87.9 us
  starting transfers between devices: 69.4 us -> 65.9 us
    ppermute x6 -> x4, waiting for transfers between devices: 23.9 us -> 7.64 us  [the longest x2 6.87 us: shards(): below, above = (lax.ppermute(quarter, 'z', turn(4, d)) for d in (1, 3))]
    all_to_all x1, waiting for transfers between devices: 0.01 us -> 11 us  [shards(): dpre = lax.all_to_all(d_send, ('yh', 'x'), 0, 0, tiled=True)]
    ppermute x2 -> x4, waiting for transfers between devices: 4.39 us -> 10.5 us  [added(): return v + lax.ppermute(v.astype(BF16), axis, pairs).astype(F32)]
    ppermute x7 -> x8, waiting for transfers between devices: 10.8 us -> 5.58 us  [swap(): return lax.ppermute(v, axis, turn(2, 1))]
    ppermute x6 -> x4, starting transfers between devices: 9.96 us -> 6.63 us  [the longest x2 3.83 us: shards(): below, above = (lax.ppermute(quarter, 'z', turn(4, d)) for d in (1, 3))]
    ppermute x3, starting transfers between devices: 1.54 us -> 4.67 us  [halved(): return mine + lax.ppermute(theirs.astype(BF16), axis, pairs).astype(F32)]
    unnamed x18 -> x14, local copies, waits for them, and re-layouts: 5.35 us -> 2.49 us
    all_to_all x1, starting transfers between devices: 7.6 us -> 4.8 us  [shards(): lax.all_to_all(back, ('yh', 'x'), 0, 0, tiled=True)]
  transfers between devices with their start and end apart: 30 -> 31, of which waited for: 19 -> 20; matrix products, arithmetic and copies ran while one was open for 1% -> 1% of each run, Pallas kernels for 9% -> 14%
where the time goes in v8:
time: 204 us; the launch traced here: 203 us
  waiting for transfers between devices  87.9 us (43%)
  starting transfers between devices  65.9 us (32%)
  Pallas kernels  42.2 us (21%)
  local copies, waits for them, and re-layouts  3.9 us (2%)
  other arithmetic  2.26 us (1%)
    all_to_all x1, waiting for transfers between devices, shards(): got = lax.all_to_all(partial, ('yh', 'x'), 0, 0, tiled=True)  25 us
    ppermute x8, starting transfers between devices, swap(): return lax.ppermute(v, axis, turn(2, 1))  16.6 us
    pallas_call x1, Pallas kernels, feature_grad(): pl.pallas_call(feature_grad_kernel, out_shape=jax.ShapeDtypeStruct((CHIPS...  12 us
    all_to_all x1, waiting for transfers between devices, shards(): dpre = lax.all_to_all(d_send, ('yh', 'x'), 0, 0, tiled=True)  11 us
    ppermute x4, waiting for transfers between devices, added(): return v + lax.ppermute(v.astype(BF16), axis, pairs).astype(F32)  10.5 us
    pallas_call x1, Pallas kernels, forward(): pl.pallas_call(forward_kernel, out_shape=(jax.ShapeDtypeStruct((CHIPS, CE...  9.89 us
    pallas_call x1, Pallas kernels, kernel_grad(): pl.pallas_call(kernel_grad_kernel, out_shape=(jax.ShapeDtypeStruct((8, 2,...  9.82 us
    ppermute x3, waiting for transfers between devices, halved(): return mine + lax.ppermute(theirs.astype(BF16), axis, pairs).astype(F32)  8.17 us
  transfers between devices with their start and end apart: 31, of which 20 were waited for; matrix products, arithmetic and copies ran while one was open for 1% of the time, Pallas kernels for 14%

profile of v8, /device:TPU:1, one launch (start us, length us, event | category | flops | bytes accessed | tf_op | source)
XLA Modules:
  0.0 203.1 jit_solution(6387215117626160326)
XLA Ops:
  13.8 6.3 %all-to-all-start = ((bf16[8,224,512]{2,1,0:T(8,128)(2,1)}), bf16[8,224,512]{2,1,0:T(8,128)(2,1)}, u32[]{:S(2)}, u32[]{:S(2)}) async-start(bf16[8,224,512]{2,1,0:T(8,128)(2,1)} %shard_map.92), calls=%async_computation | async-start | bytes 3670016 | tf_op jit(solution)/shard_map/all_to_all | solution.py:585
  26.0 6.9 %collective-permute-done.3.refs_1_ = bf16[4,7,16,512]{3,2,1,0:T(8,128)(2,1)S(1)} collective-permute-done((bf16[4,7,16,512]{3,2,1,0:T(8,128)(2,1)S(1)}, bf16[4,7,16,512]{3,2,1,0:T(8,128)(2,1)S(1)}, u32[]{:S(2)}, u32[]{:S(2)}) %collective-permute-start.3) | collective-permute-done | bytes 458784 | tf_op jit(solution)/shard_map/ppermute | solution.py:578
  33.1 2.7 %collective-permute-start.5 = (bf16[2,7,16,512]{3,2,1,0:T(8,128)(2,1)S(1)}, bf16[2,7,16,512]{3,2,1,0:T(8,128)(2,1)S(1)}, u32[]{:S(2)}, u32[]{:S(2)}) collective-permute-start(bf16[2,7,16,512]{3,2,1,0:T(8,128)(2,1)S(1)} %slice.21), channel_id=1, source_target_pairs={{0,96},{32,0},{64,32},{96,64},{1,97},{33,1},{65,33},{97,65},{2,98}... | collective-permute-start | bytes 688136 | tf_op jit(solution)/shard_map/ppermute | solution.py:579
  35.8 3.0 %collective-permute-start.11 = (bf16[4,7,16,512]{3,2,1,0:T(8,128)(2,1)S(1)}, bf16[4,7,16,512]{3,2,1,0:T(8,128)(2,1)S(1)}, u32[]{:S(2)}, u32[]{:S(2)}) collective-permute-start(bf16[4,7,16,512]{3,2,1,0:T(8,128)(2,1)S(1)} %collective-permute-done.4.refs_4_), channel_id=1, source_target_pairs={{0,1},{1,0},{2,3},{3,2},{4,5},{5,4},{6,7},{7,6},{8,9},{9,8},{10,11... | collective-permute-start | bytes 1376264 | tf_op jit(solution)/shard_map/ppermute | solution.py:546
  39.5 3.1 %collective-permute-start.10 = (bf16[2,7,16,512]{3,2,1,0:T(8,128)(2,1)S(1)}, bf16[2,7,16,512]{3,2,1,0:T(8,128)(2,1)S(1)}, u32[]{:S(2)}, u32[]{:S(2)}) collective-permute-start(bf16[2,7,16,512]{3,2,1,0:T(8,128)(2,1)S(1)} %collective-permute-done.6.refs_3_), channel_id=1, source_target_pairs={{0,1},{1,0},{2,3},{3,2},{4,5},{5,4},{6,7},{7,6},{8,9},{9,8},{10,11... | collective-permute-start | bytes 688136 | tf_op jit(solution)/shard_map/ppermute | solution.py:546
  45.9 9.9 %shard_map.95 = (bf16[8,216,512]{2,1,0:T(8,128)(2,1)}, bf16[2,4,4,7,16,512]{5,4,3,2,1,0:T(8,128)(2,1)}, bf16[4,128,1792]{2,1,0:T(8,128)(2,1)}) custom-call(s32[5]{0:T(128)S(1)} %stack.23.place, bf16[8,224,512]{2,1,0:T(8,128)(2,1)} %all-to-all-done.x, bf16[4,7,16,512]{3,2,1,0:T(8,128)(2,1)S(1)} %shard_map.94.refs_0_, ...), custom_call_target="tpu_custom_call" | custom-call | flops 6341787648 | bytes 8388608 | tf_op jit(solution)/shard_map/pallas_call | solution.py:191
  55.8 5.8 %all-to-all-start.1 = ((bf16[8,216,512]{2,1,0:T(8,128)(2,1)}), bf16[8,216,512]{2,1,0:T(8,128)(2,1)S(1)}, u32[]{:S(2)}, u32[]{:S(2)}) async-start(bf16[8,216,512]{2,1,0:T(8,128)(2,1)} %get-tuple-element.39), calls=%async_computation.1 | async-start | bytes 3538944 | tf_op jit(solution)/shard_map/all_to_all | solution.py:588
  61.7 25.0 %all-to-all-done.1.got = bf16[8,216,512]{2,1,0:T(8,128)(2,1)S(1)} async-done(((bf16[8,216,512]{2,1,0:T(8,128)(2,1)}), bf16[8,216,512]{2,1,0:T(8,128)(2,1)S(1)}, u32[]{:S(2)}, u32[]{:S(2)}) %all-to-all-start.1) | async-done | bytes 1769504 | tf_op jit(solution)/shard_map/all_to_all | solution.py:588
  89.2 4.3 %all-to-all-start.2 = ((bf16[8,216,512]{2,1,0:T(8,128)(2,1)}), bf16[8,216,512]{2,1,0:T(8,128)(2,1)S(1)}, u32[]{:S(2)}, u32[]{:S(2)}) async-start(bf16[8,216,512]{2,1,0:T(8,128)(2,1)} %copy-done.1), calls=%async_computation.2 | async-start | bytes 3538944 | tf_op jit(solution)/shard_map/all_to_all | solution.py:591
  98.0 4.7 %collective-permute-done.13 = bf16[256,256]{1,0:T(8,128)(2,1)S(1)} collective-permute-done((bf16[256,256]{1,0:T(8,128)(2,1)S(1)}, bf16[256,256]{1,0:T(8,128)(2,1)S(1)}, u32[]{:S(2)}, u32[]{:S(2)}) %collective-permute-start.13) | collective-permute-done | bytes 131104 | tf_op jit(solution)/shard_map/ppermute | solution.py:561
  107.5 11.0 %all-to-all-done.2.got = bf16[8,216,512]{2,1,0:T(8,128)(2,1)S(1)} async-done(((bf16[8,216,512]{2,1,0:T(8,128)(2,1)}), bf16[8,216,512]{2,1,0:T(8,128)(2,1)S(1)}, u32[]{:S(2)}, u32[]{:S(2)}) %all-to-all-start.2) | async-done | bytes 1769504 | tf_op jit(solution)/shard_map/all_to_all | solution.py:591
  118.9 9.8 %shard_map.97 = (bf16[8,2,16,3584]{3,2,1,0:T(8,128)(2,1)S(1)}, bf16[8,2,16,3584]{3,2,1,0:T(8,128)(2,1)}, bf16[8,216,512]{2,1,0:T(8,128)(2,1)S(1)}) custom-call(bf16[8,216,512]{2,1,0:T(8,128)(2,1)S(1)} %all-to-all-done.2.got, bf16[4,128,1792]{2,1,0:T(8,128)(2,1)} %get-tuple-element.44.xt), custom_call_target="tpu_custom_call" | custom-call | flops 6341787648 | bytes 8388608 | tf_op jit(solution)/shard_map/pallas_call | solution.py:344
  130.5 3.3 %collective-permute-done.17 = bf16[128,256]{1,0:T(8,128)(2,1)S(1)} collective-permute-done((bf16[128,256]{1,0:T(8,128)(2,1)S(1)}, bf16[128,256]{1,0:T(8,128)(2,1)S(1)}, u32[]{:S(2)}, u32[]{:S(2)}) %collective-permute-start.17) | collective-permute-done | bytes 65568 | tf_op jit(solution)/shard_map/ppermute | solution.py:565
  135.6 6.2 %all-to-all-start.3 = ((bf16[16,16,3584]{2,1,0:T(8,128)(2,1)}), bf16[16,16,3584]{2,1,0:T(8,128)(2,1)S(1)}, u32[]{:S(2)}, u32[]{:S(2)}) async-start(bf16[16,16,3584]{2,1,0:T(8,128)(2,1)} %bitcast.25), calls=%async_computation.3 | async-start | bytes 3670016 | tf_op jit(solution)/shard_map/all_to_all | solution.py:606
  141.7 12.0 %shard_map.99 = bf16[8,216,512]{2,1,0:T(8,128)(2,1)} custom-call(bf16[8,216,512]{2,1,0:T(8,128)(2,1)} %copy-done.4, bf16[2,4,4,7,16,512]{5,4,3,2,1,0:T(8,128)(2,1)} %get-tuple-element.53.kept), custom_call_target="tpu_custom_call" | custom-call | flops 6341787648 | bytes 8388608 | tf_op jit(solution)/shard_map/pallas_call | solution.py:416
  154.5 2.8 %collective-permute-done.18 = bf16[128,256]{1,0:T(8,128)(2,1)S(1)} collective-permute-done((bf16[128,256]{1,0:T(8,128)(2,1)S(1)}, bf16[128,256]{1,0:T(8,128)(2,1)S(1)}, u32[]{:S(2)}, u32[]{:S(2)}) %collective-permute-start.18) | collective-permute-done | bytes 65568 | tf_op jit(solution)/shard_map/ppermute | solution.py:565
  157.7 4.3 %collective-permute-done.19 = bf16[128,256]{1,0:T(8,128)(2,1)S(1)} collective-permute-done((bf16[128,256]{1,0:T(8,128)(2,1)S(1)}, bf16[128,256]{1,0:T(8,128)(2,1)S(1)}, u32[]{:S(2)}, u32[]{:S(2)}) %collective-permute-start.19) | collective-permute-done | bytes 65568 | tf_op jit(solution)/shard_map/ppermute | solution.py:565
  162.0 3.0 %all-to-all-done.3.got = bf16[16,16,3584]{2,1,0:T(8,128)(2,1)S(1)} async-done(((bf16[16,16,3584]{2,1,0:T(8,128)(2,1)}), bf16[16,16,3584]{2,1,0:T(8,128)(2,1)S(1)}, u32[]{:S(2)}, u32[]{:S(2)}) %all-to-all-start.3) | async-done | bytes 1835040 | tf_op jit(solution)/shard_map/all_to_all | solution.py:606
  166.5 4.1 %collective-permute-done.20.other = bf16[2,16,3584]{2,1,0:T(8,128)(2,1)S(1)} collective-permute-done((bf16[2,16,3584]{2,1,0:T(8,128)(2,1)S(1)}, bf16[2,16,3584]{2,1,0:T(8,128)(2,1)S(1)}, u32[]{:S(2)}, u32[]{:S(2)}) %collective-permute-start.20) | collective-permute-done | bytes 229408 | tf_op jit(solution)/shard_map/ppermute | solution.py:546
  172.1 4.8 %all-to-all-start.4 = ((bf16[8,216,512]{2,1,0:T(8,128)(2,1)}), bf16[8,216,512]{2,1,0:T(8,128)(2,1)S(1)}, u32[]{:S(2)}, u32[]{:S(2)}) async-start(bf16[8,216,512]{2,1,0:T(8,128)(2,1)} %shard_map.99), calls=%async_computation.4 | async-start | bytes 3538944 | tf_op jit(solution)/shard_map/all_to_all | solution.py:622
  176.9 4.3 %collective-permute-done.22.refs_4_ = bf16[2,2,16,4096]{3,2,1,0:T(8,128)(2,1)S(1)} collective-permute-done((bf16[2,2,16,4096]{3,2,1,0:T(8,128)(2,1)S(1)}, bf16[2,2,16,4096]{3,2,1,0:T(8,128)(2,1)S(1)}, u32[]{:S(2)}, u32[]{:S(2)}) %collective-permute-start.22) | collective-permute-done | bytes 524320 | tf_op jit(solution)/shard_map/ppermute | solution.py:619
  182.9 4.5 %collective-permute-done.23.refs_2_ = bf16[2,16,4096]{2,1,0:T(8,128)(2,1)S(1)} collective-permute-done((bf16[2,16,4096]{2,1,0:T(8,128)(2,1)S(1)}, bf16[2,16,4096]{2,1,0:T(8,128)(2,1)S(1)}, u32[]{:S(2)}, u32[]{:S(2)}) %collective-permute-start.23) | collective-permute-done | bytes 262176 | tf_op jit(solution)/shard_map/ppermute | solution.py:620
  189.7 5.9 %collective-permute-start.25 = (bf16[512,256]{1,0:T(8,128)(2,1)S(1)}, bf16[512,256]{1,0:T(8,128)(2,1)S(1)}, u32[]{:S(2)}, u32[]{:S(2)}) collective-permute-start(bf16[512,256]{1,0:T(8,128)(2,1)S(1)} %shard_map.104.mine), channel_id=1, source_target_pairs={{0,1},{1,0},{2,3},{3,2},{4,5},{5,4},{6,7},{7,6},{8,9},{9,8},{10,11... | collective-permute-start | bytes 786440 | tf_op jit(solution)/shard_map/ppermute | solution.py:546
  195.6 2.6 %shard_map.103 = (f32[128,256]{1,0:T(8,128)}, f32[27,128,256]{2,1,0:T(8,128)}) custom-call(s32[5]{0:T(128)S(1)} %stack.23.place, bf16[2,2,16,4096]{3,2,1,0:T(8,128)(2,1)S(1)} %shard_map.102.refs_0_, bf16[2,2,16,4096]{3,2,1,0:T(8,128)(2,1)S(1)} %collective-permute-done.21.refs_1_, bf16[2,16,4096]{2,1,0:T(8,128)(2,1)S(1)} %collective-permute-done.23.refs_2_, ...), custom_call_target="tpu_custom_call" | custom-call | tf_op jit(solution)/shard_map/pallas_call | solution.py:469
  (88 shorter events, 51.7 us)
Async XLA Ops:
  3.7 7.1 %collective-permute-start = (bf16[7,16,512]{2,1,0:T(8,128)(2,1)S(1)}, bf16[7,16,512]{2,1,0:T(8,128)(2,1)S(1)}, u32[]{:S(2)}, u32[]{:S(2)}) collective-permute-start(bf16[7,16,512]{2,1,0:T(8,128)(2,1)S(1)} %get-tuple-element.35), channel_id=1, source_target_pairs={{0,2},{2,4},{4,6},{6,0},{1,3},{3,5},{5,7},{7,1},{8,10},{10,12},{12... | collective-permute-start | bytes 344072 | tf_op jit(solution)/shard_map/ppermute | solution.py:576
  5.8 7.5 %collective-permute-start.1 = (bf16[7,16,512]{2,1,0:T(8,128)(2,1)S(1)}, bf16[7,16,512]{2,1,0:T(8,128)(2,1)S(1)}, u32[]{:S(2)}, u32[]{:S(2)}) collective-permute-start(bf16[7,16,512]{2,1,0:T(8,128)(2,1)S(1)} %get-tuple-element.36), channel_id=1, source_target_pairs={{0,4},{2,6},{4,0},{6,2},{1,5},{3,7},{5,1},{7,3},{8,12},{10,14},{12... | collective-permute-start | bytes 344072 | tf_op jit(solution)/shard_map/ppermute | solution.py:576
  8.2 5.0 %collective-permute-start.2 = (bf16[7,16,512]{2,1,0:T(8,128)(2,1)S(1)}, bf16[7,16,512]{2,1,0:T(8,128)(2,1)S(1)}, u32[]{:S(2)}, u32[]{:S(2)}) collective-permute-start(bf16[7,16,512]{2,1,0:T(8,128)(2,1)S(1)} %get-tuple-element.37), channel_id=1, source_target_pairs={{0,6},{2,0},{4,2},{6,4},{1,7},{3,1},{5,3},{7,5},{8,14},{10,8},{12,... | collective-permute-start | bytes 344072 | tf_op jit(solution)/shard_map/ppermute | solution.py:576
  13.8 32.1 %all-to-all-start = ((bf16[8,224,512]{2,1,0:T(8,128)(2,1)}), bf16[8,224,512]{2,1,0:T(8,128)(2,1)}, u32[]{:S(2)}, u32[]{:S(2)}) async-start(bf16[8,224,512]{2,1,0:T(8,128)(2,1)} %shard_map.92), calls=%async_computation | async-start | bytes 3670016 | tf_op jit(solution)/shard_map/all_to_all | solution.py:585
  20.1 12.8 %collective-permute-start.3 = (bf16[4,7,16,512]{3,2,1,0:T(8,128)(2,1)S(1)}, bf16[4,7,16,512]{3,2,1,0:T(8,128)(2,1)S(1)}, u32[]{:S(2)}, u32[]{:S(2)}) collective-permute-start(bf16[4,7,16,512]{3,2,1,0:T(8,128)(2,1)S(1)} %shard_map.94.refs_0_), channel_id=1, source_target_pairs={{0,32},{32,64},{64,96},{96,0},{1,33},{33,65},{65,97},{97,1},{2,34}... | collective-permute-start | bytes 1376264 | tf_op jit(solution)/shard_map/ppermute | solution.py:578
  21.7 11.3 %collective-permute-start.4 = (bf16[4,7,16,512]{3,2,1,0:T(8,128)(2,1)S(1)}, bf16[4,7,16,512]{3,2,1,0:T(8,128)(2,1)S(1)}, u32[]{:S(2)}, u32[]{:S(2)}) collective-permute-start(bf16[4,7,16,512]{3,2,1,0:T(8,128)(2,1)S(1)} %shard_map.94.refs_0_), channel_id=1, source_target_pairs={{0,96},{32,0},{64,32},{96,64},{1,97},{33,1},{65,33},{97,65},{2,98}... | collective-permute-start | bytes 1376264 | tf_op jit(solution)/shard_map/ppermute | solution.py:578
  23.9 18.7 %collective-permute-start.7 = (bf16[4,7,16,512]{3,2,1,0:T(8,128)(2,1)S(1)}, bf16[4,7,16,512]{3,2,1,0:T(8,128)(2,1)S(1)}, u32[]{:S(2)}, u32[]{:S(2)}) collective-permute-start(bf16[4,7,16,512]{3,2,1,0:T(8,128)(2,1)S(1)} %shard_map.94.refs_0_), channel_id=1, source_target_pairs={{0,1},{1,0},{2,3},{3,2},{4,5},{5,4},{6,7},{7,6},{8,9},{9,8},{10,11... | collective-permute-start | bytes 1376264 | tf_op jit(solution)/shard_map/ppermute | solution.py:546
  32.9 6.6 %collective-permute-start.6 = (bf16[2,7,16,512]{3,2,1,0:T(8,128)(2,1)S(1)}, bf16[2,7,16,512]{3,2,1,0:T(8,128)(2,1)S(1)}, u32[]{:S(2)}, u32[]{:S(2)}) collective-permute-start(bf16[2,7,16,512]{3,2,1,0:T(8,128)(2,1)S(1)} %slice.22), channel_id=1, source_target_pairs={{0,32},{32,64},{64,96},{96,0},{1,33},{33,65},{65,97},{97,1},{2,34}... | collective-permute-start | bytes 688136 | tf_op jit(solution)/shard_map/ppermute | solution.py:579
  33.1 9.6 %collective-permute-start.5 = (bf16[2,7,16,512]{3,2,1,0:T(8,128)(2,1)S(1)}, bf16[2,7,16,512]{3,2,1,0:T(8,128)(2,1)S(1)}, u32[]{:S(2)}, u32[]{:S(2)}) collective-permute-start(bf16[2,7,16,512]{3,2,1,0:T(8,128)(2,1)S(1)} %slice.21), channel_id=1, source_target_pairs={{0,96},{32,0},{64,32},{96,64},{1,97},{33,1},{65,33},{97,65},{2,98}... | collective-permute-start | bytes 688136 | tf_op jit(solution)/shard_map/ppermute | solution.py:579
  35.8 8.3 %collective-permute-start.11 = (bf16[4,7,16,512]{3,2,1,0:T(8,128)(2,1)S(1)}, bf16[4,7,16,512]{3,2,1,0:T(8,128)(2,1)S(1)}, u32[]{:S(2)}, u32[]{:S(2)}) collective-permute-start(bf16[4,7,16,512]{3,2,1,0:T(8,128)(2,1)S(1)} %collective-permute-done.4.refs_4_), channel_id=1, source_target_pairs={{0,1},{1,0},{2,3},{3,2},{4,5},{5,4},{6,7},{7,6},{8,9},{9,8},{10,11... | collective-permute-start | bytes 1376264 | tf_op jit(solution)/shard_map/ppermute | solution.py:546
  38.7 5.4 %collective-permute-start.8 = (bf16[4,7,16,512]{3,2,1,0:T(8,128)(2,1)S(1)}, bf16[4,7,16,512]{3,2,1,0:T(8,128)(2,1)}, u32[]{:S(2)}, u32[]{:S(2)}) collective-permute-start(bf16[4,7,16,512]{3,2,1,0:T(8,128)(2,1)S(1)} %collective-permute-done.3.refs_1_), channel_id=1, source_target_pairs={{0,1},{1,0},{2,3},{3,2},{4,5},{5,4},{6,7},{7,6},{8,9},{9,8},{10,11... | collective-permute-start | bytes 1376264 | tf_op jit(solution)/shard_map/ppermute | solution.py:546
  55.8 30.8 %all-to-all-start.1 = ((bf16[8,216,512]{2,1,0:T(8,128)(2,1)}), bf16[8,216,512]{2,1,0:T(8,128)(2,1)S(1)}, u32[]{:S(2)}, u32[]{:S(2)}) async-start(bf16[8,216,512]{2,1,0:T(8,128)(2,1)} %get-tuple-element.39), calls=%async_computation.1 | async-start | bytes 3538944 | tf_op jit(solution)/shard_map/all_to_all | solution.py:588
  89.2 29.3 %all-to-all-start.2 = ((bf16[8,216,512]{2,1,0:T(8,128)(2,1)}), bf16[8,216,512]{2,1,0:T(8,128)(2,1)S(1)}, u32[]{:S(2)}, u32[]{:S(2)}) async-start(bf16[8,216,512]{2,1,0:T(8,128)(2,1)} %copy-done.1), calls=%async_computation.2 | async-start | bytes 3538944 | tf_op jit(solution)/shard_map/all_to_all | solution.py:591
  97.9 4.8 %collective-permute-start.13 = (bf16[256,256]{1,0:T(8,128)(2,1)S(1)}, bf16[256,256]{1,0:T(8,128)(2,1)S(1)}, u32[]{:S(2)}, u32[]{:S(2)}) collective-permute-start(bf16[256,256]{1,0:T(8,128)(2,1)S(1)} %dynamic-slice_convert_fusion.1), channel_id=1, source_target_pairs={{0,32},{32,0},{64,96},{96,64},{1,33},{33,1},{65,97},{97,65},{2,34}... | collective-permute-start | bytes 393224 | tf_op jit(solution)/shard_map/ppermute | solution.py:561
  118.6 10.2 %collective-permute-start.15 = (bf16[128,256]{1,0:T(8,128)(2,1)S(1)}, bf16[128,256]{1,0:T(8,128)(2,1)S(1)}, u32[]{:S(2)}, u32[]{:S(2)}) collective-permute-start(bf16[128,256]{1,0:T(8,128)(2,1)S(1)} %convert_element_type.48), channel_id=1, source_target_pairs={{0,8},{8,0},{1,9},{9,1},{2,10},{10,2},{3,11},{11,3},{4,12},{12,4},... | collective-permute-start | bytes 196616 | tf_op jit(solution)/shard_map/ppermute | solution.py:565
  128.8 5.0 %collective-permute-start.16 = (bf16[8,2,16,3584]{3,2,1,0:T(8,128)(2,1)}, bf16[8,2,16,3584]{3,2,1,0:T(8,128)(2,1)S(1)}, u32[]{:S(2)}, u32[]{:S(2)}) collective-permute-start(bf16[8,2,16,3584]{3,2,1,0:T(8,128)(2,1)} %get-tuple-element.48), channel_id=1, source_target_pairs={{0,1},{1,0},{2,3},{3,2},{4,5},{5,4},{6,7},{7,6},{8,9},{9,8},{10,11... | collective-permute-start | bytes 5505032 | tf_op jit(solution)/shard_map/ppermute | solution.py:546
  135.6 29.5 %all-to-all-start.3 = ((bf16[16,16,3584]{2,1,0:T(8,128)(2,1)}), bf16[16,16,3584]{2,1,0:T(8,128)(2,1)S(1)}, u32[]{:S(2)}, u32[]{:S(2)}) async-start(bf16[16,16,3584]{2,1,0:T(8,128)(2,1)} %bitcast.25), calls=%async_computation.3 | async-start | bytes 3670016 | tf_op jit(solution)/shard_map/all_to_all | solution.py:606
  165.3 5.3 %collective-permute-start.20 = (bf16[2,16,3584]{2,1,0:T(8,128)(2,1)S(1)}, bf16[2,16,3584]{2,1,0:T(8,128)(2,1)S(1)}, u32[]{:S(2)}, u32[]{:S(2)}) collective-permute-start(bf16[2,16,3584]{2,1,0:T(8,128)(2,1)S(1)} %shard_map.100.mine), channel_id=1, source_target_pairs={{0,16},{16,0},{1,17},{17,1},{2,18},{18,2},{3,19},{19,3},{4,20},{20... | collective-permute-start | bytes 688136 | tf_op jit(solution)/shard_map/ppermute | solution.py:546
  170.6 10.7 %collective-permute-start.22 = (bf16[2,2,16,4096]{3,2,1,0:T(8,128)(2,1)S(1)}, bf16[2,2,16,4096]{3,2,1,0:T(8,128)(2,1)S(1)}, u32[]{:S(2)}, u32[]{:S(2)}) collective-permute-start(bf16[2,2,16,4096]{3,2,1,0:T(8,128)(2,1)S(1)} %shard_map.102.refs_0_), channel_id=1, source_target_pairs={{0,96},{32,0},{64,32},{96,64},{1,97},{33,1},{65,33},{97,65},{2,98}... | collective-permute-start | bytes 1572872 | tf_op jit(solution)/shard_map/ppermute | solution.py:619
  171.1 11.0 %collective-permute-start.21 = (bf16[2,2,16,4096]{3,2,1,0:T(8,128)(2,1)S(1)}, bf16[2,2,16,4096]{3,2,1,0:T(8,128)(2,1)S(1)}, u32[]{:S(2)}, u32[]{:S(2)}) collective-permute-start(bf16[2,2,16,4096]{3,2,1,0:T(8,128)(2,1)S(1)} %shard_map.102.refs_0_), channel_id=1, source_target_pairs={{0,32},{32,64},{64,96},{96,0},{1,33},{33,65},{65,97},{97,1},{2,34}... | collective-permute-start | bytes 1572872 | tf_op jit(solution)/shard_map/ppermute | solution.py:619
  172.1 29.8 %all-to-all-start.4 = ((bf16[8,216,512]{2,1,0:T(8,128)(2,1)}), bf16[8,216,512]{2,1,0:T(8,128)(2,1)S(1)}, u32[]{:S(2)}, u32[]{:S(2)}) async-start(bf16[8,216,512]{2,1,0:T(8,128)(2,1)} %shard_map.99), calls=%async_computation.4 | async-start | bytes 3538944 | tf_op jit(solution)/shard_map/all_to_all | solution.py:622
  181.3 6.2 %collective-permute-start.23 = (bf16[2,16,4096]{2,1,0:T(8,128)(2,1)S(1)}, bf16[2,16,4096]{2,1,0:T(8,128)(2,1)S(1)}, u32[]{:S(2)}, u32[]{:S(2)}) collective-permute-start(bf16[2,16,4096]{2,1,0:T(8,128)(2,1)S(1)} %slice_bitcast_fusion.1), channel_id=1, source_target_pairs={{0,96},{32,0},{64,32},{96,64},{1,97},{33,1},{65,33},{97,65},{2,98}... | collective-permute-start | bytes 786440 | tf_op jit(solution)/shard_map/ppermute | solution.py:620
  182.1 7.0 %collective-permute-start.24 = (bf16[2,16,4096]{2,1,0:T(8,128)(2,1)S(1)}, bf16[2,16,4096]{2,1,0:T(8,128)(2,1)S(1)}, u32[]{:S(2)}, u32[]{:S(2)}) collective-permute-start(bf16[2,16,4096]{2,1,0:T(8,128)(2,1)S(1)} %slice_bitcast_fusion), channel_id=1, source_target_pairs={{0,32},{32,64},{64,96},{96,0},{1,33},{33,65},{65,97},{97,1},{2,34}... | collective-permute-start | bytes 786440 | tf_op jit(solution)/shard_map/ppermute | solution.py:620
  189.7 8.5 %collective-permute-start.25 = (bf16[512,256]{1,0:T(8,128)(2,1)S(1)}, bf16[512,256]{1,0:T(8,128)(2,1)S(1)}, u32[]{:S(2)}, u32[]{:S(2)}) collective-permute-start(bf16[512,256]{1,0:T(8,128)(2,1)S(1)} %shard_map.104.mine), channel_id=1, source_target_pairs={{0,1},{1,0},{2,3},{3,2},{4,5},{5,4},{6,7},{7,6},{8,9},{9,8},{10,11... | collective-permute-start | bytes 786440 | tf_op jit(solution)/shard_map/ppermute | solution.py:546
  (14 other events, 81.0 us)

commit v9 on v8

--- a/solution.py
+++ b/solution.py
@@ -176,7 +176,7 @@
                 + jnp.where(column >= d, minus, 0.0)
                 + jnp.where(column < WIDTH - d, plus, 0.0)
             )
-        done[j] = jnp.concatenate(parts, 1).astype(BF16)[:CELLS]
+        done[j] = jnp.concatenate(parts, 1).astype(BF16)
         pltpu.make_async_copy(done.at[j], out.at[j], out_sem.at[j]).start()
         return 0
 
@@ -191,14 +191,14 @@
     return pl.pallas_call(
         forward_kernel,
         out_shape=(
-            jax.ShapeDtypeStruct((CHIPS, CELLS, 512), BF16),
+            jax.ShapeDtypeStruct((CHIPS, PADDED, 512), BF16),
             jax.ShapeDtypeStruct(WEIGHTS, BF16),
             jax.ShapeDtypeStruct((4, 128, CHIPS * PADDED), BF16),
         ),
         in_specs=[SMEM] + [VMEM] * 11,
         out_specs=(ANY,) * 3,
         scratch_shapes=[
-            pltpu.VMEM((CHIPS, CELLS, 512), BF16),
+            pltpu.VMEM((CHIPS, PADDED, 512), BF16),
             pltpu.VMEM((10, CHIPS, PADDED, 128), F32),
             pltpu.SemaphoreType.DMA((CHIPS,)),
             pltpu.VMEM(WEIGHTS, BF16),
@@ -221,7 +221,7 @@
         total = got[yh * 4].astype(F32)
         for x in range(1, 4):
             total = total + got[yh * 4 + x].astype(F32)
-        parts.append(total)
+        parts.append(total[:CELLS])
     pre = jnp.concatenate(parts, 1).astype(BF16).astype(F32)
     sig = sigmoid(pre)
     acts = (pre * sig).astype(BF16)
@@ -237,7 +237,8 @@
     dpre = (dacts * slope).astype(BF16)
     for yh in range(2):
         for x in range(4):
-            send[yh * 4 + x] = dpre[:, yh * 512 : (yh + 1) * 512]
+            send[yh * 4 + x, :CELLS] = dpre[:, yh * 512 : (yh + 1) * 512]
+            send[yh * 4 + x, CELLS:] = jnp.zeros((PADDED - CELLS, 512), BF16)
     grad[...] = lax.dot_general(
         acts, dout, (((0,), (0,)), ((), ())), preferred_element_type=F32
     )
@@ -248,7 +249,7 @@
         middle_kernel,
         out_shape=(
             jax.ShapeDtypeStruct((CELLS, 256), BF16),
-            jax.ShapeDtypeStruct((CHIPS, CELLS, 512), BF16),
+            jax.ShapeDtypeStruct((CHIPS, PADDED, 512), BF16),
             jax.ShapeDtypeStruct((1024, 256), F32),
         ),
         in_specs=[VMEM] * 3,
@@ -261,19 +262,17 @@
 
 
 def spread_point(got, point, j):
-    point[j, :CELLS] = got[j, :, :128]
-    point[j, CELLS:] = jnp.zeros((PADDED - CELLS, 128), BF16)
+    point[j] = got[j, :, :128]
 
 
 def spread_branch(got, moved, column, g, j):
     d = DILATIONS[g]
     v = got[j, :, (g + 1) * 128 : (g + 2) * 128]
     wide = v.astype(F32)
-    minus = jnp.where(column < WIDTH - d, pltpu.roll(wide, CELLS - d, 0), 0.0)
-    plus = jnp.where(column >= d, pltpu.roll(wide, d, 0), 0.0)
+    minus = jnp.where(column < WIDTH - d, pltpu.roll(wide, PADDED - d, 0), 0.0)
+    plus = jnp.where((column >= d) & (column < WIDTH), pltpu.roll(wide, d, 0), 0.0)
     for kx, part in enumerate((minus.astype(BF16), v, plus.astype(BF16))):
-        moved[3 * g + kx, HALO + j, :CELLS] = part
-        moved[3 * g + kx, HALO + j, CELLS:] = jnp.zeros((PADDED - CELLS, 128), BF16)
+        moved[3 * g + kx, HALO + j] = part
 
 
 def spread_edges(moved, g):
@@ -283,7 +282,7 @@
 
 
 def spread(got, moved, point):
-    column = cell_column(CELLS)
+    column = cell_column(PADDED)
     for g in range(3):
         spread_edges(moved, g)
 
@@ -310,7 +309,7 @@
     load.start()
     copy_got = pltpu.make_async_copy(got, again, g_sem)
     copy_got.start()
-    column = cell_column(CELLS)
+    column = cell_column(PADDED)
     stores = []
     ready = -1
     for index, pair in enumerate(PAIRS):
@@ -344,7 +343,7 @@
     return pl.pallas_call(
         kernel_grad_kernel,
         out_shape=(jax.ShapeDtypeStruct((8, 2, 16, COLS), BF16),) * 2
-        + (jax.ShapeDtypeStruct((CHIPS, CELLS, 512), BF16),),
+        + (jax.ShapeDtypeStruct((CHIPS, PADDED, 512), BF16),),
         in_specs=[VMEM, ANY],
         out_specs=(VMEM, ANY, ANY),
         scratch_shapes=[
@@ -355,7 +354,7 @@
             pltpu.SemaphoreType.DMA((TAPS,)),
         ]
         + SPREAD,
-        compiler_params=params(48),
+        compiler_params=params(52),
         cost_estimate=CONV_COST,
     )(got, xt)
 

time: 204 us -> 208 us (1.020)
  Pallas kernels: 42.2 us -> 44.4 us
    pallas_call x1, Pallas kernels: 9.82 us -> 11.9 us  [kernel_grad(): pl.pallas_call(kernel_grad_kernel, out_shape=(jax.ShapeDtypeStruct((8, 2,...]
  transfers between devices with their start and end apart: 31 -> 31, of which waited for: 20 -> 20; matrix products, arithmetic and copies ran while one was open for 1% -> 1% of each run, Pallas kernels for 14% -> 15%
where the time goes in v9:
time: 208 us; the launch traced here: 207 us
  waiting for transfers between devices  89.2 us (43%)
  starting transfers between devices  65.5 us (31%)
  Pallas kernels  44.4 us (21%)
  local copies, waits for them, and re-layouts  4.74 us (2%)
  other arithmetic  2.26 us (1%)
    all_to_all x1, waiting for transfers between devices, shards(): got = lax.all_to_all(partial, ('yh', 'x'), 0, 0, tiled=True)  25.7 us
    ppermute x8, starting transfers between devices, swap(): return lax.ppermute(v, axis, turn(2, 1))  16.3 us
    pallas_call x1, Pallas kernels, feature_grad(): pl.pallas_call(feature_grad_kernel, out_shape=jax.ShapeDtypeStruct((CHIPS...  12.1 us
    pallas_call x1, Pallas kernels, kernel_grad(): pl.pallas_call(kernel_grad_kernel, out_shape=(jax.ShapeDtypeStruct((8, 2,...  11.9 us
    all_to_all x1, waiting for transfers between devices, shards(): dpre = lax.all_to_all(d_send, ('yh', 'x'), 0, 0, tiled=True)  11.7 us
    ppermute x4, waiting for transfers between devices, added(): return v + lax.ppermute(v.astype(BF16), axis, pairs).astype(F32)  10.5 us
    pallas_call x1, Pallas kernels, forward(): pl.pallas_call(forward_kernel, out_shape=(jax.ShapeDtypeStruct((CHIPS, PA...  9.92 us
    ppermute x3, waiting for transfers between devices, halved(): return mine + lax.ppermute(theirs.astype(BF16), axis, pairs).astype(F32)  8.17 us
  transfers between devices with their start and end apart: 31, of which 20 were waited for; matrix products, arithmetic and copies ran while one was open for 1% of the time, Pallas kernels for 15%

profile of v9, /device:TPU:1, one launch (start us, length us, event | category | flops | bytes accessed | tf_op | source)
XLA Modules:
  0.0 207.0 jit_solution(8790506471373386872)
XLA Ops:
  13.8 6.3 %all-to-all-start = ((bf16[8,224,512]{2,1,0:T(8,128)(2,1)}), bf16[8,224,512]{2,1,0:T(8,128)(2,1)}, u32[]{:S(2)}, u32[]{:S(2)}) async-start(bf16[8,224,512]{2,1,0:T(8,128)(2,1)} %shard_map.92), calls=%async_computation | async-start | bytes 3670016 | tf_op jit(solution)/shard_map/all_to_all | solution.py:584
  26.0 6.9 %collective-permute-done.3.refs_1_ = bf16[4,7,16,512]{3,2,1,0:T(8,128)(2,1)S(1)} collective-permute-done((bf16[4,7,16,512]{3,2,1,0:T(8,128)(2,1)S(1)}, bf16[4,7,16,512]{3,2,1,0:T(8,128)(2,1)S(1)}, u32[]{:S(2)}, u32[]{:S(2)}) %collective-permute-start.3) | collective-permute-done | bytes 458784 | tf_op jit(solution)/shard_map/ppermute | solution.py:577
  33.1 2.7 %collective-permute-start.5 = (bf16[2,7,16,512]{3,2,1,0:T(8,128)(2,1)S(1)}, bf16[2,7,16,512]{3,2,1,0:T(8,128)(2,1)S(1)}, u32[]{:S(2)}, u32[]{:S(2)}) collective-permute-start(bf16[2,7,16,512]{3,2,1,0:T(8,128)(2,1)S(1)} %slice.21), channel_id=1, source_target_pairs={{0,96},{32,0},{64,32},{96,64},{1,97},{33,1},{65,33},{97,65},{2,98}... | collective-permute-start | bytes 688136 | tf_op jit(solution)/shard_map/ppermute | solution.py:578
  35.8 3.0 %collective-permute-start.11 = (bf16[4,7,16,512]{3,2,1,0:T(8,128)(2,1)S(1)}, bf16[4,7,16,512]{3,2,1,0:T(8,128)(2,1)S(1)}, u32[]{:S(2)}, u32[]{:S(2)}) collective-permute-start(bf16[4,7,16,512]{3,2,1,0:T(8,128)(2,1)S(1)} %collective-permute-done.4.refs_4_), channel_id=1, source_target_pairs={{0,1},{1,0},{2,3},{3,2},{4,5},{5,4},{6,7},{7,6},{8,9},{9,8},{10,11... | collective-permute-start | bytes 1376264 | tf_op jit(solution)/shard_map/ppermute | solution.py:545
  39.5 3.1 %collective-permute-start.10 = (bf16[2,7,16,512]{3,2,1,0:T(8,128)(2,1)S(1)}, bf16[2,7,16,512]{3,2,1,0:T(8,128)(2,1)S(1)}, u32[]{:S(2)}, u32[]{:S(2)}) collective-permute-start(bf16[2,7,16,512]{3,2,1,0:T(8,128)(2,1)S(1)} %collective-permute-done.6.refs_3_), channel_id=1, source_target_pairs={{0,1},{1,0},{2,3},{3,2},{4,5},{5,4},{6,7},{7,6},{8,9},{9,8},{10,11... | collective-permute-start | bytes 688136 | tf_op jit(solution)/shard_map/ppermute | solution.py:545
  45.9 9.9 %shard_map.95 = (bf16[8,224,512]{2,1,0:T(8,128)(2,1)}, bf16[2,4,4,7,16,512]{5,4,3,2,1,0:T(8,128)(2,1)}, bf16[4,128,1792]{2,1,0:T(8,128)(2,1)}) custom-call(s32[5]{0:T(128)S(1)} %stack.23.place, bf16[8,224,512]{2,1,0:T(8,128)(2,1)} %all-to-all-done.x, bf16[4,7,16,512]{3,2,1,0:T(8,128)(2,1)S(1)} %shard_map.94.refs_0_, ...), custom_call_target="tpu_custom_call" | custom-call | flops 6341787648 | bytes 8388608 | tf_op jit(solution)/shard_map/pallas_call | solution.py:191
  55.9 5.8 %all-to-all-start.1 = ((bf16[8,224,512]{2,1,0:T(8,128)(2,1)}), bf16[8,224,512]{2,1,0:T(8,128)(2,1)S(1)}, u32[]{:S(2)}, u32[]{:S(2)}) async-start(bf16[8,224,512]{2,1,0:T(8,128)(2,1)} %get-tuple-element.39), calls=%async_computation.1 | async-start | bytes 3670016 | tf_op jit(solution)/shard_map/all_to_all | solution.py:587
  61.7 25.7 %all-to-all-done.1.got = bf16[8,224,512]{2,1,0:T(8,128)(2,1)S(1)} async-done(((bf16[8,224,512]{2,1,0:T(8,128)(2,1)}), bf16[8,224,512]{2,1,0:T(8,128)(2,1)S(1)}, u32[]{:S(2)}, u32[]{:S(2)}) %all-to-all-start.1) | async-done | bytes 1835040 | tf_op jit(solution)/shard_map/all_to_all | solution.py:587
  89.9 4.8 %all-to-all-start.2 = ((bf16[8,224,512]{2,1,0:T(8,128)(2,1)}), bf16[8,224,512]{2,1,0:T(8,128)(2,1)S(1)}, u32[]{:S(2)}, u32[]{:S(2)}) async-start(bf16[8,224,512]{2,1,0:T(8,128)(2,1)} %copy-done.1), calls=%async_computation.2 | async-start | bytes 3670016 | tf_op jit(solution)/shard_map/all_to_all | solution.py:590
  99.2 4.7 %collective-permute-done.13 = bf16[256,256]{1,0:T(8,128)(2,1)S(1)} collective-permute-done((bf16[256,256]{1,0:T(8,128)(2,1)S(1)}, bf16[256,256]{1,0:T(8,128)(2,1)S(1)}, u32[]{:S(2)}, u32[]{:S(2)}) %collective-permute-start.13) | collective-permute-done | bytes 131104 | tf_op jit(solution)/shard_map/ppermute | solution.py:560
  108.7 11.7 %all-to-all-done.2.got = bf16[8,224,512]{2,1,0:T(8,128)(2,1)S(1)} async-done(((bf16[8,224,512]{2,1,0:T(8,128)(2,1)}), bf16[8,224,512]{2,1,0:T(8,128)(2,1)S(1)}, u32[]{:S(2)}, u32[]{:S(2)}) %all-to-all-start.2) | async-done | bytes 1835040 | tf_op jit(solution)/shard_map/all_to_all | solution.py:590
  121.6 11.9 %shard_map.97 = (bf16[8,2,16,3584]{3,2,1,0:T(8,128)(2,1)S(1)}, bf16[8,2,16,3584]{3,2,1,0:T(8,128)(2,1)}, bf16[8,224,512]{2,1,0:T(8,128)(2,1)}) custom-call(bf16[8,224,512]{2,1,0:T(8,128)(2,1)} %copy-done.4, bf16[4,128,1792]{2,1,0:T(8,128)(2,1)} %get-tuple-element.44.xt), custom_call_target="tpu_custom_call" | custom-call | flops 6341787648 | bytes 8388608 | tf_op jit(solution)/shard_map/pallas_call | solution.py:343
  135.0 3.3 %collective-permute-done.17 = bf16[128,256]{1,0:T(8,128)(2,1)S(1)} collective-permute-done((bf16[128,256]{1,0:T(8,128)(2,1)S(1)}, bf16[128,256]{1,0:T(8,128)(2,1)S(1)}, u32[]{:S(2)}, u32[]{:S(2)}) %collective-permute-start.17) | collective-permute-done | bytes 65568 | tf_op jit(solution)/shard_map/ppermute | solution.py:564
  140.1 5.6 %all-to-all-start.3 = ((bf16[16,16,3584]{2,1,0:T(8,128)(2,1)}), bf16[16,16,3584]{2,1,0:T(8,128)(2,1)S(1)}, u32[]{:S(2)}, u32[]{:S(2)}) async-start(bf16[16,16,3584]{2,1,0:T(8,128)(2,1)} %bitcast.25), calls=%async_computation.3 | async-start | bytes 3670016 | tf_op jit(solution)/shard_map/all_to_all | solution.py:605
  145.7 12.1 %shard_map.99 = bf16[8,216,512]{2,1,0:T(8,128)(2,1)} custom-call(bf16[8,224,512]{2,1,0:T(8,128)(2,1)} %get-tuple-element.52.got, bf16[2,4,4,7,16,512]{5,4,3,2,1,0:T(8,128)(2,1)} %get-tuple-element.53.kept), custom_call_target="tpu_custom_call" | custom-call | flops 6341787648 | bytes 8388608 | tf_op jit(solution)/shard_map/pallas_call | solution.py:415
  158.4 2.8 %collective-permute-done.18 = bf16[128,256]{1,0:T(8,128)(2,1)S(1)} collective-permute-done((bf16[128,256]{1,0:T(8,128)(2,1)S(1)}, bf16[128,256]{1,0:T(8,128)(2,1)S(1)}, u32[]{:S(2)}, u32[]{:S(2)}) %collective-permute-start.18) | collective-permute-done | bytes 65568 | tf_op jit(solution)/shard_map/ppermute | solution.py:564
  161.7 4.3 %collective-permute-done.19 = bf16[128,256]{1,0:T(8,128)(2,1)S(1)} collective-permute-done((bf16[128,256]{1,0:T(8,128)(2,1)S(1)}, bf16[128,256]{1,0:T(8,128)(2,1)S(1)}, u32[]{:S(2)}, u32[]{:S(2)}) %collective-permute-start.19) | collective-permute-done | bytes 65568 | tf_op jit(solution)/shard_map/ppermute | solution.py:564
  166.0 3.0 %all-to-all-done.3.got = bf16[16,16,3584]{2,1,0:T(8,128)(2,1)S(1)} async-done(((bf16[16,16,3584]{2,1,0:T(8,128)(2,1)}), bf16[16,16,3584]{2,1,0:T(8,128)(2,1)S(1)}, u32[]{:S(2)}, u32[]{:S(2)}) %all-to-all-start.3) | async-done | bytes 1835040 | tf_op jit(solution)/shard_map/all_to_all | solution.py:605
  170.4 4.1 %collective-permute-done.20.other = bf16[2,16,3584]{2,1,0:T(8,128)(2,1)S(1)} collective-permute-done((bf16[2,16,3584]{2,1,0:T(8,128)(2,1)S(1)}, bf16[2,16,3584]{2,1,0:T(8,128)(2,1)S(1)}, u32[]{:S(2)}, u32[]{:S(2)}) %collective-permute-start.20) | collective-permute-done | bytes 229408 | tf_op jit(solution)/shard_map/ppermute | solution.py:545
  176.1 4.8 %all-to-all-start.4 = ((bf16[8,216,512]{2,1,0:T(8,128)(2,1)}), bf16[8,216,512]{2,1,0:T(8,128)(2,1)S(1)}, u32[]{:S(2)}, u32[]{:S(2)}) async-start(bf16[8,216,512]{2,1,0:T(8,128)(2,1)} %shard_map.99), calls=%async_computation.4 | async-start | bytes 3538944 | tf_op jit(solution)/shard_map/all_to_all | solution.py:621
  180.9 4.3 %collective-permute-done.22.refs_4_ = bf16[2,2,16,4096]{3,2,1,0:T(8,128)(2,1)S(1)} collective-permute-done((bf16[2,2,16,4096]{3,2,1,0:T(8,128)(2,1)S(1)}, bf16[2,2,16,4096]{3,2,1,0:T(8,128)(2,1)S(1)}, u32[]{:S(2)}, u32[]{:S(2)}) %collective-permute-start.22) | collective-permute-done | bytes 524320 | tf_op jit(solution)/shard_map/ppermute | solution.py:618
  186.8 4.5 %collective-permute-done.23.refs_2_ = bf16[2,16,4096]{2,1,0:T(8,128)(2,1)S(1)} collective-permute-done((bf16[2,16,4096]{2,1,0:T(8,128)(2,1)S(1)}, bf16[2,16,4096]{2,1,0:T(8,128)(2,1)S(1)}, u32[]{:S(2)}, u32[]{:S(2)}) %collective-permute-start.23) | collective-permute-done | bytes 262176 | tf_op jit(solution)/shard_map/ppermute | solution.py:619
  193.6 5.9 %collective-permute-start.25 = (bf16[512,256]{1,0:T(8,128)(2,1)S(1)}, bf16[512,256]{1,0:T(8,128)(2,1)S(1)}, u32[]{:S(2)}, u32[]{:S(2)}) collective-permute-start(bf16[512,256]{1,0:T(8,128)(2,1)S(1)} %shard_map.104.mine), channel_id=1, source_target_pairs={{0,1},{1,0},{2,3},{3,2},{4,5},{5,4},{6,7},{7,6},{8,9},{9,8},{10,11... | collective-permute-start | bytes 786440 | tf_op jit(solution)/shard_map/ppermute | solution.py:545
  199.6 2.6 %shard_map.103 = (f32[128,256]{1,0:T(8,128)}, f32[27,128,256]{2,1,0:T(8,128)}) custom-call(s32[5]{0:T(128)S(1)} %stack.23.place, bf16[2,2,16,4096]{3,2,1,0:T(8,128)(2,1)S(1)} %shard_map.102.refs_0_, bf16[2,2,16,4096]{3,2,1,0:T(8,128)(2,1)S(1)} %collective-permute-done.21.refs_1_, bf16[2,16,4096]{2,1,0:T(8,128)(2,1)S(1)} %collective-permute-done.23.refs_2_, ...), custom_call_target="tpu_custom_call" | custom-call | tf_op jit(solution)/shard_map/pallas_call | solution.py:468
  (88 shorter events, 52.2 us)
Async XLA Ops:
  3.7 7.1 %collective-permute-start = (bf16[7,16,512]{2,1,0:T(8,128)(2,1)S(1)}, bf16[7,16,512]{2,1,0:T(8,128)(2,1)S(1)}, u32[]{:S(2)}, u32[]{:S(2)}) collective-permute-start(bf16[7,16,512]{2,1,0:T(8,128)(2,1)S(1)} %get-tuple-element.35), channel_id=1, source_target_pairs={{0,2},{2,4},{4,6},{6,0},{1,3},{3,5},{5,7},{7,1},{8,10},{10,12},{12... | collective-permute-start | bytes 344072 | tf_op jit(solution)/shard_map/ppermute | solution.py:575
  5.8 7.5 %collective-permute-start.1 = (bf16[7,16,512]{2,1,0:T(8,128)(2,1)S(1)}, bf16[7,16,512]{2,1,0:T(8,128)(2,1)S(1)}, u32[]{:S(2)}, u32[]{:S(2)}) collective-permute-start(bf16[7,16,512]{2,1,0:T(8,128)(2,1)S(1)} %get-tuple-element.36), channel_id=1, source_target_pairs={{0,4},{2,6},{4,0},{6,2},{1,5},{3,7},{5,1},{7,3},{8,12},{10,14},{12... | collective-permute-start | bytes 344072 | tf_op jit(solution)/shard_map/ppermute | solution.py:575
  8.2 5.0 %collective-permute-start.2 = (bf16[7,16,512]{2,1,0:T(8,128)(2,1)S(1)}, bf16[7,16,512]{2,1,0:T(8,128)(2,1)S(1)}, u32[]{:S(2)}, u32[]{:S(2)}) collective-permute-start(bf16[7,16,512]{2,1,0:T(8,128)(2,1)S(1)} %get-tuple-element.37), channel_id=1, source_target_pairs={{0,6},{2,0},{4,2},{6,4},{1,7},{3,1},{5,3},{7,5},{8,14},{10,8},{12,... | collective-permute-start | bytes 344072 | tf_op jit(solution)/shard_map/ppermute | solution.py:575
  13.8 32.1 %all-to-all-start = ((bf16[8,224,512]{2,1,0:T(8,128)(2,1)}), bf16[8,224,512]{2,1,0:T(8,128)(2,1)}, u32[]{:S(2)}, u32[]{:S(2)}) async-start(bf16[8,224,512]{2,1,0:T(8,128)(2,1)} %shard_map.92), calls=%async_computation | async-start | bytes 3670016 | tf_op jit(solution)/shard_map/all_to_all | solution.py:584
  20.1 12.8 %collective-permute-start.3 = (bf16[4,7,16,512]{3,2,1,0:T(8,128)(2,1)S(1)}, bf16[4,7,16,512]{3,2,1,0:T(8,128)(2,1)S(1)}, u32[]{:S(2)}, u32[]{:S(2)}) collective-permute-start(bf16[4,7,16,512]{3,2,1,0:T(8,128)(2,1)S(1)} %shard_map.94.refs_0_), channel_id=1, source_target_pairs={{0,32},{32,64},{64,96},{96,0},{1,33},{33,65},{65,97},{97,1},{2,34}... | collective-permute-start | bytes 1376264 | tf_op jit(solution)/shard_map/ppermute | solution.py:577
  21.7 11.3 %collective-permute-start.4 = (bf16[4,7,16,512]{3,2,1,0:T(8,128)(2,1)S(1)}, bf16[4,7,16,512]{3,2,1,0:T(8,128)(2,1)S(1)}, u32[]{:S(2)}, u32[]{:S(2)}) collective-permute-start(bf16[4,7,16,512]{3,2,1,0:T(8,128)(2,1)S(1)} %shard_map.94.refs_0_), channel_id=1, source_target_pairs={{0,96},{32,0},{64,32},{96,64},{1,97},{33,1},{65,33},{97,65},{2,98}... | collective-permute-start | bytes 1376264 | tf_op jit(solution)/shard_map/ppermute | solution.py:577
  23.9 18.7 %collective-permute-start.7 = (bf16[4,7,16,512]{3,2,1,0:T(8,128)(2,1)S(1)}, bf16[4,7,16,512]{3,2,1,0:T(8,128)(2,1)S(1)}, u32[]{:S(2)}, u32[]{:S(2)}) collective-permute-start(bf16[4,7,16,512]{3,2,1,0:T(8,128)(2,1)S(1)} %shard_map.94.refs_0_), channel_id=1, source_target_pairs={{0,1},{1,0},{2,3},{3,2},{4,5},{5,4},{6,7},{7,6},{8,9},{9,8},{10,11... | collective-permute-start | bytes 1376264 | tf_op jit(solution)/shard_map/ppermute | solution.py:545
  32.9 6.6 %collective-permute-start.6 = (bf16[2,7,16,512]{3,2,1,0:T(8,128)(2,1)S(1)}, bf16[2,7,16,512]{3,2,1,0:T(8,128)(2,1)S(1)}, u32[]{:S(2)}, u32[]{:S(2)}) collective-permute-start(bf16[2,7,16,512]{3,2,1,0:T(8,128)(2,1)S(1)} %slice.22), channel_id=1, source_target_pairs={{0,32},{32,64},{64,96},{96,0},{1,33},{33,65},{65,97},{97,1},{2,34}... | collective-permute-start | bytes 688136 | tf_op jit(solution)/shard_map/ppermute | solution.py:578
  33.1 9.6 %collective-permute-start.5 = (bf16[2,7,16,512]{3,2,1,0:T(8,128)(2,1)S(1)}, bf16[2,7,16,512]{3,2,1,0:T(8,128)(2,1)S(1)}, u32[]{:S(2)}, u32[]{:S(2)}) collective-permute-start(bf16[2,7,16,512]{3,2,1,0:T(8,128)(2,1)S(1)} %slice.21), channel_id=1, source_target_pairs={{0,96},{32,0},{64,32},{96,64},{1,97},{33,1},{65,33},{97,65},{2,98}... | collective-permute-start | bytes 688136 | tf_op jit(solution)/shard_map/ppermute | solution.py:578
  35.8 8.3 %collective-permute-start.11 = (bf16[4,7,16,512]{3,2,1,0:T(8,128)(2,1)S(1)}, bf16[4,7,16,512]{3,2,1,0:T(8,128)(2,1)S(1)}, u32[]{:S(2)}, u32[]{:S(2)}) collective-permute-start(bf16[4,7,16,512]{3,2,1,0:T(8,128)(2,1)S(1)} %collective-permute-done.4.refs_4_), channel_id=1, source_target_pairs={{0,1},{1,0},{2,3},{3,2},{4,5},{5,4},{6,7},{7,6},{8,9},{9,8},{10,11... | collective-permute-start | bytes 1376264 | tf_op jit(solution)/shard_map/ppermute | solution.py:545
  38.7 5.4 %collective-permute-start.8 = (bf16[4,7,16,512]{3,2,1,0:T(8,128)(2,1)S(1)}, bf16[4,7,16,512]{3,2,1,0:T(8,128)(2,1)}, u32[]{:S(2)}, u32[]{:S(2)}) collective-permute-start(bf16[4,7,16,512]{3,2,1,0:T(8,128)(2,1)S(1)} %collective-permute-done.3.refs_1_), channel_id=1, source_target_pairs={{0,1},{1,0},{2,3},{3,2},{4,5},{5,4},{6,7},{7,6},{8,9},{9,8},{10,11... | collective-permute-start | bytes 1376264 | tf_op jit(solution)/shard_map/ppermute | solution.py:545
  55.9 31.6 %all-to-all-start.1 = ((bf16[8,224,512]{2,1,0:T(8,128)(2,1)}), bf16[8,224,512]{2,1,0:T(8,128)(2,1)S(1)}, u32[]{:S(2)}, u32[]{:S(2)}) async-start(bf16[8,224,512]{2,1,0:T(8,128)(2,1)} %get-tuple-element.39), calls=%async_computation.1 | async-start | bytes 3670016 | tf_op jit(solution)/shard_map/all_to_all | solution.py:587
  89.9 30.5 %all-to-all-start.2 = ((bf16[8,224,512]{2,1,0:T(8,128)(2,1)}), bf16[8,224,512]{2,1,0:T(8,128)(2,1)S(1)}, u32[]{:S(2)}, u32[]{:S(2)}) async-start(bf16[8,224,512]{2,1,0:T(8,128)(2,1)} %copy-done.1), calls=%async_computation.2 | async-start | bytes 3670016 | tf_op jit(solution)/shard_map/all_to_all | solution.py:590
  99.1 4.8 %collective-permute-start.13 = (bf16[256,256]{1,0:T(8,128)(2,1)S(1)}, bf16[256,256]{1,0:T(8,128)(2,1)S(1)}, u32[]{:S(2)}, u32[]{:S(2)}) collective-permute-start(bf16[256,256]{1,0:T(8,128)(2,1)S(1)} %dynamic-slice_convert_fusion.1), channel_id=1, source_target_pairs={{0,32},{32,0},{64,96},{96,64},{1,33},{33,1},{65,97},{97,65},{2,34}... | collective-permute-start | bytes 393224 | tf_op jit(solution)/shard_map/ppermute | solution.py:560
  120.4 13.2 %collective-permute-start.15 = (bf16[128,256]{1,0:T(8,128)(2,1)S(1)}, bf16[128,256]{1,0:T(8,128)(2,1)S(1)}, u32[]{:S(2)}, u32[]{:S(2)}) collective-permute-start(bf16[128,256]{1,0:T(8,128)(2,1)S(1)} %convert_element_type.48), channel_id=1, source_target_pairs={{0,8},{8,0},{1,9},{9,1},{2,10},{10,2},{3,11},{11,3},{4,12},{12,4},... | collective-permute-start | bytes 196616 | tf_op jit(solution)/shard_map/ppermute | solution.py:564
  133.6 4.8 %collective-permute-start.16 = (bf16[8,2,16,3584]{3,2,1,0:T(8,128)(2,1)}, bf16[8,2,16,3584]{3,2,1,0:T(8,128)(2,1)S(1)}, u32[]{:S(2)}, u32[]{:S(2)}) collective-permute-start(bf16[8,2,16,3584]{3,2,1,0:T(8,128)(2,1)} %get-tuple-element.48), channel_id=1, source_target_pairs={{0,1},{1,0},{2,3},{3,2},{4,5},{5,4},{6,7},{7,6},{8,9},{9,8},{10,11... | collective-permute-start | bytes 5505032 | tf_op jit(solution)/shard_map/ppermute | solution.py:545
  140.1 28.9 %all-to-all-start.3 = ((bf16[16,16,3584]{2,1,0:T(8,128)(2,1)}), bf16[16,16,3584]{2,1,0:T(8,128)(2,1)S(1)}, u32[]{:S(2)}, u32[]{:S(2)}) async-start(bf16[16,16,3584]{2,1,0:T(8,128)(2,1)} %bitcast.25), calls=%async_computation.3 | async-start | bytes 3670016 | tf_op jit(solution)/shard_map/all_to_all | solution.py:605
  169.2 5.3 %collective-permute-start.20 = (bf16[2,16,3584]{2,1,0:T(8,128)(2,1)S(1)}, bf16[2,16,3584]{2,1,0:T(8,128)(2,1)S(1)}, u32[]{:S(2)}, u32[]{:S(2)}) collective-permute-start(bf16[2,16,3584]{2,1,0:T(8,128)(2,1)S(1)} %shard_map.100.mine), channel_id=1, source_target_pairs={{0,16},{16,0},{1,17},{17,1},{2,18},{18,2},{3,19},{19,3},{4,20},{20... | collective-permute-start | bytes 688136 | tf_op jit(solution)/shard_map/ppermute | solution.py:545
  174.5 10.7 %collective-permute-start.22 = (bf16[2,2,16,4096]{3,2,1,0:T(8,128)(2,1)S(1)}, bf16[2,2,16,4096]{3,2,1,0:T(8,128)(2,1)S(1)}, u32[]{:S(2)}, u32[]{:S(2)}) collective-permute-start(bf16[2,2,16,4096]{3,2,1,0:T(8,128)(2,1)S(1)} %shard_map.102.refs_0_), channel_id=1, source_target_pairs={{0,96},{32,0},{64,32},{96,64},{1,97},{33,1},{65,33},{97,65},{2,98}... | collective-permute-start | bytes 1572872 | tf_op jit(solution)/shard_map/ppermute | solution.py:618
  175.1 11.0 %collective-permute-start.21 = (bf16[2,2,16,4096]{3,2,1,0:T(8,128)(2,1)S(1)}, bf16[2,2,16,4096]{3,2,1,0:T(8,128)(2,1)S(1)}, u32[]{:S(2)}, u32[]{:S(2)}) collective-permute-start(bf16[2,2,16,4096]{3,2,1,0:T(8,128)(2,1)S(1)} %shard_map.102.refs_0_), channel_id=1, source_target_pairs={{0,32},{32,64},{64,96},{96,0},{1,33},{33,65},{65,97},{97,1},{2,34}... | collective-permute-start | bytes 1572872 | tf_op jit(solution)/shard_map/ppermute | solution.py:618
  176.1 29.8 %all-to-all-start.4 = ((bf16[8,216,512]{2,1,0:T(8,128)(2,1)}), bf16[8,216,512]{2,1,0:T(8,128)(2,1)S(1)}, u32[]{:S(2)}, u32[]{:S(2)}) async-start(bf16[8,216,512]{2,1,0:T(8,128)(2,1)} %shard_map.99), calls=%async_computation.4 | async-start | bytes 3538944 | tf_op jit(solution)/shard_map/all_to_all | solution.py:621
  185.2 6.2 %collective-permute-start.23 = (bf16[2,16,4096]{2,1,0:T(8,128)(2,1)S(1)}, bf16[2,16,4096]{2,1,0:T(8,128)(2,1)S(1)}, u32[]{:S(2)}, u32[]{:S(2)}) collective-permute-start(bf16[2,16,4096]{2,1,0:T(8,128)(2,1)S(1)} %slice_bitcast_fusion.1), channel_id=1, source_target_pairs={{0,96},{32,0},{64,32},{96,64},{1,97},{33,1},{65,33},{97,65},{2,98}... | collective-permute-start | bytes 786440 | tf_op jit(solution)/shard_map/ppermute | solution.py:619
  186.0 7.0 %collective-permute-start.24 = (bf16[2,16,4096]{2,1,0:T(8,128)(2,1)S(1)}, bf16[2,16,4096]{2,1,0:T(8,128)(2,1)S(1)}, u32[]{:S(2)}, u32[]{:S(2)}) collective-permute-start(bf16[2,16,4096]{2,1,0:T(8,128)(2,1)S(1)} %slice_bitcast_fusion), channel_id=1, source_target_pairs={{0,32},{32,64},{64,96},{96,0},{1,33},{33,65},{65,97},{97,1},{2,34}... | collective-permute-start | bytes 786440 | tf_op jit(solution)/shard_map/ppermute | solution.py:619
  193.6 8.5 %collective-permute-start.25 = (bf16[512,256]{1,0:T(8,128)(2,1)S(1)}, bf16[512,256]{1,0:T(8,128)(2,1)S(1)}, u32[]{:S(2)}, u32[]{:S(2)}) collective-permute-start(bf16[512,256]{1,0:T(8,128)(2,1)S(1)} %shard_map.104.mine), channel_id=1, source_target_pairs={{0,1},{1,0},{2,3},{3,2},{4,5},{5,4},{6,7},{7,6},{8,9},{9,8},{10,11... | collective-permute-start | bytes 786440 | tf_op jit(solution)/shard_map/ppermute | solution.py:545
  (14 other events, 77.4 us)
